TPU v7x, 32 devices: a whole 2x2x4 slice. The times are simulated.
32 devices in a mesh: shard: 2 (over y), ctx: 4 (over z), tp: 4 (over x, core).
Axes of the slice: x: 2, y: 2, z: 4, core: 2. Of those that a mesh axis runs over, the one named last changes fastest.
Arguments:
- tokens: bfloat16 [2, 1536, 2048], P('shard', 'ctx'), may hold values from -6 to 6
- segments: int32 [2, 1536], P('shard'), may hold values from 0 to 3, as said below
- routes: int32 [2, 1536, 8], P('shard', 'ctx'), may hold values from 0 to 15, all different within a row; in each aligned block of 384 rows (0 to 383, 384 to 767, ..., all dimensions but the last counted through in order) at most 240 rows name the same one
- cotangent: bfloat16 [2, 1536, 2048], P('shard', 'ctx'), may hold values from -6 to 6
- first_gain: bfloat16 [2048], P('shard'), may hold values from 0.099609375 to 1.8984375
- head_gain: bfloat16 [256], P('shard'), may hold values from 1 to 1.59375
- attention_in: bfloat16 [2048, 3, 2048], P('shard', None, 'tp'), may hold values from -0.125 to 0.125
- attention_out: bfloat16 [2048, 2048], P('shard', 'tp'), may hold values from -0.5 to 0.5
- second_gain: bfloat16 [2048], P('shard'), may hold values from 0.099609375 to 1.8984375
- router_weight: bfloat16 [2048, 16], P('shard'), may hold values from -0.0625 to 0.0625
- expert_in: bfloat16 [2048, 16, 2, 1024], P('shard', None, None, 'tp'), may hold values from -0.125 to 0.125
- expert_out: bfloat16 [2048, 16, 1024], P('shard', None, 'tp'), may hold values from -1.5 to 1.5
Outputs:
- layer_output: bfloat16 [2, 1536, 2048], P('shard', 'ctx')
- input_gradient: float32 [2, 1536, 2048], P('shard', 'ctx')
- first_gradient: float32 [2048], P('shard')
- head_gradient: float32 [256], P('shard')
- entry_gradient: float32 [2048, 3, 2048], P('shard', None, 'tp')
- exit_gradient: float32 [2048, 2048], P('shard', 'tp')
- second_gradient: float32 [2048], P('shard')
- router_gradient: float32 [2048, 16], P('shard')
- upward_gradient: float32 [2048, 16, 2, 1024], P('shard', None, None, 'tp')
- downward_gradient: float32 [2048, 16, 1024], P('shard', None, 'tp')
Inputs may be any that keep to these rules, and one draw needn't show every extreme that they name: `segments`: within each pack the numbers never fall, each of 0 to 3 occurs, and one document, which one varies, starts among the pack's first 384 tokens and ends among its last 384. `routes`: each row names 8 different experts. Among the 384 rows of one index of ctx no expert is named by more than 240 rows, a bound that some block reaches.
All inputs are finite; a program needn't handle non-finite values.
Results may differ from a plain program's by a relative error of at most 0.017.
Values may be sent and summed in bfloat16 or wider, within the bound.
A program may use at most 576 MiB of HBM per device.

v0:
```python
import jax
import jax.numpy as jnp
from jax import lax
from jax.sharding import PartitionSpec as P

HEAD_DIM = 128
CAPACITY = 240


NORM_EPSILON = 1e-06
ROTARY_BASE = 50000.0
MASKED = -1e30


def lower(values):
    return values.astype(jnp.bfloat16)


def norm_scale(values, gain):
    return (
        values * lax.rsqrt(jnp.mean(values * values, axis=-1, keepdims=True) + NORM_EPSILON) * gain
    )


def rotate(values, positions):
    halfway = values.shape[-1] // 2
    steps = jnp.arange(halfway).astype(positions.dtype)
    frequency = ROTARY_BASE ** (-2.0 * steps / values.shape[-1])
    angles = positions[:, None] * frequency[None, :]
    cosine = jnp.cos(angles)[:, None, :]
    sine = jnp.sin(angles)[:, None, :]
    front = values[..., :halfway]
    back = values[..., halfway:]
    return jnp.concatenate([front * cosine - back * sine, back * cosine + front * sine], axis=-1)


def head_prepare(query_raw, key_raw, gains, positions):
    halfway = gains.shape[0] // 2
    return (
        rotate(norm_scale(query_raw, gains[:halfway]), positions),
        rotate(norm_scale(key_raw, gains[halfway:]), positions),
    )


def swiglu(gate_up):
    return jax.nn.silu(gate_up[:, :, 0]) * gate_up[:, :, 1]


def forward(tokens, segments, routes, cotangent, small_shards, expert_shards):
    first_gain, head_gain, attention_in, attention_out, second_gain, router_weight = (
        lax.all_gather(small_shards[0], "shard", axis=0, tiled=True),
        lax.all_gather(small_shards[1], "shard", axis=0, tiled=True),
        lax.all_gather(small_shards[2], "shard", axis=0, tiled=True),
        lax.all_gather(small_shards[3], "shard", axis=0, tiled=True),
        lax.all_gather(small_shards[4], "shard", axis=0, tiled=True),
        lax.all_gather(small_shards[5], "shard", axis=0, tiled=True),
    )
    layer_in = tokens[0].astype(jnp.float32)
    row_count = layer_in.shape[0]
    start_row = lax.axis_index("ctx") * row_count
    positions = (start_row + jnp.arange(row_count)).astype(jnp.float32)
    doc_all = segments[0]
    doc_local = lax.dynamic_slice_in_dim(doc_all, start_row, row_count)
    gain_one = first_gain.astype(jnp.float32)
    first_normed = lower(norm_scale(layer_in, gain_one))
    projected = jnp.einsum(
        "td,dsj->tsj", first_normed, attention_in, preferred_element_type=jnp.float32
    )
    local_heads = projected.shape[2] // HEAD_DIM
    query_raw = projected[:, 0].reshape(row_count, local_heads, HEAD_DIM)
    key_raw = projected[:, 1].reshape(row_count, local_heads, HEAD_DIM)
    head_gains = head_gain.astype(jnp.float32)
    query_rot, key_rot = head_prepare(query_raw, key_raw, head_gains, positions)
    query_low = lower(query_rot)
    memory_local = jnp.stack(
        [lower(key_rot).reshape(row_count, -1), lower(projected[:, 2])], axis=1
    )
    memory = lax.all_gather(memory_local, "ctx", axis=0, tiled=True)
    key_count = memory.shape[0]
    keys = memory[:, 0].reshape(key_count, local_heads, HEAD_DIM)
    values = memory[:, 1].reshape(key_count, local_heads, HEAD_DIM)
    scale = HEAD_DIM ** (-0.5)
    scores = jnp.einsum("qhd,khd->hqk", query_low, keys, preferred_element_type=jnp.float32) * scale
    same_doc = doc_local[:, None] == doc_all[None, :]
    chances = jax.nn.softmax(jnp.where(same_doc[None], scores, MASKED), axis=-1)
    chances_low = lower(chances)
    heads_out = jnp.einsum("hqk,khd->qhd", chances_low, values, preferred_element_type=jnp.float32)
    mixed = lower(heads_out.reshape(row_count, -1))
    partial_attend = jnp.einsum(
        "tj,dj->td", mixed, attention_out, preferred_element_type=jnp.float32
    )
    residual = layer_in + lax.psum(partial_attend, "tp")
    gain_two = second_gain.astype(jnp.float32)
    second_normed = lower(norm_scale(residual, gain_two))
    logits = jnp.einsum(
        "td,de->te", second_normed, router_weight, preferred_element_type=jnp.float32
    )
    router_chances = jax.nn.softmax(logits, axis=-1)
    choices_made = routes[0]
    expert_count = router_weight.shape[1]
    picks = choices_made[:, :, None] == jnp.arange(expert_count)[None, None, :]
    chosen = jnp.sum(picks.astype(jnp.int32), axis=1)
    earlier = jnp.cumsum(chosen, axis=0) - chosen
    slots = jnp.sum(jnp.where(picks, earlier[:, None, :], 0), axis=2)
    gates = jnp.sum(jnp.where(picks, router_chances[:, None, :], 0.0), axis=2)
    owners = jnp.broadcast_to(jnp.arange(row_count)[:, None], choices_made.shape)
    slot_token = jnp.zeros((CAPACITY, expert_count), jnp.int32).at[slots, choices_made].set(owners)
    slot_gate = jnp.zeros((CAPACITY, expert_count), jnp.float32).at[slots, choices_made].set(gates)
    routed = second_normed[slot_token]
    upstream = cotangent[0].astype(jnp.float32)
    upstream_rows = upstream[slot_token]
    result_grad = lower(upstream_rows * slot_gate[:, :, None])
    expert_in, expert_out = (
        lax.all_gather(expert_shards[0], "shard", axis=0, tiled=True),
        lax.all_gather(expert_shards[1], "shard", axis=0, tiled=True),
    )
    gate_up = jnp.einsum("ced,dexf->cexf", routed, expert_in, preferred_element_type=jnp.float32)
    hidden = lower(swiglu(gate_up))
    owner_part = jnp.einsum("cef,def->ced", hidden, expert_out, preferred_element_type=jnp.float32)
    return dict(
        layer_in=layer_in,
        positions=positions,
        gain_one=gain_one,
        first_normed=first_normed,
        attention_in=attention_in,
        attention_out=attention_out,
        query_raw=query_raw,
        key_raw=key_raw,
        head_gains=head_gains,
        query_low=query_low,
        keys=keys,
        values=values,
        chances=chances,
        chances_low=chances_low,
        mixed=mixed,
        residual=residual,
        gain_two=gain_two,
        second_normed=second_normed,
        router_weight=router_weight,
        expert_in=expert_in,
        expert_out=expert_out,
        router_chances=router_chances,
        choices_made=choices_made,
        picks=picks,
        slots=slots,
        slot_token=slot_token,
        slot_gate=slot_gate,
        routed_here=routed,
        result_here=result_grad,
        upstream=upstream,
        upstream_rows=upstream_rows,
        gate_up=gate_up,
        hidden=hidden,
        expert_part=owner_part,
    )


def local(
    tokens,
    segments,
    routes,
    cotangent,
    first_gain,
    head_gain,
    attention_in,
    attention_out,
    second_gain,
    router_weight,
    expert_in,
    expert_out,
):
    small_shards = (first_gain, head_gain, attention_in, attention_out, second_gain, router_weight)
    expert_shards = (expert_in, expert_out)
    first = forward(tokens, segments, routes, cotangent, small_shards, expert_shards)
    row_count = first["layer_in"].shape[0]
    width = first["layer_in"].shape[1]
    weighted = first["expert_part"] * first["slot_gate"][:, :, None]
    partial_expert = (
        jnp.zeros((row_count, width), jnp.float32)
        .at[first["slot_token"].reshape(-1)]
        .add(weighted.reshape(-1, width))
    )
    expert_sum = lax.psum(partial_expert, "tp")
    layer_output = lower(first["residual"] + expert_sum)[None]
    saved = forward(tokens, segments, routes, cotangent, small_shards, expert_shards)
    upstream = saved["upstream"]
    slot_token = saved["slot_token"]
    result_here = saved["result_here"]
    gate_part = jnp.sum(saved["upstream_rows"] * saved["expert_part"], axis=2)
    downward = jnp.einsum(
        "ced,cef->def", result_here, saved["hidden"], preferred_element_type=jnp.float32
    )
    hidden_grad = jnp.einsum(
        "ced,def->cef", result_here, saved["expert_out"], preferred_element_type=jnp.float32
    )
    swiglu_pull = jax.vjp(swiglu, saved["gate_up"])[1]
    gate_up_grad = lower(swiglu_pull(hidden_grad)[0])
    upward = jnp.einsum(
        "ced,cexf->dexf", saved["routed_here"], gate_up_grad, preferred_element_type=jnp.float32
    )
    routed_grad = jnp.einsum(
        "cexf,dexf->ced", gate_up_grad, saved["expert_in"], preferred_element_type=jnp.float32
    )
    upward_rows, downward_rows = (
        lax.psum_scatter(upward, "shard", scatter_dimension=0, tiled=True),
        lax.psum_scatter(downward, "shard", scatter_dimension=0, tiled=True),
    )
    partial_normed = (
        jnp.zeros((row_count, width), jnp.float32)
        .at[slot_token.reshape(-1)]
        .add(routed_grad.reshape(-1, width))
    )
    partial_gates = gate_part[saved["slots"], saved["choices_made"]]
    expert_normed, gate_grad = lax.psum((partial_normed, partial_gates), "tp")
    router_chances = saved["router_chances"]
    chance_grad = jnp.sum(jnp.where(saved["picks"], gate_grad[:, :, None], 0.0), axis=1)
    logit_grad = lower(
        router_chances
        * (chance_grad - jnp.sum(router_chances * chance_grad, axis=-1, keepdims=True))
    )
    router_grad = jnp.einsum(
        "td,te->de", saved["second_normed"], logit_grad, preferred_element_type=jnp.float32
    )
    normed_grad = expert_normed + jnp.einsum(
        "te,de->td", logit_grad, saved["router_weight"], preferred_element_type=jnp.float32
    )
    norm_two_pull = jax.vjp(norm_scale, saved["residual"], saved["gain_two"])[1]
    residual_part, second_grad = norm_two_pull(normed_grad)
    residual_grad = upstream + residual_part
    attend_grad = lower(residual_grad)
    exit_grad = jnp.einsum(
        "td,tj->dj", attend_grad, saved["mixed"], preferred_element_type=jnp.float32
    )
    mixed_grad = lower(
        jnp.einsum(
            "td,dj->tj", attend_grad, saved["attention_out"], preferred_element_type=jnp.float32
        )
    )
    query_low = saved["query_low"]
    local_heads = query_low.shape[1]
    mixed_heads = mixed_grad.reshape(row_count, local_heads, HEAD_DIM)
    chances = saved["chances"]
    chances_low = saved["chances_low"]
    weight_grad = jnp.einsum(
        "qhd,khd->hqk", mixed_heads, saved["values"], preferred_element_type=jnp.float32
    )
    score_grad = lower(
        chances * (weight_grad - jnp.sum(chances * weight_grad, axis=-1, keepdims=True))
    )
    scale = HEAD_DIM ** (-0.5)
    query_grad = (
        jnp.einsum("hqk,khd->qhd", score_grad, saved["keys"], preferred_element_type=jnp.float32)
        * scale
    )
    count = row_count * lax.axis_size("ctx")
    score_part = lax.slice_in_dim(score_grad, 0, count, axis=2)
    chance_part = lax.slice_in_dim(chances_low, 0, count, axis=2)
    key_part = (
        jnp.einsum("hqk,qhd->khd", score_part, query_low, preferred_element_type=jnp.float32)
        * scale
    )
    value_part = jnp.einsum(
        "hqk,qhd->khd", chance_part, mixed_heads, preferred_element_type=jnp.float32
    )
    memory_grad = lax.psum_scatter(
        jnp.stack([key_part.reshape(count, -1), value_part.reshape(count, -1)], axis=1),
        "ctx",
        scatter_dimension=0,
        tiled=True,
    )
    key_grad = memory_grad[:, 0].reshape(row_count, local_heads, HEAD_DIM)
    positions = saved["positions"]

    def prepare_heads(query_raw, key_raw, gains):
        return head_prepare(query_raw, key_raw, gains, positions)

    prepare_pull = jax.vjp(
        prepare_heads, saved["query_raw"], saved["key_raw"], saved["head_gains"]
    )[1]
    query_raw_grad, key_raw_grad, head_part = prepare_pull((query_grad, key_grad))
    projected_grad = lower(
        jnp.stack(
            [
                query_raw_grad.reshape(row_count, -1),
                key_raw_grad.reshape(row_count, -1),
                memory_grad[:, 1],
            ],
            axis=1,
        )
    )
    entry_grad = jnp.einsum(
        "td,tsj->dsj", saved["first_normed"], projected_grad, preferred_element_type=jnp.float32
    )
    partial_first = jnp.einsum(
        "tsj,dsj->td", projected_grad, saved["attention_in"], preferred_element_type=jnp.float32
    )
    first_normed_grad, head_grad = lax.psum((partial_first, head_part), "tp")
    norm_one_pull = jax.vjp(norm_scale, saved["layer_in"], saved["gain_one"])[1]
    input_part, first_grad = norm_one_pull(first_normed_grad)
    input_gradient = (residual_grad + input_part)[None]
    attention_rows = (
        lax.psum_scatter(first_grad, "shard", scatter_dimension=0, tiled=True),
        lax.psum_scatter(head_grad, "shard", scatter_dimension=0, tiled=True),
        lax.psum_scatter(entry_grad, "shard", scatter_dimension=0, tiled=True),
        lax.psum_scatter(exit_grad, "shard", scatter_dimension=0, tiled=True),
        lax.psum_scatter(second_grad, "shard", scatter_dimension=0, tiled=True),
        lax.psum_scatter(router_grad, "shard", scatter_dimension=0, tiled=True),
    )
    summed = lax.psum(
        (
            attention_rows[0],
            attention_rows[1],
            attention_rows[2],
            attention_rows[3],
            attention_rows[4],
            attention_rows[5],
            upward_rows,
            downward_rows,
        ),
        "ctx",
    )
    return (
        layer_output,
        input_gradient,
        summed[0],
        summed[1],
        summed[2],
        summed[3],
        summed[4],
        summed[5],
        summed[6],
        summed[7],
    )


def solution(mesh):
    return jax.shard_map(
        local,
        mesh=mesh,
        in_specs=(
            P("shard", "ctx", None),
            P("shard", None),
            P("shard", "ctx", None),
            P("shard", "ctx", None),
            P("shard"),
            P("shard"),
            P("shard", None, "tp"),
            P("shard", "tp"),
            P("shard"),
            P("shard", None),
            P("shard", None, None, "tp"),
            P("shard", None, "tp"),
        ),
        out_specs=(
            P("shard", "ctx", None),
            P("shard", "ctx", None),
            P("shard"),
            P("shard"),
            P("shard", None, "tp"),
            P("shard", "tp"),
            P("shard"),
            P("shard", None),
            P("shard", None, None, "tp"),
            P("shard", None, "tp"),
        ),
        check_vma=False,
    )
```

profile of v0, /device:TPU:0, one launch (start us, length us, event | category | flops | bytes accessed | tf_op | source)
XLA Modules:
  0.0 4786.7 jit_solution(10223798696568969903)
XLA Ops:
  19.3 73.4 %all-gather.7.cloned.1.call-done = bf16[2048,3,512]{2,0,1:T(8,128)(2,1)} async-done(((bf16[1024,3,512]{2,0,1:T(8,128)(2,1)}), bf16[2048,3,512]{2,0,1:T(8,128)(2,1)}) %all-gather.7.cloned.1.call-update) | async-done | bytes 6291472 | tf_op jit(solution)/shard_map/all_gather | solution.py:53
  107.3 61.0 %all-gather.9.cloned.1.call-done = bf16[1536,2,512]{2,0,1:T(8,128)(2,1)} async-done(((bf16[384,2,512]{2,0,1:T(8,128)(2,1)}), bf16[1536,2,512]{2,0,1:T(8,128)(2,1)}) %all-gather.9.cloned.1.call-update) | async-done | bytes 3145744 | tf_op jit(solution)/shard_map/all_gather | solution.py:78
  254.3 18.1 gather_fusion.1
  299.4 365.9 %all-gather.13.cloned.1.call-done = bf16[2048,16,2,256]{3,0,2,1:T(8,128)(2,1)} async-done(((bf16[1024,16,2,256]{3,0,2,1:T(8,128)(2,1)}), bf16[2048,16,2,256]{3,0,2,1:T(8,128)(2,1)}) %all-gather.13.cloned.1.call-update) | async-done | bytes 33554448 | tf_op jit(solution)/shard_map/all_gather | solution.py:114
  665.3 44.0 fusion.30
  713.8 152.4 %all-gather.15.cloned.1.call-done = bf16[2048,16,256]{2,0,1:T(8,128)(2,1)} async-done(((bf16[1024,16,256]{2,0,1:T(8,128)(2,1)}), bf16[2048,16,256]{2,0,1:T(8,128)(2,1)}) %all-gather.15.cloned.1.call-update) | async-done | bytes 16777232 | tf_op jit(solution)/shard_map/all_gather | solution.py:115
  866.2 35.0 fusion.3
  901.2 24.9 gather_fusion.2
  952.4 36.8 fusion.18
  989.2 25.1 fusion.4
  1014.3 37.6 copy.371
  1051.9 54.1 %scatter_custom_fusion.1 = f32[384,2048]{1,0:T(8,128)} fusion(s32[3840]{0:T(1024)} %fusion.65, f32[3840,2048]{1,0:T(8,128)} %bitcast.170, f32[]{:T(128)} %constant.19.clone.1), kind=kCustom, calls=%fused_computation.77 | custom fusion | flops 7864320 | bytes 3146240 | tf_op jit(solution)/shard_map/scatter-add | solution.py:211
  1106.6 67.4 %all-reduce.22.cloned.1.call-done = f32[384,2048]{1,0:T(8,128)} async-done(((f32[384,2048]{1,0:T(8,128)}), f32[384,2048]{1,0:T(8,128)}) %all-reduce.22.cloned.1.call-update) | async-done | bytes 3145744 | tf_op jit(solution)/shard_map/psum | solution.py:214
  1228.8 97.9 %reduce-scatter.7.cloned.1.call-done = f32[384,2,512]{2,0,1:T(8,128)} async-done(((f32[1536,2,512]{2,0,1:T(8,128)}), f32[384,2,512]{2,0,1:T(8,128)}) %reduce-scatter.7.cloned.1.call-update) | async-done | bytes 1572880 | tf_op jit(solution)/shard_map/reduce_scatter | solution.py:265
  1343.4 32.7 convolution_bitcast_fusion.1
  1376.5 38.7 convolution_bitcast_fusion
  1428.1 34.7 copy.368
  1462.8 54.1 %scatter_custom_fusion = f32[384,2048]{1,0:T(8,128)} fusion(s32[3840]{0:T(1024)} %fusion.65, f32[3840,2048]{1,0:T(8,128)} %bitcast.169, f32[]{:T(128)} %constant.19.clone.1), kind=kCustom, calls=%fused_computation.79 | custom fusion | flops 7864320 | bytes 3146240 | tf_op jit(solution)/shard_map/scatter-add | solution.py:181
  1524.2 20.1 reduce-scatter.9.cloned.1.call-done
  1544.3 371.8 %reduce-scatter.17.cloned.1.call-done = f32[1024,16,256]{0,2,1:T(8,128)} async-done(((f32[2048,16,256]{0,2,1:T(8,128)}), f32[1024,16,256]{0,2,1:T(8,128)}) %reduce-scatter.17.cloned.1.call-update) | async-done | bytes 16777232 | tf_op jit(solution)/shard_map/reduce_scatter | solution.py:206
  1916.0 730.9 %reduce-scatter.15.cloned.1.call-done = f32[1024,16,2,256]{0,3,2,1:T(8,128)} async-done(((f32[2048,16,2,256]{0,3,2,1:T(8,128)}), f32[1024,16,2,256]{0,3,2,1:T(8,128)}) %reduce-scatter.15.cloned.1.call-update) | async-done | bytes 33554448 | tf_op jit(solution)/shard_map/reduce_scatter | solution.py:205
  2649.5 120.2 %all-reduce.24.cloned.1.call-done = (f32[384,2048]{1,0:T(8,128)}, f32[384,2048]{1,0:T(8,128)}) async-done(((f32[384,2048]{1,0:T(8,128)}, f32[384,2048]{1,0:T(8,128)}), (f32[384,2048]{1,0:T(8,128)}, f32[384,2048]{1,0:T(8,128)})) %all-reduce.24.cloned.1.call-update) | async-done | bytes 6291472 | tf_op jit(solution)/shard_map/psum | solution.py:183
  2808.3 1897.3 %all-reduce.26.cloned.1.call-done = (f32[1024,3,512]{2,0,1:T(8,128)}, f32[1024,512]{1,0:T(8,128)}, f32[1024,16]{0,1:T(8,128)}, f32[1024,16,2,256]{0,3,2,1:T(8,128)}, f32[1024,16,256]{0,2,1:T(8,128)}) async-done(((f32[1024,3,512]{2,0,1:T(8,128)}, f32[1024,512]{1,0:T(8,128)}, f32[1024,16]{0,1:T(8,128)}, f32[1024,16,2,256]{0,3,2,1:T(8,128)}, f32[1024,16,256]{0,2,1:T(8,128)}), (f32[1024,3,512]{2,0,1:T(8,128)}, ...) | async-done | bytes 58785808 | tf_op jit(solution)/shard_map/psum | solution.py:309
  4723.2 48.5 %copy.397 = f32[1024,16,2,256]{3,2,1,0:T(2,128)} copy(f32[1024,16,2,256]{0,3,2,1:T(8,128)} %get-tuple-element.108) | data formatting | bytes 67108864
  (347 shorter events, 327.4 us)
Async XLA Ops:
  7.2 85.5 %all-gather.7.cloned.1.call-start = ((), (), s32[]{:S(2)}) async-start(), calls=%async_computation.6 | async-start | bytes 9437184 | tf_op jit(solution)/shard_map/all_gather | solution.py:53
  7.9 160.3 %all-gather.9.cloned.1.call-start = ((), (), s32[]{:S(2)}) async-start(), calls=%async_computation.7 | async-start | bytes 3932160 | tf_op jit(solution)/shard_map/all_gather | solution.py:78
  104.7 97.4 %all-gather.11.cloned.1.call-start = ((), (), s32[]{:S(2)}) async-start(), calls=%async_computation.8 | async-start | bytes 3145728 | tf_op jit(solution)/shard_map/all_gather | solution.py:54
  105.4 172.2 %all-reduce.20.cloned.1.call-start = ((), (), s32[]{:S(2)}) async-start(), calls=%async_computation.9 | async-start | bytes 6291456 | tf_op jit(solution)/shard_map/psum | solution.py:92
  206.5 458.8 %all-gather.13.cloned.1.call-start = ((), (), s32[]{:S(2)}) async-start(), calls=%async_computation.10 | async-start | bytes 50331648 | tf_op jit(solution)/shard_map/all_gather | solution.py:114
  222.2 643.9 %all-gather.15.cloned.1.call-start = ((), (), s32[]{:S(2)}) async-start(), calls=%async_computation.11 | async-start | bytes 25165824 | tf_op jit(solution)/shard_map/all_gather | solution.py:115
  232.4 941.6 %all-reduce.22.cloned.1.call-start = ((), (), s32[]{:S(2)}) async-start(), calls=%async_computation.12 | async-start | bytes 6291456 | tf_op jit(solution)/shard_map/psum | solution.py:214
  298.8 366.5 %copy-start.56 = (f32[384]{0:T(512)}, f32[384]{0:T(512)S(1)}, u32[]{:S(2)}) copy-start(f32[384]{0:T(512)S(1)} %get-tuple-element.146) | copy-start | bytes 4612
  299.4 365.9 %copy-start.63 = (f32[384]{0:T(512)}, f32[384]{0:T(512)S(1)}, u32[]{:S(2)}) copy-start(f32[384]{0:T(512)S(1)} %fusion.64) | copy-start | bytes 4612
  713.8 187.4 %copy-start.18 = (bf16[240,16,256]{2,0,1:T(8,128)(2,1)}, bf16[240,16,256]{2,0,1:T(8,128)(2,1)S(1)}, u32[]{:S(2)}) copy-start(bf16[240,16,256]{2,0,1:T(8,128)(2,1)S(1)} %multiply_convert_fusion.4) | copy-start | bytes 5898244
  1051.9 122.1 %copy-start.4 = (f32[384,2048]{1,0:T(8,128)S(1)}, f32[384,2048]{1,0:T(8,128)}, u32[]{:S(2)}) copy-start(f32[384,2048]{1,0:T(8,128)} %copy-done.3) | copy-start | bytes 9437188
  1051.9 122.1 %copy-start.39 = (bf16[2048,16]{0,1:T(8,128)(2,1)S(1)}, bf16[2048,16]{0,1:T(8,128)(2,1)}, u32[]{:S(2)}) copy-start(bf16[2048,16]{0,1:T(8,128)(2,1)} %copy-done.38) | copy-start | bytes 196612
  1051.9 122.1 %copy-start.46 = (f32[2048]{0:T(1024)S(1)}, f32[2048]{0:T(1024)}, u32[]{:S(2)}) copy-start(f32[2048]{0:T(1024)} %copy-done.45) | copy-start | bytes 24580
  1106.0 220.7 %reduce-scatter.7.cloned.1.call-start = ((), (), s32[]{:S(2)}) async-start(), calls=%async_computation.13 | async-start | bytes 7864320 | tf_op jit(solution)/shard_map/reduce_scatter | solution.py:265
  1215.7 308.4 %reduce-scatter.13.cloned.1.call-start = ((), (), s32[]{:S(2)}) async-start(), calls=%async_computation.16 | async-start | bytes 196608 | tf_op jit(solution)/shard_map/reduce_scatter | solution.py:307
  1218.1 306.1 %reduce-scatter.11.cloned.1.call-start = ((), (), s32[]{:S(2)}) async-start(), calls=%async_computation.15 | async-start | bytes 6291456 | tf_op jit(solution)/shard_map/reduce_scatter | solution.py:305
  1223.7 320.6 %reduce-scatter.9.cloned.1.call-start = ((), (), s32[]{:S(2)}) async-start(), calls=%async_computation.14 | async-start | bytes 18874368 | tf_op jit(solution)/shard_map/reduce_scatter | solution.py:304
  1341.9 574.1 %reduce-scatter.17.cloned.1.call-start = ((), (), s32[]{:S(2)}) async-start(), calls=%async_computation.18 | async-start | bytes 50331648 | tf_op jit(solution)/shard_map/reduce_scatter | solution.py:206
  1376.2 1270.7 %reduce-scatter.15.cloned.1.call-start = ((), (), s32[]{:S(2)}) async-start(), calls=%async_computation.17 | async-start | bytes 100663296 | tf_op jit(solution)/shard_map/reduce_scatter | solution.py:205
  1415.2 1354.5 %all-reduce.24.cloned.1.call-start = ((), (), s32[]{:S(2)}) async-start(), calls=%async_computation.19 | async-start | bytes 12582912 | tf_op jit(solution)/shard_map/psum | solution.py:183
  1524.0 3181.6 %all-reduce.26.cloned.1.call-start = ((), (), s32[]{:S(2)}) async-start(), calls=%async_computation.20 | async-start | bytes 117571584 | tf_op jit(solution)/shard_map/psum | solution.py:309
  2646.9 126.0 %copy-start.62 = (f32[2048]{0:T(1024)S(1)}, f32[2048]{0:T(1024)}, u32[]{:S(2)}) copy-start(f32[2048]{0:T(1024)} %get-tuple-element.90) | copy-start | bytes 24580
  2647.0 154.0 %copy-start.67 = (f32[384]{0:T(512)S(1)}, f32[384]{0:T(512)}, u32[]{:S(2)}) copy-start(f32[384]{0:T(512)} %copy-done.66) | copy-start | bytes 4612
  2647.0 154.0 %copy-start.5 = (f32[384,2048]{1,0:T(8,128)S(1)}, f32[384,2048]{1,0:T(8,128)}, u32[]{:S(2)}) copy-start(f32[384,2048]{1,0:T(8,128)} %copy-done.3) | copy-start | bytes 9437188
  (78 other events, 1313.7 us)
Sparse Core Ops, SparseCore 0:
  9.6 83.0 all-gather.6
  104.8 63.4 all-gather.8
  169.8 31.7 all-gather.10
  206.6 67.8 all-reduce.19
  276.6 388.6 all-gather.12
  667.3 198.8 all-gather.14
  1106.1 67.7 all-reduce.21
  1215.8 110.8 reduce-scatter.6
  1329.5 10.7 reduce-scatter.12
  1342.5 54.2 reduce-scatter.10
  1399.8 144.4 reduce-scatter.8
  1547.1 368.8 reduce-scatter.16
  1918.4 728.4 reduce-scatter.14
  2649.9 119.7 all-reduce.23
  2772.9 1932.6 all-reduce.25
where the time goes:
time: 4790 us
  waiting for transfers between devices  3960 us (83%)
  local copies, waits for them, and re-layouts  292 us (6%)
  matrix products  275 us (6%)
  other arithmetic  180 us (4%)
  blocking collectives  59.9 us (1%)
    psum x1, waiting for transfers between devices, local(): lax.psum((attention_rows[0], attention_rows[1], attention_rows[2], attent...  1900 us
    reduce_scatter x1, waiting for transfers between devices, local(): lax.psum_scatter(upward, 'shard', scatter_dimension=0, tiled=True)  731 us
    reduce_scatter x1, waiting for transfers between devices, local(): lax.psum_scatter(downward, 'shard', scatter_dimension=0, tiled=True)  372 us
    all_gather x1, waiting for transfers between devices, forward(): lax.all_gather(expert_shards[0], 'shard', axis=0, tiled=True)  366 us
    all_gather x1, waiting for transfers between devices, forward(): lax.all_gather(expert_shards[1], 'shard', axis=0, tiled=True)  152 us
    unnamed x193, local copies, waits for them, and re-layouts  140 us
    psum x1, waiting for transfers between devices, local(): expert_sum = lax.psum(partial_expert, 'tp')  120 us
    reduce_scatter x1, waiting for transfers between devices, local(): lax.psum_scatter(jnp.stack([key_part.reshape(count, -1), value_part.resha...  97.9 us
  transfers between devices with their start and end apart: 15, of which 11 were waited for; matrix products, arithmetic and copies ran while one was open for 8% of the time, Pallas kernels for 0%

commit v1 on v0

v1 whole, which is shorter than its diff:
```python
import jax
import jax.numpy as jnp
from jax import lax
from jax.sharding import PartitionSpec as P

HEAD_DIM = 128
NORM_EPSILON = 1e-06
ROTARY_BASE = 50000.0
MASKED = -1e30
F32 = jnp.float32
BF16 = jnp.bfloat16


def lower(values):
    return values.astype(BF16)


def dot(left, right, over, out=F32):
    result = lax.dot_general(left, right, (((over[0],), (over[1],)), ((), ())), preferred_element_type=F32)
    return result.astype(out)


def receive(values, axis, distance):
    size = lax.axis_size(axis)
    return lax.ppermute(values, axis, [((i + distance) % size, i) for i in range(size)])


def swap(values, axis, bit):
    size = lax.axis_size(axis)
    return lax.ppermute(values, axis, [(i, i ^ bit) for i in range(size)])


def bits(axis):
    size = lax.axis_size(axis)
    assert size & (size - 1) == 0
    found = [1 << i for i in range(size.bit_length() - 1)]
    return found


def masks(axis):
    order = [0]
    for bit in reversed(bits(axis)):
        order = order + [m ^ bit for m in order]
    return order


def gather_tp(values):
    for bit in reversed(bits("tp")):
        values = jnp.concatenate([values, swap(values, "tp", bit)], axis=0)
    return values


def scatter_tp(values):
    for bit in bits("tp"):
        half = values.shape[0] // 2
        values = values[:half].astype(F32) + swap(lower(values[half:]), "tp", bit).astype(F32)
    return values


def gather_rows(values):
    size = lax.axis_size("ctx")
    blocks = [[values] + [receive(values, "ctx", r) for r in range(1, size)]]
    for bit in reversed(bits("tp")[1:]):
        blocks = blocks + [[swap(v, "tp", bit) for v in part] for part in blocks]
    values = jnp.concatenate([v for part in blocks for v in part], axis=0)
    return jnp.concatenate([values, swap(values, "tp", 1)], axis=0)


def scatter_rows(values):
    size = lax.axis_size("ctx")
    half = values.shape[0] // 2
    values = values[:half].astype(F32) + swap(lower(values[half:]), "tp", 1).astype(F32)
    found = bits("tp")[1:]
    parts = 1 << len(found)
    blocks = values.reshape((parts, size, -1) + values.shape[1:])
    blocks = [[blocks[a, r] for r in range(size)] for a in range(parts)]
    for bit in found:
        near, far = blocks[: len(blocks) // 2], blocks[len(blocks) // 2 :]
        blocks = [
            [n + swap(lower(f), "tp", bit).astype(F32) for n, f in zip(one, other)]
            for one, other in zip(near, far)
        ]
    total = blocks[0][0]
    for r in range(1, size):
        total = total + receive(lower(blocks[0][r]), "ctx", size - r).astype(F32)
    return total


def sum_tokens(values):
    for axis in ("tp", "ctx"):
        for bit in bits(axis):
            values = values + swap(values, axis, bit)
    return values


def own_block(values, ahead=0, axis=0):
    size = lax.axis_size("shard")
    block = values.shape[axis] // size
    spot = lax.rem(lax.axis_index("shard") + ahead, size)
    return lax.dynamic_slice_in_dim(values, spot * block, block, axis=axis)


def sum_shard(values, axis):
    size = lax.axis_size("shard")
    total = own_block(values, 0, axis)
    for r in range(1, size):
        total = total + receive(own_block(values, r, axis), "shard", size - r)
    return total


def product_shard(lefts, right):
    size = lax.axis_size("shard")
    total = dot(lefts[0], right, (0, 0))
    for r in range(1, size):
        total = total + receive(dot(lefts[r], right, (0, 0), BF16), "shard", size - r).astype(F32)
    return total


def ahead_first(values, start, axis=0):
    return lax.dynamic_slice_in_dim(
        jnp.concatenate([values, values], axis=axis), start, values.shape[axis], axis=axis
    )


def gather_natural(values, axis_name, axis=0):
    return lax.all_gather(values, axis_name, axis=axis, tiled=True)


def row_order(values):
    values = ahead_first(values, lax.axis_index("ctx"))
    t = lax.axis_index("tp")
    return jnp.concatenate([lax.dynamic_index_in_dim(values, t ^ m, 1, False)[None] for m in masks("tp")], axis=0)


def natural_rows(values):
    t, order = lax.axis_index("tp"), masks("tp")
    part = values.shape[0] // len(order)
    found = []
    for q in range(len(order)):
        m, place = q ^ t, 0
        for i, bit in enumerate(reversed(bits("tp"))):
            place = place + jnp.where(m & bit, 1 << i, 0)
        found.append(lax.dynamic_slice_in_dim(values, place * part, part))
    return jnp.concatenate(found, axis=0)


def inverse_scale(values):
    return lax.rsqrt(jnp.mean(values * values, axis=-1, keepdims=True) + NORM_EPSILON)


def turn(values, cosine, sine):
    half = values.shape[-1] // 2
    front, back = values[..., :half], values[..., half:]
    return jnp.concatenate([front * cosine - back * sine, back * cosine + front * sine], axis=-1)


def norm_back(grad, values, gain):
    scale = inverse_scale(values)
    weighted = grad * gain
    middle = jnp.mean(values * weighted, axis=-1, keepdims=True)
    return scale * weighted - values * (scale * scale * scale) * middle, grad * values * scale


def local(
    tokens,
    segments,
    routes,
    cotangent,
    first_gain,
    head_gain,
    attention_in,
    attention_out,
    second_gain,
    router_weight,
    expert_in,
    expert_out,
):
    s, c, t = lax.axis_index("shard"), lax.axis_index("ctx"), lax.axis_index("tp")
    shards, ctxs, tps = lax.axis_size("shard"), lax.axis_size("ctx"), lax.axis_size("tp")
    rows, width = tokens.shape[1:]
    own = rows // tps
    block = width // shards
    every = rows * ctxs
    experts = router_weight.shape[1]
    group = experts // ctxs
    hidden_size = expert_out.shape[2]
    local_width = attention_out.shape[1]
    head_size = local_width // ctxs
    heads = head_size // HEAD_DIM

    gains = gather_natural(jnp.stack([first_gain, second_gain]), "shard", 1).astype(F32)
    gain_one, gain_two = gains[0], gains[1]
    head_gains = gather_natural(head_gain, "shard").astype(F32)
    head_in = lax.dynamic_slice_in_dim(attention_in, c * head_size, head_size, axis=2)
    head_in = gather_natural(head_in.reshape(block, 3 * head_size), "shard")
    exit_weight = gather_natural(ahead_first(attention_out, c * head_size, 1), "shard")
    router = gather_natural(router_weight, "shard")
    choices_all = gather_natural(routes[0], "ctx").reshape(ctxs, tps, own, -1)
    group_out = lax.dynamic_slice_in_dim(expert_out, c * group, group, axis=1)
    group_out = gather_natural(group_out.reshape(block, group * hidden_size), "shard")
    group_in = lax.dynamic_slice_in_dim(expert_in, c * group, group, axis=1)
    in_weights = [
        gather_natural(group_in[:, i].reshape(block, 2 * hidden_size), "shard") for i in range(group)
    ]

    first = t * own
    layer_in = lax.dynamic_slice_in_dim(tokens[0], first, own).astype(F32)
    cot_own = lax.dynamic_slice_in_dim(cotangent[0], first, own)
    upstream = cot_own.astype(F32)
    picks_all = jnp.any(row_order(choices_all)[..., None] == jnp.arange(experts), axis=3)
    picks = picks_all[0, 0]
    picks_all = picks_all.reshape(every, experts)

    normed_one = lower(layer_in * inverse_scale(layer_in) * gain_one)
    normed_one_all = gather_rows(normed_one)
    cot_own, _ = lax.optimization_barrier((cot_own, normed_one_all))
    cot_all = gather_rows(cot_own)
    spot = row_order(jnp.arange(every, dtype=jnp.int32).reshape(ctxs, tps, own)).reshape(-1)
    documents = row_order(segments[0].reshape(ctxs, tps, own)).reshape(-1)
    steps = jnp.arange(HEAD_DIM // 2).astype(F32)
    frequency = ROTARY_BASE ** (-2.0 * steps / HEAD_DIM)
    angles = spot.astype(F32)[:, None] * frequency[None, :]
    cosine, sine = jnp.cos(angles)[:, None], jnp.sin(angles)[:, None]
    projected = dot(normed_one_all, head_in, (1, 0)).reshape(every, 3, heads, HEAD_DIM)
    query_raw, key_raw = projected[:, 0], projected[:, 1]
    gain_q, gain_k = head_gains[:HEAD_DIM], head_gains[HEAD_DIM:]
    queries = lower(turn(query_raw * inverse_scale(query_raw) * gain_q, cosine, sine))
    keys = lower(turn(key_raw * inverse_scale(key_raw) * gain_k, cosine, sine))
    values = lower(projected[:, 2])
    scale = HEAD_DIM ** (-0.5)
    scores = jnp.einsum("qhd,khd->hqk", queries, keys, preferred_element_type=F32) * scale
    same = documents[:, None] == documents[None, :]
    chances = jax.nn.softmax(jnp.where(same[None], scores, MASKED), axis=-1)
    chances_low = lower(chances)
    mixed_head = lower(jnp.einsum("hqk,khd->qhd", chances_low, values, preferred_element_type=F32))
    blocks = mixed_head.reshape(tps, ctxs, own, head_size)
    mixed = [blocks[:, 0]] + [receive(blocks[:, ctxs - j], "ctx", j) for j in range(1, ctxs)]
    mixed = jnp.concatenate([m.reshape(rows, head_size) for m in mixed], axis=1)
    residual = layer_in + scatter_tp(dot(mixed, exit_weight, (1, 1)))

    normed_two = lower(residual * inverse_scale(residual) * gain_two)
    normed_two_all = gather_rows(normed_two)
    chances_all = jax.nn.softmax(dot(normed_two_all, router, (1, 0)), axis=-1)
    gates = jnp.where(picks_all, chances_all, 0.0)
    gates = lax.dynamic_slice_in_dim(gates, c * group, group, axis=1)
    out_weights = [group_out[:, i * hidden_size : (i + 1) * hidden_size] for i in range(group)]
    normed_blocks = [own_block(normed_two_all, r, 1) for r in range(shards)]
    cot_blocks = [own_block(cot_all, r, 1) for r in range(shards)]
    backs = dot(cot_all, group_out, (1, 0))
    scaled, gate_parts, inner_grads, chunks = [], [], [], []
    rows_now = normed_two_all
    for i in range(group):
        gate_up = dot(rows_now, in_weights[i], (1, 0))
        gate, up = gate_up[:, :hidden_size], gate_up[:, hidden_size:]
        back = backs[:, i * hidden_size : (i + 1) * hidden_size]
        sigmoid = jax.nn.sigmoid(gate)
        silu = gate * sigmoid
        hidden = lower(silu * up).astype(F32)
        weight = gates[:, i : i + 1]
        scaled.append(lower(hidden * weight))
        gate_parts.append(jnp.sum(hidden * back, axis=1))
        hidden_grad = back * weight
        inner_grads.append(
            lower(
                jnp.concatenate(
                    [hidden_grad * up * sigmoid * (1.0 + gate * (1.0 - sigmoid)), hidden_grad * silu], axis=1
                )
            )
        )
        upward = product_shard(normed_blocks, inner_grads[i])
        downward = product_shard(cot_blocks, scaled[i])
        chunks.append(
            lax.all_gather(lower(jnp.concatenate([upward, downward], axis=1)), "ctx", axis=0, tiled=False)
        )
        rows_now, _ = lax.optimization_barrier((normed_two_all, scaled[i]))

    normed_part = sum(dot(inner_grads[i], in_weights[i], (1, 1)) for i in range(group))
    gate_part = lax.dynamic_update_slice(
        jnp.zeros((every, 128), F32), jnp.stack(gate_parts, axis=1), (0, c * group)
    )
    normed_sum = scatter_rows(jnp.concatenate([normed_part, gate_part], axis=1))
    normed_sum, gate_grad = normed_sum[:, :width], normed_sum[:, width : width + experts]
    result_part = dot(jnp.concatenate(scaled, axis=1), group_out, (1, 1))
    result_part, _ = lax.optimization_barrier((result_part, normed_sum))
    result_sum = scatter_rows(result_part)
    layer_output = natural_rows(gather_tp(lower(residual + result_sum)))[None]

    router_chances = jax.nn.softmax(dot(normed_two, router, (1, 0)), axis=-1)
    chance_grad = jnp.where(picks, gate_grad, 0.0)
    logit_grad = lower(
        router_chances * (chance_grad - jnp.sum(router_chances * chance_grad, axis=-1, keepdims=True))
    )
    router_part = dot(logit_grad, normed_two, (0, 0))
    normed_grad = normed_sum + dot(logit_grad, router, (1, 1))
    residual_back, second_part = norm_back(normed_grad, residual, gain_two)
    residual_grad = upstream + residual_back

    attend_grad = gather_tp(lower(residual_grad))
    exit_part = product_shard([own_block(attend_grad, r, 1) for r in range(shards)], mixed)
    exit_head = exit_part[:, :head_size]
    for r in range(1, ctxs):
        exit_head = exit_head + receive(
            lower(exit_part[:, r * head_size : (r + 1) * head_size]), "ctx", ctxs - r
        ).astype(F32)
    mixed_grad = lower(dot(attend_grad, exit_weight, (1, 0))).reshape(tps, own, ctxs, head_size)
    parts = [mixed_grad[:, :, 0]] + [receive(mixed_grad[:, :, ctxs - j], "ctx", j) for j in range(1, ctxs)]
    mixed_grad = jnp.stack(parts, axis=1).reshape(every, heads, HEAD_DIM)
    weight_grad = jnp.einsum("qhd,khd->hqk", mixed_grad, values, preferred_element_type=F32)
    score_grad = lower(chances * (weight_grad - jnp.sum(chances * weight_grad, axis=-1, keepdims=True)))
    query_grad = jnp.einsum("hqk,khd->qhd", score_grad, keys, preferred_element_type=F32) * scale
    key_grad = jnp.einsum("hqk,qhd->khd", score_grad, queries, preferred_element_type=F32) * scale
    value_grad = jnp.einsum("hqk,qhd->khd", chances_low, mixed_grad, preferred_element_type=F32)
    query_raw_grad, gain_q_part = norm_back(turn(query_grad, cosine, -sine), query_raw, gain_q)
    key_raw_grad, gain_k_part = norm_back(turn(key_grad, cosine, -sine), key_raw, gain_k)
    projected_grad = lower(
        jnp.stack([query_raw_grad, key_raw_grad, value_grad], axis=1).reshape(every, 3 * head_size)
    )
    entry_head = product_shard([own_block(normed_one_all, r, 1) for r in range(shards)], projected_grad)
    attention_chunk = lax.all_gather(
        lower(jnp.concatenate([entry_head, exit_head], axis=1)), "ctx", axis=0, tiled=False
    )
    first_normed_grad = scatter_rows(dot(projected_grad, head_in, (1, 1)))
    input_back, first_part = norm_back(first_normed_grad, layer_in, gain_one)
    input_gradient = natural_rows(gather_tp(lower(residual_grad + input_back))).astype(F32)[None]

    early = jnp.concatenate([jnp.sum(second_part, axis=0)[None], router_part], axis=0)
    early = sum_shard(sum_tokens(early), 1)
    head_part = jnp.concatenate([jnp.sum(gain_q_part, axis=(0, 1)), jnp.sum(gain_k_part, axis=(0, 1))])
    late = sum_tokens(jnp.concatenate([jnp.sum(first_part, axis=0), head_part])[None])
    first_gradient = sum_shard(late[:, :width], 1)[0]
    head_gradient = sum_shard(late[:, width:], 1)[0]

    wide = jnp.moveaxis(attention_chunk, 0, 1).astype(F32)
    entry_gradient = jnp.moveaxis(
        wide[:, :, : 3 * head_size].reshape(block, ctxs, 3, head_size), 1, 2
    ).reshape(block, 3, local_width)
    exit_gradient = wide[:, :, 3 * head_size :].reshape(block, local_width)
    upward_gradient = jnp.stack([chunk[:, :, : 2 * hidden_size] for chunk in chunks], axis=1)
    upward_gradient = jnp.moveaxis(upward_gradient, 2, 0).astype(F32)
    upward_gradient = upward_gradient.reshape(block, experts, 2, hidden_size)
    downward_gradient = jnp.stack([chunk[:, :, 2 * hidden_size :] for chunk in chunks], axis=1)
    downward_gradient = jnp.moveaxis(downward_gradient, 2, 0).astype(F32)
    downward_gradient = downward_gradient.reshape(block, experts, hidden_size)
    return (
        layer_output,
        input_gradient,
        first_gradient,
        head_gradient,
        entry_gradient,
        exit_gradient,
        early[0],
        early[1:].T,
        upward_gradient,
        downward_gradient,
    )


def solution(mesh):
    return jax.shard_map(
        local,
        mesh=mesh,
        in_specs=(
            P("shard", "ctx", None),
            P("shard", None),
            P("shard", "ctx", None),
            P("shard", "ctx", None),
            P("shard"),
            P("shard"),
            P("shard", None, "tp"),
            P("shard", "tp"),
            P("shard"),
            P("shard", None),
            P("shard", None, None, "tp"),
            P("shard", None, "tp"),
        ),
        out_specs=(
            P("shard", "ctx", None),
            P("shard", "ctx", None),
            P("shard"),
            P("shard"),
            P("shard", None, "tp"),
            P("shard", "tp"),
            P("shard"),
            P("shard", None),
            P("shard", None, None, "tp"),
            P("shard", None, "tp"),
        ),
        check_vma=False,
    )
```

time: 4790 us -> 1200 us (0.25)
  waiting for transfers between devices: 3960 us -> 525 us
  matrix products: 275 us -> 191 us
  other arithmetic: 180 us -> 96.5 us
  starting transfers between devices: 2.82 us -> 83.9 us
    psum x4 -> x0, waiting for transfers between devices: 2080 us -> none  [the longest x1 1900 us: local(): lax.psum((attention_rows[0], attention_rows[1], attention_rows[2], attent...]
    reduce_scatter x6 -> x0, waiting for transfers between devices: 1220 us -> none  [the longest x1 731 us: local(): lax.psum_scatter(upward, 'shard', scatter_dimension=0, tiled=True)]
    all_gather x5 -> x12, waiting for transfers between devices: 653 us -> 0.04 us  [the longest x7 0.03 us: gather_natural(): return lax.all_gather(values, axis_name, axis=axis, tiled=True)]
    ppermute x0 -> x86, waiting for transfers between devices: none -> 524 us  [the longest x40 347 us: receive(): lax.ppermute(values, axis, [((i + distance) % size, i) for i in range(siz...]
    scatter-add x2 -> x0, other arithmetic: 108 us -> none  [the longest x1 54.1 us: local(): partial_normed = jnp.zeros((row_count, width), jnp.float32).at[slot_token...]
    dot_general x21 -> x44, matrix products: 275 us -> 191 us  [the longest x38 177 us: dot(): lax.dot_general(left, right, (((over[0],), (over[1],)), ((), ())), prefer...]
    ppermute x0 -> x86, starting transfers between devices: none -> 83.4 us  [the longest x40 45.9 us: receive(): lax.ppermute(values, axis, [((i + distance) % size, i) for i in range(siz...]
    gather x4 -> x0, local copies, waits for them, and re-layouts: 58.8 us -> none  [the longest x2 25 us: local(): partial_gates = gate_part[saved['slots'], saved['choices_made']]]
  transfers between devices with their start and end apart: 15 -> 98, of which waited for: 11 -> 47; matrix products, arithmetic and copies ran while one was open for 8% -> 39% of each run, Pallas kernels for 0% -> 0%
where the time goes in v1:
time: 1200 us; the launch traced here: 1190 us
  waiting for transfers between devices  525 us (44%)
  local copies, waits for them, and re-layouts  248 us (21%)
  matrix products  191 us (16%)
  other arithmetic  96.5 us (8%)
  starting transfers between devices  83.9 us (7%)
  blocking collectives  27.7 us (2%)
  between operations  17 us (1%)
    ppermute x40, waiting for transfers between devices, receive(): lax.ppermute(values, axis, [((i + distance) % size, i) for i in range(siz...  347 us
    ppermute x46, waiting for transfers between devices, swap(): return lax.ppermute(values, axis, [(i, i ^ bit) for i in range(size)])  178 us
    dot_general x38, matrix products, dot(): lax.dot_general(left, right, (((over[0],), (over[1],)), ((), ())), prefer...  177 us
    unnamed x314, local copies, waits for them, and re-layouts  163 us
    ppermute x40, starting transfers between devices, receive(): lax.ppermute(values, axis, [((i + distance) % size, i) for i in range(siz...  45.9 us
    ppermute x46, starting transfers between devices, swap(): return lax.ppermute(values, axis, [(i, i ^ bit) for i in range(size)])  37.5 us
    all_gather x4, blocking collectives, gather_natural(): return lax.all_gather(values, axis_name, axis=axis, tiled=True)  27.7 us
  transfers between devices with their start and end apart: 98, of which 47 were waited for; matrix products, arithmetic and copies ran while one was open for 39% of the time, Pallas kernels for 0%

profile of v1, /device:TPU:0, one launch (start us, length us, event | category | flops | bytes accessed | tf_op | source)
XLA Modules:
  0.0 1188.4 jit_solution(3259119741204251169)
XLA Ops:
  53.1 21.5 %collective-permute-done.1 = bf16[96,2048]{1,0:T(8,128)(2,1)S(1)} collective-permute-done((bf16[96,2048]{1,0:T(8,128)(2,1)S(1)}, bf16[96,2048]{1,0:T(8,128)(2,1)S(1)}, u32[]{:S(2)}, u32[]{:S(2)}) %collective-permute-start.1) | collective-permute-done | bytes 393248 | tf_op jit(solution)/shard_map/ppermute | solution.py:25
  102.1 13.2 %all-gather = s32[1,1536,8]{1,2,0:T(8,128)S(1)} all-gather(s32[1,384,8]{1,2,0:T(8,128)S(1)} %copy-done.100), channel_id=2, replica_groups=mesh['shard'=2,'ctx'=4,'tp'=4] {'ctx'}, dimensions={1}, use_global_device_ids=true | all-gather | bytes 61440 | tf_op jit(solution)/shard_map/all_gather | solution.py:126
  149.9 30.6 %collective-permute-done.9 = bf16[4,96,128]{2,1,0:T(8,128)(2,1)S(1)} collective-permute-done((bf16[4,96,128]{2,1,0:T(8,128)(2,1)S(1)}, bf16[4,96,128]{2,1,0:T(8,128)(2,1)S(1)}, u32[]{:S(2)}, u32[]{:S(2)}) %collective-permute-start.9) | collective-permute-done | bytes 98336 | tf_op jit(solution)/shard_map/ppermute | solution.py:25
  241.2 21.3 %collective-permute-done.14 = bf16[96,2048]{1,0:T(8,128)(2,1)S(1)} collective-permute-done((bf16[96,2048]{1,0:T(8,128)(2,1)S(1)}, bf16[96,2048]{1,0:T(8,128)(2,1)S(1)}, u32[]{:S(2)}, u32[]{:S(2)}) %collective-permute-start.14) | collective-permute-done | bytes 393248 | tf_op jit(solution)/shard_map/ppermute | solution.py:25
  291.3 11.7 fusion.333
  358.7 30.2 %collective-permute-done.85 = bf16[1024,256]{0,1:T(8,128)(2,1)} collective-permute-done((bf16[1024,256]{0,1:T(8,128)(2,1)}, bf16[1024,256]{0,1:T(8,128)(2,1)}, u32[]{:S(2)}, u32[]{:S(2)}) %collective-permute-start.85) | collective-permute-done | bytes 524320 | tf_op jit(solution)/shard_map/ppermute | solution.py:25
  416.5 29.7 %collective-permute-done.83 = bf16[1024,256]{0,1:T(8,128)(2,1)S(1)} collective-permute-done((bf16[1024,256]{0,1:T(8,128)(2,1)S(1)}, bf16[1024,256]{0,1:T(8,128)(2,1)S(1)}, u32[]{:S(2)}, u32[]{:S(2)}) %collective-permute-start.83) | collective-permute-done | bytes 524320 | tf_op jit(solution)/shard_map/ppermute | solution.py:25
  454.9 9.4 fusion.6
  499.6 19.1 %add_add_fusion = f32[1536,2048]{1,0:T(8,128)} fusion(f32[1536,2048]{1,0:T(8,128)} %fusion.242, f32[1536,2048]{1,0:T(8,128)} %fusion.244, f32[1536,2048]{1,0:T(8,128)} %fusion.243, bf16[2048,512]{1,0:T(8,128)(2,1)} %all-gather.25.cloned.1.call-done, bf16[1536,256]{0,1:T(8,128)(2,1)S(1)} %copy-done.28, bf16[1536,256]{0,1:T(8,128)(2,1)S(1)} %copy-done.25), kind=kOutput, calls=%fused_computation.3 | convolution fusion | flops 3233808384 | bytes 54001664 | tf_op jit(solution)/shard_map/dot_general | solution.py:19
  561.6 8.3 collective-permute-done.31
  570.2 8.6 collective-permute-done.35
  579.2 8.6 collective-permute-done.33
  596.2 8.4 collective-permute-done.43
  605.2 7.9 collective-permute-done.41
  625.0 47.0 %collective-permute-done.34 = bf16[96,2176]{1,0:T(8,128)(2,1)S(1)} collective-permute-done((bf16[96,2176]{1,0:T(8,128)(2,1)S(1)}, bf16[96,2176]{1,0:T(8,128)(2,1)S(1)}, u32[]{:S(2)}, u32[]{:S(2)}) %collective-permute-start.34) | collective-permute-done | bytes 417824 | tf_op jit(solution)/shard_map/ppermute | solution.py:25
  673.8 60.9 %collective-permute-done.42 = bf16[96,2048]{1,0:T(8,128)(2,1)S(1)} collective-permute-done((bf16[96,2048]{1,0:T(8,128)(2,1)S(1)}, bf16[96,2048]{1,0:T(8,128)(2,1)S(1)}, u32[]{:S(2)}, u32[]{:S(2)}) %collective-permute-start.42) | collective-permute-done | bytes 393248 | tf_op jit(solution)/shard_map/ppermute | solution.py:25
  828.2 18.1 %collective-permute-done.75 = f32[17,2048]{1,0:T(8,128)S(1)} collective-permute-done((f32[17,2048]{1,0:T(8,128)S(1)}, f32[17,2048]{1,0:T(8,128)S(1)}, u32[]{:S(2)}, u32[]{:S(2)}) %collective-permute-start.75) | collective-permute-done | bytes 139296 | tf_op jit(solution)/shard_map/ppermute | solution.py:30
  846.6 24.7 %collective-permute-done.76 = f32[17,2048]{1,0:T(8,128)} collective-permute-done((f32[17,2048]{1,0:T(8,128)S(1)}, f32[17,2048]{1,0:T(8,128)}, u32[]{:S(2)}, u32[]{:S(2)}) %collective-permute-start.76) | collective-permute-done | bytes 139296 | tf_op jit(solution)/shard_map/ppermute | solution.py:30
  896.5 11.1 collective-permute-done.69
  931.8 21.0 %collective-permute-done.71 = bf16[1024,128]{0,1:T(8,128)(2,1)S(1)} collective-permute-done((bf16[1024,128]{0,1:T(8,128)(2,1)S(1)}, bf16[1024,128]{0,1:T(8,128)(2,1)S(1)}, u32[]{:S(2)}, u32[]{:S(2)}) %collective-permute-start.71) | collective-permute-done | bytes 262176 | tf_op jit(solution)/shard_map/ppermute | solution.py:25
  955.6 31.2 %collective-permute-done.57 = bf16[96,2048]{1,0:T(8,128)(2,1)S(1)} collective-permute-done((bf16[96,2048]{1,0:T(8,128)(2,1)S(1)}, bf16[96,2048]{1,0:T(8,128)(2,1)S(1)}, u32[]{:S(2)}, u32[]{:S(2)}) %collective-permute-start.57) | collective-permute-done | bytes 393248 | tf_op jit(solution)/shard_map/ppermute | solution.py:25
  1054.5 18.5 %maximum_convert_fusion = f32[4,4,1024,512]{2,3,1,0:T(8,128)} fusion(bf16[4,1,1024,512]{2,3,1,0:T(8,128)(2,1)} %bitcast.399, bf16[4,1,1024,512]{2,3,1,0:T(8,128)(2,1)} %bitcast.400, bf16[4,1,1024,512]{2,3,1,0:T(8,128)(2,1)} %bitcast.401, bf16[4,1,1024,512]{2,3,1,0:T(8,128)(2,1)} %bitcast.402), kind=kLoop, calls=%fused_computation | loop fusion | flops 33554432 | bytes 50331648 | tf_op jit(solution)/shard_map/reshape | solution.py:340
  1073.0 48.5 %copy.276 = f32[1024,16,2,256]{3,2,1,0:T(2,128)} copy(f32[1024,16,2,256]{0,3,2,1:T(8,128)} %bitcast.380) | data formatting | bytes 67108864
  1129.9 22.9 %copy.277 = f32[1024,16,256]{2,1,0:T(8,128)} copy(f32[1024,16,256]{2,0,1:T(8,128)S(1)} %bitcast.383) | data formatting | bytes 33554432
  (714 shorter events, 638.8 us)
Async XLA Ops:
  7.2 114.9 %all-gather.15.cloned.1.call-start = ((), (), s32[]{:S(2)}) async-start(), calls=%async_computation | async-start | bytes 2359296 | tf_op jit(solution)/shard_map/all_gather | solution.py:126
  12.4 169.6 %all-gather.17.cloned.1.call-start = ((), (), s32[]{:S(2)}) async-start(), calls=%async_computation.1 | async-start | bytes 3145728 | tf_op jit(solution)/shard_map/all_gather | solution.py:126
  15.1 276.2 %all-gather.27.cloned.1.call-start = ((), (), s32[]{:S(2)}) async-start(), calls=%async_computation.6 | async-start | bytes 6291456 | tf_op jit(solution)/shard_map/all_gather | solution.py:126
  21.4 288.4 %all-gather.19.cloned.1.call-start = ((), (), s32[]{:S(2)}) async-start(), calls=%async_computation.2 | async-start | bytes 3145728 | tf_op jit(solution)/shard_map/all_gather | solution.py:126
  27.4 290.3 %all-gather.21.cloned.1.call-start = ((), (), s32[]{:S(2)}) async-start(), calls=%async_computation.3 | async-start | bytes 3145728 | tf_op jit(solution)/shard_map/all_gather | solution.py:126
  28.7 298.7 %all-gather.23.cloned.1.call-start = ((), (), s32[]{:S(2)}) async-start(), calls=%async_computation.4 | async-start | bytes 3145728 | tf_op jit(solution)/shard_map/all_gather | solution.py:126
  45.6 291.5 %all-gather.25.cloned.1.call-start = ((), (), s32[]{:S(2)}) async-start(), calls=%async_computation.5 | async-start | bytes 3145728 | tf_op jit(solution)/shard_map/all_gather | solution.py:126
  96.8 914.8 %all-gather.37.cloned.1.call-start = ((), (), s32[]{:S(2)}) async-start(), calls=%async_computation.11 | async-start | bytes 7864320 | tf_op jit(solution)/shard_map/all_gather | solution.py:273
  215.7 71.5 %collective-permute-start.28 = (bf16[768,2048]{1,0:T(8,128)(2,1)}, bf16[768,2048]{1,0:T(8,128)(2,1)}, u32[]{:S(2)}, u32[]{:S(2)}) collective-permute-start(bf16[768,2048]{1,0:T(8,128)(2,1)} %get-tuple-element.198), channel_id=1, source_target_pairs={{0,1},{1,0},{2,3},{3,2},{4,5},{5,4},{6,7},{7,6},{8,9},{9,8},{10,11... | collective-permute-start | bytes 9437192 | tf_op jit(solution)/shard_map/ppermute | solution.py:30
  400.0 622.2 %all-gather.35.cloned.1.call-start = ((), (), s32[]{:S(2)}) async-start(), calls=%async_computation.10 | async-start | bytes 7864320 | tf_op jit(solution)/shard_map/all_gather | solution.py:273
  454.7 578.2 %all-gather.33.cloned.1.call-start = ((), (), s32[]{:S(2)}) async-start(), calls=%async_computation.9 | async-start | bytes 7864320 | tf_op jit(solution)/shard_map/all_gather | solution.py:273
  466.8 78.8 %collective-permute-start.37 = (bf16[768,2048]{1,0:T(8,128)(2,1)}, bf16[768,2048]{1,0:T(8,128)(2,1)}, u32[]{:S(2)}, u32[]{:S(2)}) collective-permute-start(bf16[768,2048]{1,0:T(8,128)(2,1)} %slice.747), channel_id=1, source_target_pairs={{0,1},{1,0},{2,3},{3,2},{4,5},{5,4},{6,7},{7,6},{8,9},{9,8},{10,11... | collective-permute-start | bytes 9437192 | tf_op jit(solution)/shard_map/ppermute | solution.py:30
  473.0 55.1 %collective-permute-start.81 = (bf16[1024,256]{0,1:T(8,128)(2,1)}, bf16[1024,256]{0,1:T(8,128)(2,1)}, u32[]{:S(2)}, u32[]{:S(2)}) collective-permute-start(bf16[1024,256]{0,1:T(8,128)(2,1)} %fusion.142), channel_id=1, source_target_pairs={{16,0},{0,16},{17,1},{1,17},{18,2},{2,18},{19,3},{3,19},{20,4},{4,... | collective-permute-start | bytes 1572872 | tf_op jit(solution)/shard_map/ppermute | solution.py:25
  537.0 506.7 %all-gather.31.cloned.1.call-start = ((), (), s32[]{:S(2)}) async-start(), calls=%async_computation.8 | async-start | bytes 7864320 | tf_op jit(solution)/shard_map/all_gather | solution.py:273
  544.1 210.4 %collective-permute-start.78 = (bf16[1024,512]{0,1:T(8,128)(2,1)}, bf16[1024,512]{0,1:T(8,128)(2,1)}, u32[]{:S(2)}, u32[]{:S(2)}) collective-permute-start(bf16[1024,512]{0,1:T(8,128)(2,1)} %fusion.81), channel_id=1, source_target_pairs={{16,0},{0,16},{17,1},{1,17},{18,2},{2,18},{19,3},{3,19},{20,4},{4,... | collective-permute-start | bytes 3145736 | tf_op jit(solution)/shard_map/ppermute | solution.py:25
  604.6 67.4 %collective-permute-start.34 = (bf16[96,2176]{1,0:T(8,128)(2,1)S(1)}, bf16[96,2176]{1,0:T(8,128)(2,1)S(1)}, u32[]{:S(2)}, u32[]{:S(2)}) collective-permute-start(bf16[96,2176]{1,0:T(8,128)(2,1)S(1)} %get-tuple-element.147), channel_id=1, source_target_pairs={{8,0},{12,4},{0,8},{4,12},{9,1},{13,5},{1,9},{5,13},{10,2},{14,6},... | collective-permute-start | bytes 1253384 | tf_op jit(solution)/shard_map/ppermute | solution.py:25
  613.1 59.0 %collective-permute-start.32 = (bf16[96,2176]{1,0:T(8,128)(2,1)S(1)}, bf16[96,2176]{1,0:T(8,128)(2,1)S(1)}, u32[]{:S(2)}, u32[]{:S(2)}) collective-permute-start(bf16[96,2176]{1,0:T(8,128)(2,1)S(1)} %get-tuple-element.145), channel_id=1, source_target_pairs={{12,0},{0,4},{4,8},{8,12},{13,1},{1,5},{5,9},{9,13},{14,2},{2,6},{... | collective-permute-start | bytes 1253384 | tf_op jit(solution)/shard_map/ppermute | solution.py:25
  621.2 52.7 %collective-permute-start.38 = (bf16[96,2048]{1,0:T(8,128)(2,1)S(1)}, bf16[96,2048]{1,0:T(8,128)(2,1)S(1)}, u32[]{:S(2)}, u32[]{:S(2)}) collective-permute-start(bf16[96,2048]{1,0:T(8,128)(2,1)S(1)} %get-tuple-element.166), channel_id=1, source_target_pairs={{0,2},{1,3},{2,0},{3,1},{4,6},{5,7},{6,4},{7,5},{8,10},{9,11},{10,... | collective-permute-start | bytes 1179656 | tf_op jit(solution)/shard_map/ppermute | solution.py:30
  672.1 62.7 %collective-permute-start.42 = (bf16[96,2048]{1,0:T(8,128)(2,1)S(1)}, bf16[96,2048]{1,0:T(8,128)(2,1)S(1)}, u32[]{:S(2)}, u32[]{:S(2)}) collective-permute-start(bf16[96,2048]{1,0:T(8,128)(2,1)S(1)} %get-tuple-element.157), channel_id=1, source_target_pairs={{8,0},{12,4},{0,8},{4,12},{9,1},{13,5},{1,9},{5,13},{10,2},{14,6},... | collective-permute-start | bytes 1179656 | tf_op jit(solution)/shard_map/ppermute | solution.py:25
  672.1 62.7 %collective-permute-start.40 = (bf16[96,2048]{1,0:T(8,128)(2,1)S(1)}, bf16[96,2048]{1,0:T(8,128)(2,1)S(1)}, u32[]{:S(2)}, u32[]{:S(2)}) collective-permute-start(bf16[96,2048]{1,0:T(8,128)(2,1)S(1)} %get-tuple-element.155), channel_id=1, source_target_pairs={{12,0},{0,4},{4,8},{8,12},{13,1},{1,5},{5,9},{9,13},{14,2},{2,6},{... | collective-permute-start | bytes 1179656 | tf_op jit(solution)/shard_map/ppermute | solution.py:25
  760.4 396.0 %all-gather.29.cloned.1.call-start = ((), (), s32[]{:S(2)}) async-start(), calls=%async_computation.7 | async-start | bytes 5242880 | tf_op jit(solution)/shard_map/all_gather | solution.py:319
  810.3 78.5 %collective-permute-start.52 = (bf16[768,2048]{1,0:T(8,128)(2,1)}, bf16[768,2048]{1,0:T(8,128)(2,1)}, u32[]{:S(2)}, u32[]{:S(2)}) collective-permute-start(bf16[768,2048]{1,0:T(8,128)(2,1)} %slice.746), channel_id=1, source_target_pairs={{0,1},{1,0},{2,3},{3,2},{4,5},{5,4},{6,7},{7,6},{8,9},{9,8},{10,11... | collective-permute-start | bytes 9437192 | tf_op jit(solution)/shard_map/ppermute | solution.py:30
  926.5 60.3 %collective-permute-start.57 = (bf16[96,2048]{1,0:T(8,128)(2,1)S(1)}, bf16[96,2048]{1,0:T(8,128)(2,1)S(1)}, u32[]{:S(2)}, u32[]{:S(2)}) collective-permute-start(bf16[96,2048]{1,0:T(8,128)(2,1)S(1)} %get-tuple-element.150), channel_id=1, source_target_pairs={{8,0},{12,4},{0,8},{4,12},{9,1},{13,5},{1,9},{5,13},{10,2},{14,6},... | collective-permute-start | bytes 1179656 | tf_op jit(solution)/shard_map/ppermute | solution.py:25
  1011.6 141.3 %collective-permute-start.61 = (bf16[192,2048]{1,0:T(8,128)(2,1)}, bf16[192,2048]{1,0:T(8,128)(2,1)}, u32[]{:S(2)}, u32[]{:S(2)}) collective-permute-start(bf16[192,2048]{1,0:T(8,128)(2,1)} %pad_maximum_fusion.18), channel_id=1, source_target_pairs={{0,1},{1,0},{2,3},{3,2},{4,5},{5,4},{6,7},{7,6},{8,9},{9,8},{10,11... | collective-permute-start | bytes 2359304 | tf_op jit(solution)/shard_map/ppermute | solution.py:30
  (210 other events, 4537.7 us)
Sparse Core Ops, SparseCore 0:
  12.5 29.9 all-gather.14
  44.7 33.1 all-gather.16
  79.9 56.7 all-gather.26
  138.1 33.1 all-gather.18
  172.7 33.1 all-gather.20
  207.8 33.1 all-gather.22
  242.5 33.1 all-gather.24
  400.2 112.8 all-gather.36
  514.6 148.1 all-gather.34
  664.2 143.3 all-gather.32
  809.1 145.8 all-gather.30
  990.2 79.3 all-gather.28

commit v2 on v1

--- a/solution.py
+++ b/solution.py
@@ -1,6 +1,10 @@
+import functools
+
 import jax
 import jax.numpy as jnp
 from jax import lax
+from jax.experimental import pallas as pl
+from jax.experimental.pallas import tpu as pltpu
 from jax.sharding import PartitionSpec as P
 
 HEAD_DIM = 128
@@ -57,33 +61,180 @@
     return values
 
 
+def spread_tp(block):
+    parts = [block]
+    for bit in reversed(bits("tp")[1:]):
+        parts = parts + [swap(part, "tp", bit) for part in parts]
+    return jnp.concatenate(parts + [swap(part, "tp", 1) for part in parts], axis=0)
+
+
+def gather_ctx(values):
+    size = lax.axis_size("ctx")
+    whole = jnp.concatenate([values] + [receive(values, "ctx", r) for r in range(1, size)], axis=0)
+    return ahead_first(whole, lax.rem(size - lax.axis_index("ctx"), size) * values.shape[0])
+
+
+def greet(peers):
+    barrier = pltpu.get_barrier_semaphore()
+    for peer in peers:
+        pl.semaphore_signal(barrier, inc=1, device_id=peer, device_id_type=pl.DeviceIdType.MESH)
+    pl.semaphore_wait(barrier, len(peers))
+
+
+def remote(source, target, sent, arrived, place, peer):
+    return pltpu.make_async_remote_copy(
+        src_ref=source,
+        dst_ref=target,
+        send_sem=sent.at[place],
+        recv_sem=arrived.at[place],
+        device_id=peer,
+        device_id_type=pl.DeviceIdType.MESH,
+    )
+
+
+def far_first(size):
+    return sorted(range(1, size), key=lambda r: min(r, size - r))
+
+
+def gather_kernel(size, pieces, own, out, local, z_sent, z_here, x_sent, x_here, core_sent, core_here):
+    c, t = lax.axis_index("ctx"), lax.axis_index("tp")
+    x_peer, core_peer = {"tp": t ^ 2}, {"tp": t ^ 1}
+    behind = {r: {"ctx": lax.rem(c + size - r, size)} for r in range(1, size)}
+    greet([x_peer, core_peer] + [behind[r] for r in range(1, size)])
+    step = own.shape[0] // pieces
+    rows = [pl.ds(h * step, step) for h in range(pieces)]
+    spot = [lax.rem(c + r, size) for r in range(size)]
+    keep = pltpu.make_async_copy(own, out.at[0, c], local)
+    keep.start()
+    order = [(r, h) for r in far_first(size) for h in range(pieces)]
+    mine = [(0, h) for h in range(pieces)]
+    z = {
+        (r, h): remote(own.at[rows[h]], out.at[0, c, rows[h]], z_sent, z_here, (r - 1) * pieces + h, behind[r])
+        for r, h in order
+    }
+    x, core = {}, {}
+    for r, h in mine + order:
+        source = own.at[rows[h]] if r == 0 else out.at[0, spot[r], rows[h]]
+        near, far = [out.at[1 + m, spot[r], rows[h]] for m in range(2)], out.at[3, spot[r], rows[h]]
+        place = r * pieces + h
+        x[r, h] = remote(source, near[0], x_sent, x_here, place, x_peer)
+        core[0, r, h] = remote(source, near[1], core_sent, core_here, place, core_peer)
+        core[1, r, h] = remote(near[0], far, core_sent, core_here, size * pieces + place, core_peer)
+    for key in order:
+        z[key].start()
+    for key in mine:
+        x[key].start()
+        core[(0,) + key].start()
+    for key in order:
+        z[key].wait_recv()
+        x[key].start()
+        core[(0,) + key].start()
+    for key in mine + order:
+        x[key].wait_recv()
+        core[(1,) + key].start()
+    for copy in core.values():
+        copy.wait()
+    for copy in list(x.values()) + list(z.values()):
+        copy.wait_send()
+    keep.wait()
+
+
 def gather_rows(values):
     size = lax.axis_size("ctx")
-    blocks = [[values] + [receive(values, "ctx", r) for r in range(1, size)]]
-    for bit in reversed(bits("tp")[1:]):
-        blocks = blocks + [[swap(v, "tp", bit) for v in part] for part in blocks]
-    values = jnp.concatenate([v for part in blocks for v in part], axis=0)
-    return jnp.concatenate([values, swap(values, "tp", 1)], axis=0)
-
-
-def scatter_rows(values):
+    assert lax.axis_size("tp") == 4
+    pieces = 2
+    count = size * pieces
+    return pl.pallas_call(
+        functools.partial(gather_kernel, size, pieces),
+        out_shape=jax.ShapeDtypeStruct((4, size) + values.shape, values.dtype),
+        in_specs=[pl.BlockSpec(memory_space=pl.ANY)],
+        out_specs=pl.BlockSpec(memory_space=pl.ANY),
+        scratch_shapes=[pltpu.SemaphoreType.DMA(())]
+        + [pltpu.SemaphoreType.DMA((n,)) for n in (count - pieces, count - pieces, count, count, 2 * count, 2 * count)],
+        compiler_params=pltpu.CompilerParams(collective_id=0, has_side_effects=True),
+        name="gather_rows",
+    )(values)
+
+
+def scatter_kernel(size, parts, out, held, core_in, x_in, z_in, local, z_sent, z_here, x_sent, x_here, core_sent, core_here):
+    c, t = lax.axis_index("ctx"), lax.axis_index("tp")
+    x_peer, core_peer = {"tp": t ^ 2}, {"tp": t ^ 1}
+    ahead = {r: {"ctx": lax.rem(c + r, size)} for r in range(1, size)}
+    greet([x_peer, core_peer] + [ahead[r] for r in range(1, size)])
+    spot = [lax.rem(c + r, size) for r in range(size)]
+    keep = pltpu.make_async_copy(parts.at[pl.ds(0, 2)], held, local)
+    keep.start()
+    order = far_first(size) + [0]
+    core = {
+        (m, r): remote(parts.at[2 + m, spot[r]], core_in.at[m, r], core_sent, core_here, m * size + r, core_peer)
+        for m in (1, 0)
+        for r in order
+    }
+    x = {r: remote(held.at[1, spot[r]], x_in.at[r], x_sent, x_here, r, x_peer) for r in order}
+    z = {r: remote(held.at[0, spot[r]], z_in.at[r - 1], z_sent, z_here, r - 1, ahead[r]) for r in order[:-1]}
+    for copy in core.values():
+        copy.start()
+    keep.wait()
+    tall = 16
+    steps = out.shape[0] // tall
+
+    for r in order:
+        core[1, r].wait_recv()
+
+        @pl.loop(0, steps)
+        def _(i):
+            rows = pl.ds(pl.multiple_of(i * tall, tall), tall)
+            held[1, spot[r], rows] = (held[1, spot[r], rows].astype(F32) + core_in[1, r, rows].astype(F32)).astype(BF16)
+
+        x[r].start()
+    for r in order:
+        core[0, r].wait_recv()
+        x[r].wait_recv()
+
+        @pl.loop(0, steps)
+        def _(i):
+            rows = pl.ds(pl.multiple_of(i * tall, tall), tall)
+            total = held[0, spot[r], rows].astype(F32) + core_in[0, r, rows].astype(F32) + x_in[r, rows].astype(F32)
+            if r == 0:
+                out[rows] = total
+            else:
+                held[0, spot[r], rows] = total.astype(BF16)
+
+        if r:
+            z[r].start()
+    for r in order[:-1]:
+        z[r].wait_recv()
+
+        @pl.loop(0, steps)
+        def _(i):
+            rows = pl.ds(pl.multiple_of(i * tall, tall), tall)
+            out[rows] = out[rows] + z_in[r - 1, rows].astype(F32)
+
+    for copy in list(core.values()) + list(x.values()) + list(z.values()):
+        copy.wait_send()
+
+
+def scatter_rows(parts, collective):
     size = lax.axis_size("ctx")
-    half = values.shape[0] // 2
-    values = values[:half].astype(F32) + swap(lower(values[half:]), "tp", 1).astype(F32)
-    found = bits("tp")[1:]
-    parts = 1 << len(found)
-    blocks = values.reshape((parts, size, -1) + values.shape[1:])
-    blocks = [[blocks[a, r] for r in range(size)] for a in range(parts)]
-    for bit in found:
-        near, far = blocks[: len(blocks) // 2], blocks[len(blocks) // 2 :]
-        blocks = [
-            [n + swap(lower(f), "tp", bit).astype(F32) for n, f in zip(one, other)]
-            for one, other in zip(near, far)
+    rows, width = parts.shape[2:]
+    return pl.pallas_call(
+        functools.partial(scatter_kernel, size),
+        out_shape=jax.ShapeDtypeStruct((rows, width), F32),
+        in_specs=[pl.BlockSpec(memory_space=pl.ANY)],
+        out_specs=pl.BlockSpec(memory_space=pltpu.VMEM),
+        scratch_shapes=[
+            pltpu.VMEM((2, size, rows, width), BF16),
+            pltpu.VMEM((2, size, rows, width), BF16),
+            pltpu.VMEM((size, rows, width), BF16),
+            pltpu.VMEM((size - 1, rows, width), BF16),
+            pltpu.SemaphoreType.DMA(()),
         ]
-    total = blocks[0][0]
-    for r in range(1, size):
-        total = total + receive(lower(blocks[0][r]), "ctx", size - r).astype(F32)
-    return total
+        + [pltpu.SemaphoreType.DMA((n,)) for n in (size - 1, size - 1, size, size, 2 * size, 2 * size)],
+        compiler_params=pltpu.CompilerParams(
+            collective_id=collective, has_side_effects=True, vmem_limit_bytes=32 * 1024 * 1024
+        ),
+        name="scatter_rows",
+    )(parts)
 
 
 def sum_tokens(values):
@@ -108,12 +259,20 @@
     return total
 
 
-def product_shard(lefts, right):
+def product_parts(pairs):
+    own = jnp.concatenate([dot(lefts[0], right, (0, 0)) for lefts, right in pairs], axis=1)
+    others = tuple(
+        jnp.concatenate([dot(lefts[r], right, (0, 0), BF16) for lefts, right in pairs], axis=1)
+        for r in range(1, lax.axis_size("shard"))
+    )
+    return own, others
+
+
+def product_sum(own, others):
     size = lax.axis_size("shard")
-    total = dot(lefts[0], right, (0, 0))
     for r in range(1, size):
-        total = total + receive(dot(lefts[r], right, (0, 0), BF16), "shard", size - r).astype(F32)
-    return total
+        own = own + receive(others[r - 1], "shard", size - r).astype(F32)
+    return own
 
 
 def ahead_first(values, start, axis=0):
@@ -126,8 +285,17 @@
     return lax.all_gather(values, axis_name, axis=axis, tiled=True)
 
 
-def row_order(values):
-    values = ahead_first(values, lax.axis_index("ctx"))
+def gather_small(values, axis):
+    size = lax.axis_size("shard")
+    whole = jnp.concatenate([values] + [receive(values, "shard", r) for r in range(1, size)], axis=axis)
+    return ahead_first(whole, lax.rem(size - lax.axis_index("shard"), size) * values.shape[axis], axis)
+
+
+def after(values, *earlier):
+    return lax.optimization_barrier((values,) + earlier)[0]
+
+
+def part_order(values):
     t = lax.axis_index("tp")
     return jnp.concatenate([lax.dynamic_index_in_dim(values, t ^ m, 1, False)[None] for m in masks("tp")], axis=0)
 
@@ -182,41 +350,48 @@
     block = width // shards
     every = rows * ctxs
     experts = router_weight.shape[1]
-    group = experts // ctxs
     hidden_size = expert_out.shape[2]
     local_width = attention_out.shape[1]
     head_size = local_width // ctxs
     heads = head_size // HEAD_DIM
 
-    gains = gather_natural(jnp.stack([first_gain, second_gain]), "shard", 1).astype(F32)
+    group = experts // ctxs
+    base = c * group
+
+    gains = gather_small(jnp.stack([first_gain, second_gain]), 1).astype(F32)
     gain_one, gain_two = gains[0], gains[1]
-    head_gains = gather_natural(head_gain, "shard").astype(F32)
+    head_gains = gather_small(head_gain[None], 1)[0].astype(F32)
     head_in = lax.dynamic_slice_in_dim(attention_in, c * head_size, head_size, axis=2)
-    head_in = gather_natural(head_in.reshape(block, 3 * head_size), "shard")
+    head_in = head_in.reshape(block, 3 * head_size)
+    first = t * own
+    tokens_own = after(lax.dynamic_slice_in_dim(tokens[0], first, own), head_in)
+    head_in = gather_natural(head_in, "shard")
+    tokens_all = gather_rows(tokens_own).reshape(every, width)
+    attention_out, expert_in, expert_out, cotangent, routes = lax.optimization_barrier(
+        (attention_out, expert_in, expert_out, cotangent, routes, tokens_all)
+    )[:-1]
     exit_weight = gather_natural(ahead_first(attention_out, c * head_size, 1), "shard")
-    router = gather_natural(router_weight, "shard")
-    choices_all = gather_natural(routes[0], "ctx").reshape(ctxs, tps, own, -1)
-    group_out = lax.dynamic_slice_in_dim(expert_out, c * group, group, axis=1)
+    group_out = lax.dynamic_slice_in_dim(expert_out, base, group, axis=1)
     group_out = gather_natural(group_out.reshape(block, group * hidden_size), "shard")
-    group_in = lax.dynamic_slice_in_dim(expert_in, c * group, group, axis=1)
+    group_in = lax.dynamic_slice_in_dim(expert_in, base, group, axis=1)
     in_weights = [
         gather_natural(group_in[:, i].reshape(block, 2 * hidden_size), "shard") for i in range(group)
     ]
 
-    first = t * own
-    layer_in = lax.dynamic_slice_in_dim(tokens[0], first, own).astype(F32)
+    layer_in = tokens_own.astype(F32)
     cot_own = lax.dynamic_slice_in_dim(cotangent[0], first, own)
     upstream = cot_own.astype(F32)
-    picks_all = jnp.any(row_order(choices_all)[..., None] == jnp.arange(experts), axis=3)
-    picks = picks_all[0, 0]
+    cot_all = spread_tp(gather_ctx(cot_own))
+    choices_all = gather_ctx(routes[0]).reshape(ctxs, tps, own, -1)
+    picks_all = jnp.any(part_order(choices_all)[..., None] == jnp.arange(experts), axis=3)
+    picks = lax.dynamic_index_in_dim(picks_all[0], c, 0, False)
     picks_all = picks_all.reshape(every, experts)
-
-    normed_one = lower(layer_in * inverse_scale(layer_in) * gain_one)
-    normed_one_all = gather_rows(normed_one)
-    cot_own, _ = lax.optimization_barrier((cot_own, normed_one_all))
-    cot_all = gather_rows(cot_own)
-    spot = row_order(jnp.arange(every, dtype=jnp.int32).reshape(ctxs, tps, own)).reshape(-1)
-    documents = row_order(segments[0].reshape(ctxs, tps, own)).reshape(-1)
+    router = gather_small(router_weight, 0)
+
+    tokens_wide = tokens_all.astype(F32)
+    normed_one_all = lower(tokens_wide * inverse_scale(tokens_wide) * gain_one)
+    spot = part_order(jnp.arange(every, dtype=jnp.int32).reshape(ctxs, tps, own)).reshape(-1)
+    documents = part_order(segments[0].reshape(ctxs, tps, own)).reshape(-1)
     steps = jnp.arange(HEAD_DIM // 2).astype(F32)
     frequency = ROTARY_BASE ** (-2.0 * steps / HEAD_DIM)
     angles = spot.astype(F32)[:, None] * frequency[None, :]
@@ -233,21 +408,20 @@
     chances = jax.nn.softmax(jnp.where(same[None], scores, MASKED), axis=-1)
     chances_low = lower(chances)
     mixed_head = lower(jnp.einsum("hqk,khd->qhd", chances_low, values, preferred_element_type=F32))
-    blocks = mixed_head.reshape(tps, ctxs, own, head_size)
+    blocks = ahead_first(mixed_head.reshape(tps, ctxs, own, head_size), c, 1)
     mixed = [blocks[:, 0]] + [receive(blocks[:, ctxs - j], "ctx", j) for j in range(1, ctxs)]
     mixed = jnp.concatenate([m.reshape(rows, head_size) for m in mixed], axis=1)
     residual = layer_in + scatter_tp(dot(mixed, exit_weight, (1, 1)))
 
     normed_two = lower(residual * inverse_scale(residual) * gain_two)
-    normed_two_all = gather_rows(normed_two)
+    normed_two_all = gather_rows(normed_two).reshape(every, width)
     chances_all = jax.nn.softmax(dot(normed_two_all, router, (1, 0)), axis=-1)
     gates = jnp.where(picks_all, chances_all, 0.0)
-    gates = lax.dynamic_slice_in_dim(gates, c * group, group, axis=1)
-    out_weights = [group_out[:, i * hidden_size : (i + 1) * hidden_size] for i in range(group)]
+    gates = lax.dynamic_slice_in_dim(gates, base, group, axis=1)
     normed_blocks = [own_block(normed_two_all, r, 1) for r in range(shards)]
     cot_blocks = [own_block(cot_all, r, 1) for r in range(shards)]
     backs = dot(cot_all, group_out, (1, 0))
-    scaled, gate_parts, inner_grads, chunks = [], [], [], []
+    scaled, gate_parts, inner_grads, products = [], [], [], []
     rows_now = normed_two_all
     for i in range(group):
         gate_up = dot(rows_now, in_weights[i], (1, 0))
@@ -267,23 +441,19 @@
                 )
             )
         )
-        upward = product_shard(normed_blocks, inner_grads[i])
-        downward = product_shard(cot_blocks, scaled[i])
-        chunks.append(
-            lax.all_gather(lower(jnp.concatenate([upward, downward], axis=1)), "ctx", axis=0, tiled=False)
-        )
-        rows_now, _ = lax.optimization_barrier((normed_two_all, scaled[i]))
+        products.append(product_parts([(normed_blocks, inner_grads[i]), (cot_blocks, scaled[i])]))
+        rows_now = after(rows_now, *products[i])
 
     normed_part = sum(dot(inner_grads[i], in_weights[i], (1, 1)) for i in range(group))
     gate_part = lax.dynamic_update_slice(
-        jnp.zeros((every, 128), F32), jnp.stack(gate_parts, axis=1), (0, c * group)
-    )
-    normed_sum = scatter_rows(jnp.concatenate([normed_part, gate_part], axis=1))
+        jnp.zeros((every, 128), F32), jnp.stack(gate_parts, axis=1), (0, base)
+    )
+    normed_part = lower(jnp.concatenate([normed_part, gate_part], axis=1))
+    normed_sum = scatter_rows(normed_part.reshape(tps, ctxs, own, -1), 1)
     normed_sum, gate_grad = normed_sum[:, :width], normed_sum[:, width : width + experts]
-    result_part = dot(jnp.concatenate(scaled, axis=1), group_out, (1, 1))
-    result_part, _ = lax.optimization_barrier((result_part, normed_sum))
-    result_sum = scatter_rows(result_part)
-    layer_output = natural_rows(gather_tp(lower(residual + result_sum)))[None]
+    chunks = [
+        lax.all_gather(lower(product_sum(*products[i])), "ctx", axis=0, tiled=False) for i in range(group)
+    ]
 
     router_chances = jax.nn.softmax(dot(normed_two, router, (1, 0)), axis=-1)
     chance_grad = jnp.where(picks, gate_grad, 0.0)
@@ -296,7 +466,7 @@
     residual_grad = upstream + residual_back
 
     attend_grad = gather_tp(lower(residual_grad))
-    exit_part = product_shard([own_block(attend_grad, r, 1) for r in range(shards)], mixed)
+    exit_part = product_sum(*product_parts([([own_block(attend_grad, r, 1) for r in range(shards)], mixed)]))
     exit_head = exit_part[:, :head_size]
     for r in range(1, ctxs):
         exit_head = exit_head + receive(
@@ -304,7 +474,8 @@
         ).astype(F32)
     mixed_grad = lower(dot(attend_grad, exit_weight, (1, 0))).reshape(tps, own, ctxs, head_size)
     parts = [mixed_grad[:, :, 0]] + [receive(mixed_grad[:, :, ctxs - j], "ctx", j) for j in range(1, ctxs)]
-    mixed_grad = jnp.stack(parts, axis=1).reshape(every, heads, HEAD_DIM)
+    mixed_grad = ahead_first(jnp.stack(parts, axis=1), lax.rem(ctxs - c, ctxs), 1)
+    mixed_grad = mixed_grad.reshape(every, heads, HEAD_DIM)
     weight_grad = jnp.einsum("qhd,khd->hqk", mixed_grad, values, preferred_element_type=F32)
     score_grad = lower(chances * (weight_grad - jnp.sum(chances * weight_grad, axis=-1, keepdims=True)))
     query_grad = jnp.einsum("hqk,khd->qhd", score_grad, keys, preferred_element_type=F32) * scale
@@ -315,41 +486,52 @@
     projected_grad = lower(
         jnp.stack([query_raw_grad, key_raw_grad, value_grad], axis=1).reshape(every, 3 * head_size)
     )
-    entry_head = product_shard([own_block(normed_one_all, r, 1) for r in range(shards)], projected_grad)
+    entry_blocks = [own_block(normed_one_all, r, 1) for r in range(shards)]
+    entry_head = product_sum(*product_parts([(entry_blocks, projected_grad)]))
     attention_chunk = lax.all_gather(
         lower(jnp.concatenate([entry_head, exit_head], axis=1)), "ctx", axis=0, tiled=False
     )
-    first_normed_grad = scatter_rows(dot(projected_grad, head_in, (1, 1)))
+    first_part = dot(projected_grad, head_in, (1, 1), BF16)
+    first_normed_grad = scatter_rows(first_part.reshape(tps, ctxs, own, width), 2)
+
+    result_part = dot(after(jnp.concatenate(scaled, axis=1), mixed_grad), group_out, (1, 1), BF16)
+    result_sum = scatter_rows(result_part.reshape(tps, ctxs, own, width), 2)
+    layer_output = natural_rows(gather_tp(lower(residual + result_sum)))[None]
+
     input_back, first_part = norm_back(first_normed_grad, layer_in, gain_one)
     input_gradient = natural_rows(gather_tp(lower(residual_grad + input_back))).astype(F32)[None]
 
-    early = jnp.concatenate([jnp.sum(second_part, axis=0)[None], router_part], axis=0)
-    early = sum_shard(sum_tokens(early), 1)
     head_part = jnp.concatenate([jnp.sum(gain_q_part, axis=(0, 1)), jnp.sum(gain_k_part, axis=(0, 1))])
-    late = sum_tokens(jnp.concatenate([jnp.sum(first_part, axis=0), head_part])[None])
-    first_gradient = sum_shard(late[:, :width], 1)[0]
-    head_gradient = sum_shard(late[:, width:], 1)[0]
+    small_part = jnp.concatenate(
+        [jnp.sum(second_part, axis=0)[None], jnp.sum(first_part, axis=0)[None], router_part], axis=0
+    )
+    small_part = jnp.concatenate([small_part, jnp.pad(head_part, (0, width - head_part.shape[0]))[None]], axis=0)
+    small_sum = sum_tokens(small_part)
+    head_gradient = sum_shard(small_sum[-1:, : head_part.shape[0]], 1)[0]
+    small_sum = sum_shard(small_sum[:-1], 1)
 
     wide = jnp.moveaxis(attention_chunk, 0, 1).astype(F32)
     entry_gradient = jnp.moveaxis(
         wide[:, :, : 3 * head_size].reshape(block, ctxs, 3, head_size), 1, 2
     ).reshape(block, 3, local_width)
     exit_gradient = wide[:, :, 3 * head_size :].reshape(block, local_width)
-    upward_gradient = jnp.stack([chunk[:, :, : 2 * hidden_size] for chunk in chunks], axis=1)
-    upward_gradient = jnp.moveaxis(upward_gradient, 2, 0).astype(F32)
-    upward_gradient = upward_gradient.reshape(block, experts, 2, hidden_size)
-    downward_gradient = jnp.stack([chunk[:, :, 2 * hidden_size :] for chunk in chunks], axis=1)
-    downward_gradient = jnp.moveaxis(downward_gradient, 2, 0).astype(F32)
-    downward_gradient = downward_gradient.reshape(block, experts, hidden_size)
+    upward_gradient = jnp.zeros((block, experts, 2, hidden_size), F32)
+    downward_gradient = jnp.zeros((block, experts, hidden_size), F32)
+    for i in range(group):
+        for j in range(ctxs):
+            up = chunks[i][j][:, : 2 * hidden_size].astype(F32).reshape(block, 1, 2, hidden_size)
+            down = chunks[i][j][:, 2 * hidden_size :].astype(F32)[:, None]
+            upward_gradient = lax.dynamic_update_slice(upward_gradient, up, (0, j * group + i, 0, 0))
+            downward_gradient = lax.dynamic_update_slice(downward_gradient, down, (0, j * group + i, 0))
     return (
         layer_output,
         input_gradient,
-        first_gradient,
+        small_sum[1],
         head_gradient,
         entry_gradient,
         exit_gradient,
-        early[0],
-        early[1:].T,
+        small_sum[0],
+        small_sum[2:].T,
         upward_gradient,
         downward_gradient,
     )

time: 1200 us -> 1320 us (1.10)
  Pallas kernels: 0 us -> 306 us
  waiting for transfers between devices: 525 us -> 407 us
  other arithmetic: 96.5 us -> 141 us
  local copies, waits for them, and re-layouts: 248 us -> 208 us
  starting transfers between devices: 83.9 us -> 46.9 us
  blocking collectives: 27.7 us -> 0 us
    pallas_call x0 -> x5, Pallas kernels: none -> 306 us  [the longest x3 192 us: scatter_rows(): pl.pallas_call(functools.partial(scatter_kernel, size), out_shape=jax.Sha...]
    ppermute x40 -> x26, waiting for transfers between devices: 347 us -> 139 us  [receive(): lax.ppermute(values, axis, [((i + distance) % size, i) for i in range(siz...]
    all_gather x4, waiting for transfers between devices: 0.01 us -> 157 us  [local(): lax.all_gather(lower(product_sum(*products[i])), 'ctx', axis=0, tiled=False)]
    unnamed x314 -> x320, local copies, waits for them, and re-layouts: 163 us -> 58.6 us
    ppermute x46 -> x15, waiting for transfers between devices: 178 us -> 110 us  [swap(): return lax.ppermute(values, axis, [(i, i ^ bit) for i in range(size)])]
    dynamic_update_slice x0 -> x17, other arithmetic: none -> 56.6 us  [the longest x16 40.1 us: local(): lax.dynamic_update_slice(downward_gradient, down, (0, j * group + i, 0))]
    reshape x1 -> x17, local copies, waits for them, and re-layouts: 0.73 us -> 53.9 us  [the longest x16 53.8 us: local(): chunks[i][j][:, :2 * hidden_size].astype(F32)]
    dynamic_update_slice x0 -> x15, local copies, waits for them, and re-layouts: none -> 32.2 us  [local(): lax.dynamic_update_slice(upward_gradient, up, (0, j * group + i, 0, 0))]
  transfers between devices with their start and end apart: 98 -> 53, of which waited for: 47 -> 22; matrix products, arithmetic and copies ran while one was open for 39% -> 25% of each run, Pallas kernels for 0% -> 15%
where the time goes in v2:
time: 1320 us; the launch traced here: 1310 us
  waiting for transfers between devices  407 us (31%)
  Pallas kernels  306 us (23%)
  local copies, waits for them, and re-layouts  208 us (16%)
  matrix products  182 us (14%)
  other arithmetic  141 us (11%)
  starting transfers between devices  46.9 us (4%)
  between operations  17.1 us (1%)
    pallas_call x3, Pallas kernels, scatter_rows(): pl.pallas_call(functools.partial(scatter_kernel, size), out_shape=jax.Sha...  192 us
    dot_general x38, matrix products, dot(): lax.dot_general(left, right, (((over[0],), (over[1],)), ((), ())), prefer...  168 us
    all_gather x4, waiting for transfers between devices, local(): lax.all_gather(lower(product_sum(*products[i])), 'ctx', axis=0, tiled=False)  157 us
    ppermute x26, waiting for transfers between devices, receive(): lax.ppermute(values, axis, [((i + distance) % size, i) for i in range(siz...  139 us
    pallas_call x2, Pallas kernels, gather_rows(): pl.pallas_call(functools.partial(gather_kernel, size, pieces), out_shape=...  114 us
    ppermute x15, waiting for transfers between devices, swap(): return lax.ppermute(values, axis, [(i, i ^ bit) for i in range(size)])  110 us
    unnamed x320, local copies, waits for them, and re-layouts  58.6 us
    reshape x16, local copies, waits for them, and re-layouts, local(): chunks[i][j][:, :2 * hidden_size].astype(F32)  53.8 us
  transfers between devices with their start and end apart: 53, of which 22 were waited for; matrix products, arithmetic and copies ran while one was open for 25% of the time, Pallas kernels for 15%

profile of v2, /device:TPU:0, one launch (start us, length us, event | category | flops | bytes accessed | tf_op | source)
XLA Modules:
  0.0 1308.0 jit_solution(16896601012440176578)
XLA Ops:
  20.9 12.2 copy.252
  52.5 69.2 %gather_rows.2 = bf16[4,4,96,2048]{3,2,1,0:T(8,128)(2,1)} custom-call(bf16[96,2048]{1,0:T(8,128)(2,1)} %dynamic-slice_bitcast_fusion.5.own), custom_call_target="tpu_custom_call" | custom-call | tf_op jit(solution)/shard_map/gather_rows/pallas_call | solution.py:147
  194.0 31.9 %collective-permute-done.14 = bf16[384,2048]{1,0:T(8,128)(2,1)} collective-permute-done((bf16[384,2048]{1,0:T(8,128)(2,1)}, bf16[384,2048]{1,0:T(8,128)(2,1)}, u32[]{:S(2)}, u32[]{:S(2)}) %collective-permute-start.14) | collective-permute-done | bytes 1572896 | tf_op jit(solution)/shard_map/ppermute | solution.py:34
  237.3 45.1 %gather_rows.3 = bf16[4,4,96,2048]{3,2,1,0:T(8,128)(2,1)} custom-call(bf16[96,2048]{1,0:T(8,128)(2,1)} %multiply_convert_fusion.14.own), custom_call_target="tpu_custom_call" | custom-call | tf_op jit(solution)/shard_map/gather_rows/pallas_call | solution.py:147
  288.4 8.6 fusion.241
  302.7 10.2 fusion.242
  375.9 10.5 fusion.143
  399.5 17.5 %add_convert_fusion = bf16[1536,2048]{1,0:T(8,128)(2,1)} fusion(f32[1536,2048]{1,0:T(8,128)} %fusion.143, f32[1536,2048]{1,0:T(8,128)} %fusion.145, f32[1536,2048]{1,0:T(8,128)} %fusion.144, bf16[2048,512]{1,0:T(8,128)(2,1)} %all-gather.29.cloned.1.call-done, bf16[1536,256]{0,1:T(8,128)(2,1)} %get-tuple-element.138, bf16[1536,256]{0,1:T(8,128)(2,1)S(1)} %copy-done.44), kind=kOutput, calls=%fused_computation.7 | convolution fusion | flops 3236954112 | bytes 47710208 | tf_op jit(solution)/shard_map/dot_general | solution.py:23
  420.5 55.2 %scatter_rows.4 = f32[96,2176]{1,0:T(8,128)S(1)} custom-call(bf16[4,4,96,2176]{3,2,1,0:T(8,128)(2,1)S(1)} %pad_maximum_fusion.parts), custom_call_target="tpu_custom_call" | custom-call | tf_op jit(solution)/shard_map/scatter_rows/pallas_call | solution.py:220
  487.6 51.0 %scatter_rows.3 = f32[96,2048]{1,0:T(8,128)S(1)} custom-call(bf16[4,4,96,2048]{3,2,1,0:T(8,128)(2,1)S(1)} %bitcast.368), custom_call_target="tpu_custom_call" | custom-call | tf_op jit(solution)/shard_map/scatter_rows/pallas_call | solution.py:220
  541.5 9.6 collective-permute-done.19
  602.5 12.2 collective-permute-done.32
  632.3 27.9 %collective-permute-done.37 = bf16[1024,768]{0,1:T(8,128)(2,1)S(1)} collective-permute-done((bf16[1024,768]{0,1:T(8,128)(2,1)}, bf16[1024,768]{0,1:T(8,128)(2,1)S(1)}, u32[]{:S(2)}, u32[]{:S(2)}) %collective-permute-start.37) | collective-permute-done | bytes 1572896 | tf_op jit(solution)/shard_map/ppermute | solution.py:29
  669.6 27.0 %collective-permute-done.38 = bf16[1024,768]{0,1:T(8,128)(2,1)S(1)} collective-permute-done((bf16[1024,768]{0,1:T(8,128)(2,1)}, bf16[1024,768]{0,1:T(8,128)(2,1)S(1)}, u32[]{:S(2)}, u32[]{:S(2)}) %collective-permute-start.38) | collective-permute-done | bytes 1572896 | tf_op jit(solution)/shard_map/ppermute | solution.py:29
  705.9 26.3 %collective-permute-done.39 = bf16[1024,768]{0,1:T(8,128)(2,1)S(1)} collective-permute-done((bf16[1024,768]{0,1:T(8,128)(2,1)}, bf16[1024,768]{0,1:T(8,128)(2,1)S(1)}, u32[]{:S(2)}, u32[]{:S(2)}) %collective-permute-start.39) | collective-permute-done | bytes 1572896 | tf_op jit(solution)/shard_map/ppermute | solution.py:29
  750.2 24.3 %collective-permute-done.40 = bf16[1024,768]{0,1:T(8,128)(2,1)S(1)} collective-permute-done((bf16[1024,768]{0,1:T(8,128)(2,1)S(1)}, bf16[1024,768]{0,1:T(8,128)(2,1)S(1)}, u32[]{:S(2)}, u32[]{:S(2)}) %collective-permute-start.40) | collective-permute-done | bytes 1572896 | tf_op jit(solution)/shard_map/ppermute | solution.py:29
  783.6 85.7 %scatter_rows.5 = f32[96,2048]{1,0:T(8,128)S(1)} custom-call(bf16[4,4,96,2048]{3,2,1,0:T(8,128)(2,1)S(1)} %bitcast.369), custom_call_target="tpu_custom_call" | custom-call | tf_op jit(solution)/shard_map/scatter_rows/pallas_call | solution.py:220
  873.5 12.7 collective-permute-done.27
  887.6 18.8 %collective-permute-done.28 = f32[19,2048]{1,0:T(8,128)S(1)} collective-permute-done((f32[19,2048]{1,0:T(8,128)S(1)}, f32[19,2048]{1,0:T(8,128)S(1)}, u32[]{:S(2)}, u32[]{:S(2)}) %collective-permute-start.28) | collective-permute-done | bytes 155680 | tf_op jit(solution)/shard_map/ppermute | solution.py:34
  906.9 24.3 %collective-permute-done.29 = f32[19,2048]{1,0:T(8,128)S(1)} collective-permute-done((f32[19,2048]{1,0:T(8,128)S(1)}, f32[19,2048]{1,0:T(8,128)S(1)}, u32[]{:S(2)}, u32[]{:S(2)}) %collective-permute-start.29) | collective-permute-done | bytes 155680 | tf_op jit(solution)/shard_map/ppermute | solution.py:34
  999.0 78.3 %all-gather.37.cloned.1.call-done = bf16[4096,768]{0,1:T(8,128)(2,1)} async-done(((bf16[1024,768]{0,1:T(8,128)(2,1)}), bf16[4096,768]{0,1:T(8,128)(2,1)}) %all-gather.37.cloned.1.call-update) | async-done | bytes 6291472 | tf_op jit(solution)/shard_map/all_gather | solution.py:455
  1096.9 16.5 %pad_convert_fusion = f32[1024,16,2,256]{3,2,1,0:T(2,128)} fusion(bf16[1024,1,2,256]{3,2,1,0:T(2,128)(2,1)S(1)} %copy.268), kind=kLoop, calls=%fused_computation | loop fusion | flops 8388608 | bytes 34603008 | tf_op jit(solution)/shard_map/dynamic_update_slice | solution.py:524
  1113.4 78.8 %all-gather.39.cloned.1.call-done = bf16[4096,768]{0,1:T(8,128)(2,1)} async-done(((bf16[1024,768]{0,1:T(8,128)(2,1)}), bf16[4096,768]{0,1:T(8,128)(2,1)}) %all-gather.39.cloned.1.call-update) | async-done | bytes 6291472 | tf_op jit(solution)/shard_map/all_gather | solution.py:455
  1251.1 17.6 %copy.286 = f32[1024,16,256]{2,1,0:T(8,128)} copy(f32[1024,16,256]{0,2,1:T(8,128)} %convert_dynamic-update-slice_fusion) | data formatting | bytes 33554432
  (658 shorter events, 519.6 us)
Async XLA Ops:
  7.2 149.9 %all-gather.17.cloned.1.call-start = ((), (), s32[]{:S(2)}) async-start(), calls=%async_computation | async-start | bytes 2359296 | tf_op jit(solution)/shard_map/all_gather | solution.py:285
  12.4 170.9 %all-gather.19.cloned.1.call-start = ((), (), s32[]{:S(2)}) async-start(), calls=%async_computation.1 | async-start | bytes 3145728 | tf_op jit(solution)/shard_map/all_gather | solution.py:285
  15.1 273.3 %all-gather.21.cloned.1.call-start = ((), (), s32[]{:S(2)}) async-start(), calls=%async_computation.2 | async-start | bytes 3145728 | tf_op jit(solution)/shard_map/all_gather | solution.py:285
  20.9 281.8 %all-gather.23.cloned.1.call-start = ((), (), s32[]{:S(2)}) async-start(), calls=%async_computation.3 | async-start | bytes 6291456 | tf_op jit(solution)/shard_map/all_gather | solution.py:285
  36.3 288.9 %all-gather.25.cloned.1.call-start = ((), (), s32[]{:S(2)}) async-start(), calls=%async_computation.4 | async-start | bytes 3145728 | tf_op jit(solution)/shard_map/all_gather | solution.py:285
  37.5 306.1 %all-gather.27.cloned.1.call-start = ((), (), s32[]{:S(2)}) async-start(), calls=%async_computation.5 | async-start | bytes 3145728 | tf_op jit(solution)/shard_map/all_gather | solution.py:285
  38.8 323.7 %all-gather.29.cloned.1.call-start = ((), (), s32[]{:S(2)}) async-start(), calls=%async_computation.6 | async-start | bytes 3145728 | tf_op jit(solution)/shard_map/all_gather | solution.py:285
  40.7 111.7 %collective-permute-start.11 = (bf16[96,2048]{1,0:T(8,128)(2,1)S(1)}, bf16[96,2048]{1,0:T(8,128)(2,1)S(1)}, u32[]{:S(2)}, u32[]{:S(2)}) collective-permute-start(bf16[96,2048]{1,0:T(8,128)(2,1)S(1)} %get-tuple-element.126), channel_id=1, source_target_pairs={{4,0},{8,4},{12,8},{0,12},{5,1},{9,5},{13,9},{1,13},{6,2},{10,6},{... | collective-permute-start | bytes 1179656 | tf_op jit(solution)/shard_map/ppermute | solution.py:29
  45.7 107.5 %collective-permute-start.12 = (bf16[96,2048]{1,0:T(8,128)(2,1)S(1)}, bf16[96,2048]{1,0:T(8,128)(2,1)S(1)}, u32[]{:S(2)}, u32[]{:S(2)}) collective-permute-start(bf16[96,2048]{1,0:T(8,128)(2,1)S(1)} %get-tuple-element.126), channel_id=1, source_target_pairs={{8,0},{12,4},{0,8},{4,12},{9,1},{13,5},{1,9},{5,13},{10,2},{14,6},... | collective-permute-start | bytes 1179656 | tf_op jit(solution)/shard_map/ppermute | solution.py:29
  45.7 108.3 %collective-permute-start.13 = (bf16[96,2048]{1,0:T(8,128)(2,1)S(1)}, bf16[96,2048]{1,0:T(8,128)(2,1)S(1)}, u32[]{:S(2)}, u32[]{:S(2)}) collective-permute-start(bf16[96,2048]{1,0:T(8,128)(2,1)S(1)} %get-tuple-element.126), channel_id=1, source_target_pairs={{12,0},{0,4},{4,8},{8,12},{13,1},{1,5},{5,9},{9,13},{14,2},{2,6},{... | collective-permute-start | bytes 1179656 | tf_op jit(solution)/shard_map/ppermute | solution.py:29
  46.8 85.5 %collective-permute-start = (bf16[2,1024]{1,0:T(2,128)(2,1)S(1)}, bf16[2,1024]{1,0:T(2,128)(2,1)S(1)}, u32[]{:S(2)}, u32[]{:S(2)}) collective-permute-start(bf16[2,1024]{1,0:T(2,128)(2,1)S(1)} %pad_maximum_fusion.45), channel_id=1, source_target_pairs={{16,0},{0,16},{17,1},{1,17},{18,2},{2,18},{19,3},{3,19},{20,4},{4,... | collective-permute-start | bytes 12296 | tf_op jit(solution)/shard_map/ppermute | solution.py:29
  48.4 79.8 %collective-permute-start.1 = (bf16[1,128]{1,0:T(2,128)(2,1)S(1)}, bf16[1,128]{1,0:T(2,128)(2,1)S(1)}, u32[]{:S(2)}, u32[]{:S(2)}) collective-permute-start(bf16[1,128]{1,0:T(2,128)(2,1)S(1)} %bitcast.476), channel_id=1, source_target_pairs={{16,0},{0,16},{17,1},{1,17},{18,2},{2,18},{19,3},{3,19},{20,4},{4,... | collective-permute-start | bytes 776 | tf_op jit(solution)/shard_map/ppermute | solution.py:29
  50.1 891.1 %all-gather.31.cloned.1.call-start = ((), (), s32[]{:S(2)}) async-start(), calls=%async_computation.7 | async-start | bytes 5242880 | tf_op jit(solution)/shard_map/all_gather | solution.py:491
  146.2 46.9 %collective-permute-start.10 = (bf16[1024,16]{0,1:T(8,128)(2,1)}, bf16[1024,16]{0,1:T(8,128)(2,1)}, u32[]{:S(2)}, u32[]{:S(2)}) collective-permute-start(bf16[1024,16]{0,1:T(8,128)(2,1)} %param.21), channel_id=1, source_target_pairs={{16,0},{0,16},{17,1},{1,17},{18,2},{2,18},{19,3},{3,19},{20,4},{4,... | collective-permute-start | bytes 98312 | tf_op jit(solution)/shard_map/ppermute | solution.py:29
  188.4 37.5 %collective-permute-start.14 = (bf16[384,2048]{1,0:T(8,128)(2,1)}, bf16[384,2048]{1,0:T(8,128)(2,1)}, u32[]{:S(2)}, u32[]{:S(2)}) collective-permute-start(bf16[384,2048]{1,0:T(8,128)(2,1)} %constant_dynamic-slice_fusion.21), channel_id=1, source_target_pairs={{0,2},{1,3},{2,0},{3,1},{4,6},{5,7},{6,4},{7,5},{8,10},{9,11},{10,... | collective-permute-start | bytes 4718600 | tf_op jit(solution)/shard_map/ppermute | solution.py:34
  190.8 43.0 %collective-permute-start.6 = (bf16[96,2048]{1,0:T(8,128)(2,1)S(1)}, bf16[96,2048]{1,0:T(8,128)(2,1)S(1)}, u32[]{:S(2)}, u32[]{:S(2)}) collective-permute-start(bf16[96,2048]{1,0:T(8,128)(2,1)S(1)} %slice.782), channel_id=1, source_target_pairs={{0,2},{1,3},{2,0},{3,1},{4,6},{5,7},{6,4},{7,5},{8,10},{9,11},{10,... | collective-permute-start | bytes 1179656 | tf_op jit(solution)/shard_map/ppermute | solution.py:34
  193.9 103.0 %collective-permute-start.15 = (bf16[384,2048]{1,0:T(8,128)(2,1)}, bf16[384,2048]{1,0:T(8,128)(2,1)S(1)}, u32[]{:S(2)}, u32[]{:S(2)}) collective-permute-start(bf16[384,2048]{1,0:T(8,128)(2,1)} %constant_dynamic-slice_fusion.21), channel_id=1, source_target_pairs={{0,1},{1,0},{2,3},{3,2},{4,5},{5,4},{6,7},{7,6},{8,9},{9,8},{10,11... | collective-permute-start | bytes 4718600 | tf_op jit(solution)/shard_map/ppermute | solution.py:34
  225.9 71.0 %collective-permute-start.16 = (bf16[384,2048]{1,0:T(8,128)(2,1)}, bf16[384,2048]{1,0:T(8,128)(2,1)}, u32[]{:S(2)}, u32[]{:S(2)}) collective-permute-start(bf16[384,2048]{1,0:T(8,128)(2,1)} %collective-permute-done.14), channel_id=1, source_target_pairs={{0,1},{1,0},{2,3},{3,2},{4,5},{5,4},{6,7},{7,6},{8,9},{9,8},{10,11... | collective-permute-start | bytes 4718600 | tf_op jit(solution)/shard_map/ppermute | solution.py:34
  624.7 341.2 %all-gather.33.cloned.1.call-start = ((), (), s32[]{:S(2)}) async-start(), calls=%async_computation.8 | async-start | bytes 7864320 | tf_op jit(solution)/shard_map/all_gather | solution.py:455
  624.8 35.3 %collective-permute-start.37 = (bf16[1024,768]{0,1:T(8,128)(2,1)}, bf16[1024,768]{0,1:T(8,128)(2,1)S(1)}, u32[]{:S(2)}, u32[]{:S(2)}) collective-permute-start(bf16[1024,768]{0,1:T(8,128)(2,1)} %pad_maximum_fusion.7), channel_id=1, source_target_pairs={{16,0},{0,16},{17,1},{1,17},{18,2},{2,18},{19,3},{3,19},{20,4},{4,... | collective-permute-start | bytes 4718600 | tf_op jit(solution)/shard_map/ppermute | solution.py:29
  661.9 317.5 %all-gather.35.cloned.1.call-start = ((), (), s32[]{:S(2)}) async-start(), calls=%async_computation.9 | async-start | bytes 7864320 | tf_op jit(solution)/shard_map/all_gather | solution.py:455
  698.5 378.8 %all-gather.37.cloned.1.call-start = ((), (), s32[]{:S(2)}) async-start(), calls=%async_computation.10 | async-start | bytes 7864320 | tf_op jit(solution)/shard_map/all_gather | solution.py:455
  734.0 458.2 %all-gather.39.cloned.1.call-start = ((), (), s32[]{:S(2)}) async-start(), calls=%async_computation.11 | async-start | bytes 7864320 | tf_op jit(solution)/shard_map/all_gather | solution.py:455
  870.9 35.6 %collective-permute-start.24 = (bf16[96,2048]{1,0:T(8,128)(2,1)S(1)}, bf16[96,2048]{1,0:T(8,128)(2,1)S(1)}, u32[]{:S(2)}, u32[]{:S(2)}) collective-permute-start(bf16[96,2048]{1,0:T(8,128)(2,1)S(1)} %fusion.98), channel_id=1, source_target_pairs={{0,2},{1,3},{2,0},{3,1},{4,6},{5,7},{6,4},{7,5},{8,10},{9,11},{10,... | collective-permute-start | bytes 1179656 | tf_op jit(solution)/shard_map/ppermute | solution.py:34
  (174 other events, 3184.1 us)
Sparse Core Ops, SparseCore 0:
  12.5 29.8 all-gather.16
  44.6 33.1 all-gather.18
  79.3 33.1 all-gather.20
  114.4 57.4 all-gather.22
  173.3 33.1 all-gather.24
  207.9 33.1 all-gather.26
  243.1 33.1 all-gather.28
  624.9 78.0 all-gather.30
  704.6 128.1 all-gather.32
  834.2 127.9 all-gather.34
  963.8 113.4 all-gather.36
  1078.7 113.5 all-gather.38

commit v3 on v2

--- a/solution.py
+++ b/solution.py
@@ -61,24 +61,23 @@
     return values
 
 
-def spread_tp(block):
-    parts = [block]
-    for bit in reversed(bits("tp")[1:]):
-        parts = parts + [swap(part, "tp", bit) for part in parts]
-    return jnp.concatenate(parts + [swap(part, "tp", 1) for part in parts], axis=0)
-
-
 def gather_ctx(values):
     size = lax.axis_size("ctx")
     whole = jnp.concatenate([values] + [receive(values, "ctx", r) for r in range(1, size)], axis=0)
     return ahead_first(whole, lax.rem(size - lax.axis_index("ctx"), size) * values.shape[0])
 
 
-def greet(peers):
+def greet(peers, neighbours):
     barrier = pltpu.get_barrier_semaphore()
     for peer in peers:
         pl.semaphore_signal(barrier, inc=1, device_id=peer, device_id_type=pl.DeviceIdType.MESH)
-    pl.semaphore_wait(barrier, len(peers))
+    for there, peer in neighbours:
+
+        @pl.when(there)
+        def _():
+            pl.semaphore_signal(barrier, inc=1, device_id=peer, device_id_type=pl.DeviceIdType.MESH)
+
+    pl.semaphore_wait(barrier, len(peers) + sum(jnp.where(there, 1, 0) for there, _ in neighbours))
 
 
 def remote(source, target, sent, arrived, place, peer):
@@ -96,152 +95,299 @@
     return sorted(range(1, size), key=lambda r: min(r, size - r))
 
 
-def gather_kernel(size, pieces, own, out, local, z_sent, z_here, x_sent, x_here, core_sent, core_here):
+def gather_kernel(size, pieces, arrays, shared, earlier, *refs):
+    owns, outs = refs[:arrays], refs[arrays + earlier : 2 * arrays + earlier]
+    held = refs[2 * arrays + earlier : 3 * arrays + earlier]
+    local, z_sent, z_here, x_sent, x_here, core_sent, core_here = refs[3 * arrays + earlier :]
     c, t = lax.axis_index("ctx"), lax.axis_index("tp")
     x_peer, core_peer = {"tp": t ^ 2}, {"tp": t ^ 1}
-    behind = {r: {"ctx": lax.rem(c + size - r, size)} for r in range(1, size)}
-    greet([x_peer, core_peer] + [behind[r] for r in range(1, size)])
-    step = own.shape[0] // pieces
-    rows = [pl.ds(h * step, step) for h in range(pieces)]
-    spot = [lax.rem(c + r, size) for r in range(size)]
-    keep = pltpu.make_async_copy(own, out.at[0, c], local)
-    keep.start()
-    order = [(r, h) for r in far_first(size) for h in range(pieces)]
-    mine = [(0, h) for h in range(pieces)]
-    z = {
-        (r, h): remote(own.at[rows[h]], out.at[0, c, rows[h]], z_sent, z_here, (r - 1) * pieces + h, behind[r])
-        for r, h in order
-    }
-    x, core = {}, {}
-    for r, h in mine + order:
-        source = own.at[rows[h]] if r == 0 else out.at[0, spot[r], rows[h]]
-        near, far = [out.at[1 + m, spot[r], rows[h]] for m in range(2)], out.at[3, spot[r], rows[h]]
-        place = r * pieces + h
-        x[r, h] = remote(source, near[0], x_sent, x_here, place, x_peer)
-        core[0, r, h] = remote(source, near[1], core_sent, core_here, place, core_peer)
-        core[1, r, h] = remote(near[0], far, core_sent, core_here, size * pieces + place, core_peer)
-    for key in order:
-        z[key].start()
-    for key in mine:
-        x[key].start()
-        core[(0,) + key].start()
-    for key in order:
-        z[key].wait_recv()
-        x[key].start()
-        core[(0,) + key].start()
-    for key in mine + order:
-        x[key].wait_recv()
-        core[(1,) + key].start()
-    for copy in core.values():
-        copy.wait()
-    for copy in list(x.values()) + list(z.values()):
-        copy.wait_send()
-    keep.wait()
-
-
-def gather_rows(values):
-    size = lax.axis_size("ctx")
-    assert lax.axis_size("tp") == 4
-    pieces = 2
-    count = size * pieces
+    before, behind = {"ctx": lax.max(c - 1, 0)}, {"ctx": lax.min(c + 1, size - 1)}
+    greet([x_peer, core_peer], ((c > 0, before), (c < size - 1, behind)))
+    rows = outs[0].shape[2]
+    step = rows // pieces
+    cuts = [pl.ds(h * step, step) for h in range(pieces)]
+    loads, keeps, z, x, core, places = [], [], {}, {}, {}, {}
+    for n in range(arrays):
+        loads.append(pltpu.make_async_copy(owns[n], held[n], local.at[n * 5 + 4]))
+        for m in range(4 if shared else 1):
+            part = held[n].at[pl.ds(pl.multiple_of((t ^ masks("tp")[m]) * rows, rows), rows)] if shared else held[n]
+            keeps.append(pltpu.make_async_copy(part, outs[n].at[m, c], local.at[n * 5 + m]))
+    for n in range(arrays):
+        for r in range(size):
+            for side in range(2 if r else 1):
+                spot = lax.rem((c + r if side else c + size - r), size)
+                for h in range(pieces):
+                    key = (n, r, side, h)
+                    place = (n * size + r) * pieces + h
+                    if r:
+                        source = outs[n].at[0, spot, cuts[h]]
+                    else:
+                        source = owns[n].at[pl.ds(pl.multiple_of(t * rows + h * step, step) if shared else h * step, step)]
+                    there = [outs[n].at[m, spot, cuts[h]] for m in range(4)]
+                    count = arrays * size * pieces
+                    if r < size - 1:
+                        for way in (0, 1) if r == 0 else (side,):
+                            z[key + (way,)] = remote(
+                                source, there[0], z_sent, z_here, way * count + place, before if way else behind
+                            )
+                    near = (n * size + spot) * pieces + h
+                    if shared and not r:
+                        continue
+                    x[key] = remote(source, there[1], x_sent, x_here, near, x_peer)
+                    core[(0,) + key] = remote(source, there[2], core_sent, core_here, near, core_peer)
+                    core[(1,) + key] = remote(there[1], there[3], core_sent, core_here, count + near, core_peer)
+                    if r:
+                        places[key] = remote(
+                            source, there[0], z_sent, z_here, side * count + place - pieces, before if side else behind
+                        )
+
+    def go_on(way):
+        return c > 0 if way else c < size - 1
+
+    pieces_of = [(n, h) for n in range(arrays) for h in range(pieces)]
+    for n, h in pieces_of:
+        for way in range(2):
+
+            @pl.when(go_on(way))
+            def _():
+                z[n, 0, 0, h, way].start()
+
+    for load in loads:
+        load.start()
+    if not shared:
+        for n, h in pieces_of:
+            x[n, 0, 0, h].start()
+            core[0, n, 0, 0, h].start()
+    for load in loads:
+        load.wait()
+    for keep in keeps:
+        keep.start()
+    arrivals = [(n, r, side, h) for r in range(1, size) for n in range(arrays) for side in range(2) for h in range(pieces)]
+
+    def there_is(key):
+        return c + key[1] < size if key[2] else c >= key[1]
+
+    for key in arrivals:
+
+        @pl.when(there_is(key))
+        def _():
+            places[key].wait_recv()
+            if key[1] < size - 1:
+
+                @pl.when(go_on(key[2]))
+                def _():
+                    z[key + (key[2],)].start()
+
+            x[key].start()
+            core[(0,) + key].start()
+
+    if not shared:
+        for n, h in pieces_of:
+            x[n, 0, 0, h].wait_recv()
+            core[1, n, 0, 0, h].start()
+    for key in arrivals:
+
+        @pl.when(there_is(key))
+        def _():
+            x[key].wait_recv()
+            core[(1,) + key].start()
+
+    if not shared:
+        for n, h in pieces_of:
+            x[n, 0, 0, h].wait_send()
+            core[0, n, 0, 0, h].wait()
+            core[1, n, 0, 0, h].wait()
+    for key in arrivals:
+
+        @pl.when(there_is(key))
+        def _():
+            x[key].wait_send()
+            core[(0,) + key].wait()
+            core[(1,) + key].wait()
+            if key[1] < size - 1:
+
+                @pl.when(go_on(key[2]))
+                def _():
+                    z[key + (key[2],)].wait_send()
+
+    for n, h in pieces_of:
+        for way in range(2):
+
+            @pl.when(go_on(way))
+            def _():
+                z[n, 0, 0, h, way].wait_send()
+
+    for keep in keeps:
+        keep.wait()
+
+
+def gather_rows(values, collective, *earlier, shared=False):
+    size, tps = lax.axis_size("ctx"), lax.axis_size("tp")
+    assert tps == 4
+    pieces, arrays = 2, len(values)
+    rows = values[0].shape[0] // (tps if shared else 1)
+    count = arrays * size * pieces
+    anywhere = pl.BlockSpec(memory_space=pl.ANY)
     return pl.pallas_call(
-        functools.partial(gather_kernel, size, pieces),
-        out_shape=jax.ShapeDtypeStruct((4, size) + values.shape, values.dtype),
-        in_specs=[pl.BlockSpec(memory_space=pl.ANY)],
-        out_specs=pl.BlockSpec(memory_space=pl.ANY),
-        scratch_shapes=[pltpu.SemaphoreType.DMA(())]
-        + [pltpu.SemaphoreType.DMA((n,)) for n in (count - pieces, count - pieces, count, count, 2 * count, 2 * count)],
-        compiler_params=pltpu.CompilerParams(collective_id=0, has_side_effects=True),
+        functools.partial(gather_kernel, size, pieces, arrays, shared, len(earlier)),
+        out_shape=[jax.ShapeDtypeStruct((tps, size, rows, v.shape[1]), v.dtype) for v in values],
+        in_specs=[anywhere] * (arrays + len(earlier)),
+        out_specs=[anywhere] * arrays,
+        scratch_shapes=[pltpu.VMEM(v.shape, v.dtype) for v in values]
+        + [
+            pltpu.SemaphoreType.DMA((n,))
+            for n in (5 * arrays, 2 * count, 2 * count, count, count, 2 * count, 2 * count)
+        ],
+        compiler_params=pltpu.CompilerParams(collective_id=collective, has_side_effects=True),
         name="gather_rows",
-    )(values)
-
-
-def scatter_kernel(size, parts, out, held, core_in, x_in, z_in, local, z_sent, z_here, x_sent, x_here, core_sent, core_here):
+    )(*values, *earlier)
+
+
+def scatter_kernel(size, earlier, parts, *refs):
+    out, held, core_in, x_in, z_in, local, z_sent, z_here, x_sent, x_here, core_sent, core_here = refs[earlier:]
     c, t = lax.axis_index("ctx"), lax.axis_index("tp")
     x_peer, core_peer = {"tp": t ^ 2}, {"tp": t ^ 1}
-    ahead = {r: {"ctx": lax.rem(c + r, size)} for r in range(1, size)}
-    greet([x_peer, core_peer] + [ahead[r] for r in range(1, size)])
-    spot = [lax.rem(c + r, size) for r in range(size)]
+    first, last = c == 0, c == size - 1
+    upper = c // (size // 2)
+    spot = [size - 1 - k + upper * (2 * k - size + 1) for k in range(size)]
+    before, behind = {"ctx": lax.max(c - 1, 0)}, {"ctx": lax.min(c + 1, size - 1)}
+    greet([x_peer, core_peer], ((jnp.logical_not(first), before), (jnp.logical_not(last), behind)))
     keep = pltpu.make_async_copy(parts.at[pl.ds(0, 2)], held, local)
     keep.start()
-    order = far_first(size) + [0]
     core = {
-        (m, r): remote(parts.at[2 + m, spot[r]], core_in.at[m, r], core_sent, core_here, m * size + r, core_peer)
+        (m, k): remote(parts.at[2 + m, spot[k]], core_in.at[m, k], core_sent, core_here, m * size + k, core_peer)
         for m in (1, 0)
-        for r in order
+        for k in range(size)
     }
-    x = {r: remote(held.at[1, spot[r]], x_in.at[r], x_sent, x_here, r, x_peer) for r in order}
-    z = {r: remote(held.at[0, spot[r]], z_in.at[r - 1], z_sent, z_here, r - 1, ahead[r]) for r in order[:-1]}
+    x = [remote(held.at[1, spot[k]], x_in.at[k], x_sent, x_here, k, x_peer) for k in range(size)]
+    rising = [remote(held.at[0, spot[k]], z_in.at[0, spot[k]], z_sent, z_here, spot[k], behind) for k in range(size)]
+    falling = [
+        remote(held.at[0, spot[k]], z_in.at[1, spot[k]], z_sent, z_here, size + spot[k], before) for k in range(size)
+    ]
     for copy in core.values():
         copy.start()
     keep.wait()
     tall = 16
-    steps = out.shape[0] // tall
-
-    for r in order:
-        core[1, r].wait_recv()
-
-        @pl.loop(0, steps)
+
+    def each(body):
+        @pl.loop(0, out.shape[0] // tall)
         def _(i):
-            rows = pl.ds(pl.multiple_of(i * tall, tall), tall)
-            held[1, spot[r], rows] = (held[1, spot[r], rows].astype(F32) + core_in[1, r, rows].astype(F32)).astype(BF16)
-
-        x[r].start()
-    for r in order:
-        core[0, r].wait_recv()
-        x[r].wait_recv()
-
-        @pl.loop(0, steps)
-        def _(i):
-            rows = pl.ds(pl.multiple_of(i * tall, tall), tall)
-            total = held[0, spot[r], rows].astype(F32) + core_in[0, r, rows].astype(F32) + x_in[r, rows].astype(F32)
-            if r == 0:
-                out[rows] = total
-            else:
-                held[0, spot[r], rows] = total.astype(BF16)
-
-        if r:
-            z[r].start()
-    for r in order[:-1]:
-        z[r].wait_recv()
-
-        @pl.loop(0, steps)
-        def _(i):
-            rows = pl.ds(pl.multiple_of(i * tall, tall), tall)
-            out[rows] = out[rows] + z_in[r - 1, rows].astype(F32)
-
-    for copy in list(core.values()) + list(x.values()) + list(z.values()):
+            body(pl.ds(pl.multiple_of(i * tall, tall), tall))
+
+    for k in range(size):
+        a = spot[k]
+        core[1, k].wait_recv()
+
+        def add_core(rows):
+            held[1, a, rows] = (held[1, a, rows].astype(F32) + core_in[1, k, rows].astype(F32)).astype(BF16)
+
+        each(add_core)
+        x[k].start()
+    for k in range(size):
+        a = spot[k]
+        core[0, k].wait_recv()
+        x[k].wait_recv()
+
+        def total(rows):
+            return held[0, a, rows].astype(F32) + core_in[0, k, rows].astype(F32) + x_in[k, rows].astype(F32)
+
+        def add(rows):
+            held[0, a, rows] = total(rows).astype(BF16)
+
+        def add_rising(rows):
+            held[0, a, rows] = (total(rows) + z_in[0, a, rows].astype(F32)).astype(BF16)
+
+        def add_falling(rows):
+            held[0, a, rows] = (total(rows) + z_in[1, a, rows].astype(F32)).astype(BF16)
+
+        def keep_total(rows):
+            out[rows] = total(rows)
+
+        @pl.when(a == c)
+        def _():
+            each(keep_total)
+
+        @pl.when(a > c)
+        def _():
+            @pl.when(first)
+            def _():
+                each(add)
+
+            @pl.when(jnp.logical_not(first))
+            def _():
+                rising[k].wait_recv()
+                each(add_rising)
+
+            rising[k].start()
+
+        @pl.when(a < c)
+        def _():
+            @pl.when(last)
+            def _():
+                each(add)
+
+            @pl.when(jnp.logical_not(last))
+            def _():
+                falling[k].wait_recv()
+                each(add_falling)
+
+            falling[k].start()
+
+    for side, edge in enumerate((first, last)):
+
+        @pl.when(jnp.logical_not(edge))
+        def _():
+            remote(
+                held.at[0, c], z_in.at[side, c], z_sent, z_here, side * size + c, before if side else behind
+            ).wait_recv()
+
+            def add_side(rows):
+                out[rows] = out[rows] + z_in[side, c, rows].astype(F32)
+
+            each(add_side)
+
+    for copy in list(core.values()) + x:
         copy.wait_send()
-
-
-def scatter_rows(parts, collective):
+    for k in range(size):
+
+        @pl.when(spot[k] > c)
+        def _():
+            rising[k].wait_send()
+
+        @pl.when(spot[k] < c)
+        def _():
+            falling[k].wait_send()
+
+
+def scatter_rows(parts, collective, *earlier):
     size = lax.axis_size("ctx")
     rows, width = parts.shape[2:]
     return pl.pallas_call(
-        functools.partial(scatter_kernel, size),
+        functools.partial(scatter_kernel, size, len(earlier)),
         out_shape=jax.ShapeDtypeStruct((rows, width), F32),
-        in_specs=[pl.BlockSpec(memory_space=pl.ANY)],
+        in_specs=[pl.BlockSpec(memory_space=pl.ANY)] * (1 + len(earlier)),
         out_specs=pl.BlockSpec(memory_space=pltpu.VMEM),
         scratch_shapes=[
             pltpu.VMEM((2, size, rows, width), BF16),
             pltpu.VMEM((2, size, rows, width), BF16),
             pltpu.VMEM((size, rows, width), BF16),
-            pltpu.VMEM((size - 1, rows, width), BF16),
+            pltpu.VMEM((2, size, rows, width), BF16),
             pltpu.SemaphoreType.DMA(()),
         ]
-        + [pltpu.SemaphoreType.DMA((n,)) for n in (size - 1, size - 1, size, size, 2 * size, 2 * size)],
+        + [pltpu.SemaphoreType.DMA((n,)) for n in (2 * size, 2 * size, size, size, 2 * size, 2 * size)],
         compiler_params=pltpu.CompilerParams(
-            collective_id=collective, has_side_effects=True, vmem_limit_bytes=32 * 1024 * 1024
+            collective_id=collective, has_side_effects=True, vmem_limit_bytes=40 * 1024 * 1024
         ),
         name="scatter_rows",
-    )(parts)
+    )(parts, *earlier)
 
 
 def sum_tokens(values):
-    for axis in ("tp", "ctx"):
-        for bit in bits(axis):
-            values = values + swap(values, axis, bit)
-    return values
+    size = lax.axis_size("ctx")
+    for bit in bits("tp"):
+        values = values + swap(values, "tp", bit)
+    found = jnp.stack([values] + [receive(values, "ctx", r) for r in range(1, size)])
+    return jnp.sum(ahead_first(found, lax.rem(size - lax.axis_index("ctx"), size)), axis=0)
 
 
 def own_block(values, ahead=0, axis=0):
@@ -291,8 +437,17 @@
     return ahead_first(whole, lax.rem(size - lax.axis_index("shard"), size) * values.shape[axis], axis)
 
 
-def after(values, *earlier):
-    return lax.optimization_barrier((values,) + earlier)[0]
+def corner(values):
+    return values[(0,) * values.ndim]
+
+
+def start_after(values):
+    first = corner(values)
+    return (first != first).astype(jnp.int32)
+
+
+def tie(values, earlier):
+    return values + (corner(earlier).astype(F32) * 0.0).astype(values.dtype)
 
 
 def part_order(values):
@@ -327,6 +482,81 @@
     weighted = grad * gain
     middle = jnp.mean(values * weighted, axis=-1, keepdims=True)
     return scale * weighted - values * (scale * scale * scale) * middle, grad * values * scale
+
+
+def expert_kernel(group, tall, hidden, *refs):
+    chunks, up, down, up_rows, down_rows = refs[:group], *refs[group:]
+    pieces = hidden // 128
+    ctxs = chunks[0].shape[0]
+    experts = group * ctxs
+    for i in range(group):
+        for j in range(ctxs):
+            e = j * group + i
+            for p in range(2 * pieces):
+                side, piece = p // pieces, p % pieces
+                value = chunks[i][j, :, p * 128 : p * 128 + 128].astype(F32)
+                up_rows[pl.ds((e * pieces + piece) * 2 + side, tall, stride=experts * pieces * 2), :] = value
+            for piece in range(pieces):
+                value = chunks[i][j, :, (2 * pieces + piece) * 128 : (2 * pieces + piece) * 128 + 128].astype(F32)
+                row = (e // 8 * pieces + piece) * 8 + e % 8
+                down_rows[pl.ds(row, tall, stride=experts * pieces), :] = value
+    up[...] = up_rows[...].reshape(up.shape)
+    down[...] = down_rows[...].reshape(down.shape)
+
+
+def expert_gradients(chunks):
+    group = len(chunks)
+    ctxs, rows, width = chunks[0].shape
+    hidden, experts = width // 3, group * ctxs
+    pieces = hidden // 128
+    assert experts % 8 == 0 and hidden % 128 == 0
+    tall = 32
+    up, down = pl.pallas_call(
+        functools.partial(expert_kernel, group, tall, hidden),
+        grid=(rows // tall,),
+        in_specs=[pl.BlockSpec((ctxs, tall, width), lambda b: (0, b, 0))] * group,
+        out_specs=[
+            pl.BlockSpec((tall, experts * pieces * 2, 128), lambda b: (b, 0, 0)),
+            pl.BlockSpec((tall, experts * pieces, 128), lambda b: (b, 0, 0)),
+        ],
+        out_shape=[
+            jax.ShapeDtypeStruct((rows, experts * pieces * 2, 128), F32),
+            jax.ShapeDtypeStruct((rows, experts * pieces, 128), F32),
+        ],
+        scratch_shapes=[
+            pltpu.VMEM((tall * experts * pieces * 2, 128), F32),
+            pltpu.VMEM((tall * experts * pieces, 128), F32),
+        ],
+        compiler_params=pltpu.CompilerParams(vmem_limit_bytes=32 * 1024 * 1024),
+        name="expert_gradients",
+    )(*chunks)
+    up = up.reshape(rows, experts, pieces, 2, 128).transpose(0, 1, 3, 2, 4).reshape(rows, experts, 2, hidden)
+    down = down.reshape(rows, experts // 8, pieces, 8, 128).transpose(0, 1, 3, 2, 4).reshape(rows, experts, hidden)
+    return up, down
+
+
+def attention_kernel(chunk, entry, exit_out):
+    ctxs, _, width = chunk.shape
+    head = width // 4
+    for j in range(ctxs):
+        for k in range(3):
+            entry[k, :, j * head : (j + 1) * head] = chunk[j, :, k * head : (k + 1) * head].astype(F32)
+        exit_out[:, j * head : (j + 1) * head] = chunk[j, :, 3 * head :].astype(F32)
+
+
+def attention_gradients(chunk):
+    ctxs, rows, width = chunk.shape
+    wide = ctxs * width // 4
+    tall = 128
+    entry, exit_out = pl.pallas_call(
+        attention_kernel,
+        grid=(rows // tall,),
+        in_specs=[pl.BlockSpec((ctxs, tall, width), lambda b: (0, b, 0))],
+        out_specs=[pl.BlockSpec((3, tall, wide), lambda b: (0, b, 0)), pl.BlockSpec((tall, wide), lambda b: (b, 0))],
+        out_shape=[jax.ShapeDtypeStruct((3, rows, wide), F32), jax.ShapeDtypeStruct((rows, wide), F32)],
+        name="attention_gradients",
+    )(chunk)
+    return entry.transpose(1, 0, 2), exit_out
 
 
 def local(
@@ -362,26 +592,27 @@
     gain_one, gain_two = gains[0], gains[1]
     head_gains = gather_small(head_gain[None], 1)[0].astype(F32)
     head_in = lax.dynamic_slice_in_dim(attention_in, c * head_size, head_size, axis=2)
-    head_in = head_in.reshape(block, 3 * head_size)
+    head_in = gather_natural(head_in.reshape(block, 3 * head_size), "shard")
+    exit_weight = gather_natural(ahead_first(attention_out, c * head_size, 1), "shard")
+
+    def expert_weights(start, count):
+        inward = lax.dynamic_slice_in_dim(expert_in, start, count, axis=1)
+        outward = lax.dynamic_slice_in_dim(expert_out, start, count, axis=1)
+        inward = [inward[:, i].reshape(block, 2 * hidden_size) for i in range(count)]
+        outward = outward.reshape(block, count * hidden_size)
+        return inward, outward
+
     first = t * own
-    tokens_own = after(lax.dynamic_slice_in_dim(tokens[0], first, own), head_in)
-    head_in = gather_natural(head_in, "shard")
-    tokens_all = gather_rows(tokens_own).reshape(every, width)
-    attention_out, expert_in, expert_out, cotangent, routes = lax.optimization_barrier(
-        (attention_out, expert_in, expert_out, cotangent, routes, tokens_all)
-    )[:-1]
-    exit_weight = gather_natural(ahead_first(attention_out, c * head_size, 1), "shard")
-    group_out = lax.dynamic_slice_in_dim(expert_out, base, group, axis=1)
-    group_out = gather_natural(group_out.reshape(block, group * hidden_size), "shard")
-    group_in = lax.dynamic_slice_in_dim(expert_in, base, group, axis=1)
-    in_weights = [
-        gather_natural(group_in[:, i].reshape(block, 2 * hidden_size), "shard") for i in range(group)
-    ]
+    tokens_own = lax.dynamic_slice_in_dim(tokens[0], first, own)
+    cot_own = lax.dynamic_slice_in_dim(cotangent[0], first, own)
+    inward, outward = expert_weights(base, 1)
+    tokens_all, cot_all = gather_rows([tokens[0], cotangent[0]], 3, inward[0], outward, shared=True)
+    tokens_all, cot_all = tokens_all.reshape(every, width), cot_all.reshape(every, width)
+    in_weights = [gather_natural(inward[0], "shard")]
+    out_weights = [gather_natural(outward, "shard")]
 
     layer_in = tokens_own.astype(F32)
-    cot_own = lax.dynamic_slice_in_dim(cotangent[0], first, own)
     upstream = cot_own.astype(F32)
-    cot_all = spread_tp(gather_ctx(cot_own))
     choices_all = gather_ctx(routes[0]).reshape(ctxs, tps, own, -1)
     picks_all = jnp.any(part_order(choices_all)[..., None] == jnp.arange(experts), axis=3)
     picks = lax.dynamic_index_in_dim(picks_all[0], c, 0, False)
@@ -411,26 +642,38 @@
     blocks = ahead_first(mixed_head.reshape(tps, ctxs, own, head_size), c, 1)
     mixed = [blocks[:, 0]] + [receive(blocks[:, ctxs - j], "ctx", j) for j in range(1, ctxs)]
     mixed = jnp.concatenate([m.reshape(rows, head_size) for m in mixed], axis=1)
+    inward, outward = expert_weights(base + 1 + start_after(mixed), group - 1)
+    in_weights.append(gather_natural(inward[0], "shard"))
+    outward = gather_natural(outward, "shard")
+    out_weights += [outward[:, i * hidden_size : (i + 1) * hidden_size] for i in range(group - 1)]
+    in_weights += [gather_natural(inward[i], "shard") for i in range(1, group - 1)]
     residual = layer_in + scatter_tp(dot(mixed, exit_weight, (1, 1)))
 
     normed_two = lower(residual * inverse_scale(residual) * gain_two)
-    normed_two_all = gather_rows(normed_two).reshape(every, width)
+    normed_two_all = gather_rows([normed_two], 0)[0].reshape(every, width)
     chances_all = jax.nn.softmax(dot(normed_two_all, router, (1, 0)), axis=-1)
     gates = jnp.where(picks_all, chances_all, 0.0)
     gates = lax.dynamic_slice_in_dim(gates, base, group, axis=1)
     normed_blocks = [own_block(normed_two_all, r, 1) for r in range(shards)]
     cot_blocks = [own_block(cot_all, r, 1) for r in range(shards)]
-    backs = dot(cot_all, group_out, (1, 0))
-    scaled, gate_parts, inner_grads, products = [], [], [], []
-    rows_now = normed_two_all
+    scaled, gate_parts, inner_grads, products, chunks, gathered = [], [], [], [], [], []
+
+    def finish(i):
+        own_part, others = products[i]
+        chunks.append(lower(product_sum(tie(own_part, products[-1][1][0]), others)))
+        chunk = chunks[i] if i < 2 else tie(chunks[i], gathered[i - 2])
+        gathered.append(lax.all_gather(chunk, "ctx", axis=0, tiled=False))
+
     for i in range(group):
-        gate_up = dot(rows_now, in_weights[i], (1, 0))
+        gate_up = dot(normed_two_all, in_weights[i], (1, 0))
         gate, up = gate_up[:, :hidden_size], gate_up[:, hidden_size:]
-        back = backs[:, i * hidden_size : (i + 1) * hidden_size]
+        back = dot(cot_all, out_weights[i], (1, 0))
         sigmoid = jax.nn.sigmoid(gate)
         silu = gate * sigmoid
         hidden = lower(silu * up).astype(F32)
         weight = gates[:, i : i + 1]
+        if i >= 2:
+            weight = tie(weight, chunks[max(i - 3, 0)])
         scaled.append(lower(hidden * weight))
         gate_parts.append(jnp.sum(hidden * back, axis=1))
         hidden_grad = back * weight
@@ -442,18 +685,19 @@
             )
         )
         products.append(product_parts([(normed_blocks, inner_grads[i]), (cot_blocks, scaled[i])]))
-        rows_now = after(rows_now, *products[i])
+        if i != 1:
+            finish(max(i - 1, 0))
+    finish(group - 1)
 
     normed_part = sum(dot(inner_grads[i], in_weights[i], (1, 1)) for i in range(group))
     gate_part = lax.dynamic_update_slice(
         jnp.zeros((every, 128), F32), jnp.stack(gate_parts, axis=1), (0, base)
     )
     normed_part = lower(jnp.concatenate([normed_part, gate_part], axis=1))
-    normed_sum = scatter_rows(normed_part.reshape(tps, ctxs, own, -1), 1)
+    normed_sum = scatter_rows(normed_part.reshape(tps, ctxs, own, -1), 1, chunks[-2])
+    result_part = lower(sum(dot(scaled[i], out_weights[i], (1, 1)) for i in range(group)))
+    result_sum = scatter_rows(result_part.reshape(tps, ctxs, own, width), 2, normed_sum)
     normed_sum, gate_grad = normed_sum[:, :width], normed_sum[:, width : width + experts]
-    chunks = [
-        lax.all_gather(lower(product_sum(*products[i])), "ctx", axis=0, tiled=False) for i in range(group)
-    ]
 
     router_chances = jax.nn.softmax(dot(normed_two, router, (1, 0)), axis=-1)
     chance_grad = jnp.where(picks, gate_grad, 0.0)
@@ -488,14 +732,11 @@
     )
     entry_blocks = [own_block(normed_one_all, r, 1) for r in range(shards)]
     entry_head = product_sum(*product_parts([(entry_blocks, projected_grad)]))
-    attention_chunk = lax.all_gather(
-        lower(jnp.concatenate([entry_head, exit_head], axis=1)), "ctx", axis=0, tiled=False
-    )
+    attention_chunk = tie(lower(jnp.concatenate([entry_head, exit_head], axis=1)), gathered[-2])
+    attention_chunk = lax.all_gather(attention_chunk, "ctx", axis=0, tiled=False)
     first_part = dot(projected_grad, head_in, (1, 1), BF16)
-    first_normed_grad = scatter_rows(first_part.reshape(tps, ctxs, own, width), 2)
-
-    result_part = dot(after(jnp.concatenate(scaled, axis=1), mixed_grad), group_out, (1, 1), BF16)
-    result_sum = scatter_rows(result_part.reshape(tps, ctxs, own, width), 2)
+    first_normed_grad = scatter_rows(first_part.reshape(tps, ctxs, own, width), 4, chunks[-1])
+
     layer_output = natural_rows(gather_tp(lower(residual + result_sum)))[None]
 
     input_back, first_part = norm_back(first_normed_grad, layer_in, gain_one)
@@ -510,19 +751,8 @@
     head_gradient = sum_shard(small_sum[-1:, : head_part.shape[0]], 1)[0]
     small_sum = sum_shard(small_sum[:-1], 1)
 
-    wide = jnp.moveaxis(attention_chunk, 0, 1).astype(F32)
-    entry_gradient = jnp.moveaxis(
-        wide[:, :, : 3 * head_size].reshape(block, ctxs, 3, head_size), 1, 2
-    ).reshape(block, 3, local_width)
-    exit_gradient = wide[:, :, 3 * head_size :].reshape(block, local_width)
-    upward_gradient = jnp.zeros((block, experts, 2, hidden_size), F32)
-    downward_gradient = jnp.zeros((block, experts, hidden_size), F32)
-    for i in range(group):
-        for j in range(ctxs):
-            up = chunks[i][j][:, : 2 * hidden_size].astype(F32).reshape(block, 1, 2, hidden_size)
-            down = chunks[i][j][:, 2 * hidden_size :].astype(F32)[:, None]
-            upward_gradient = lax.dynamic_update_slice(upward_gradient, up, (0, j * group + i, 0, 0))
-            downward_gradient = lax.dynamic_update_slice(downward_gradient, down, (0, j * group + i, 0))
+    upward_gradient, downward_gradient = expert_gradients(gathered)
+    entry_gradient, exit_gradient = attention_gradients(attention_chunk)
     return (
         layer_output,
         input_gradient,

time: 1320 us -> 1020 us (0.77)
  waiting for transfers between devices: 407 us -> 174 us
  local copies, waits for them, and re-layouts: 208 us -> 73.5 us
  Pallas kernels: 306 us -> 404 us
  other arithmetic: 141 us -> 72.8 us
  matrix products: 182 us -> 214 us
    all_gather x5, waiting for transfers between devices: 157 us -> 0.03 us  [the longest x4 0.03 us: finish(): gathered.append(lax.all_gather(chunk, 'ctx', axis=0, tiled=False))]
    pallas_call x5 -> x7, Pallas kernels: 306 us -> 404 us  [the longest x3 238 us: scatter_rows(): pl.pallas_call(functools.partial(scatter_kernel, size, len(earlier)), out...]
    ppermute x15 -> x10, waiting for transfers between devices: 110 us -> 32.7 us  [swap(): return lax.ppermute(values, axis, [(i, i ^ bit) for i in range(size)])]
    dynamic_update_slice x17 -> x0, other arithmetic: 56.6 us -> none  [the longest x16 40.1 us: local(): lax.dynamic_update_slice(downward_gradient, down, (0, j * group + i, 0))]
    reshape x16 -> x0, local copies, waits for them, and re-layouts: 53.8 us -> none  [local(): chunks[i][j][:, :2 * hidden_size].astype(F32)]
    dynamic_update_slice x15 -> x0, local copies, waits for them, and re-layouts: 32.2 us -> none  [local(): lax.dynamic_update_slice(upward_gradient, up, (0, j * group + i, 0, 0))]
    dot_general x38 -> x44, matrix products: 168 us -> 199 us  [dot(): lax.dot_general(left, right, (((over[0],), (over[1],)), ((), ())), prefer...]
    unnamed x320 -> x327, local copies, waits for them, and re-layouts: 58.6 us -> 33.1 us
  transfers between devices with their start and end apart: 53 -> 49, of which waited for: 22 -> 18; matrix products, arithmetic and copies ran while one was open for 25% -> 33% of each run, Pallas kernels for 15% -> 39%
where the time goes in v3:
time: 1020 us; the launch traced here: 1010 us
  Pallas kernels  404 us (40%)
  matrix products  214 us (21%)
  waiting for transfers between devices  174 us (17%)
  local copies, waits for them, and re-layouts  73.5 us (7%)
  other arithmetic  72.8 us (7%)
  starting transfers between devices  44.7 us (4%)
  between operations  22.9 us (2%)
    pallas_call x3, Pallas kernels, scatter_rows(): pl.pallas_call(functools.partial(scatter_kernel, size, len(earlier)), out...  238 us
    dot_general x44, matrix products, dot(): lax.dot_general(left, right, (((over[0],), (over[1],)), ((), ())), prefer...  199 us
    ppermute x26, waiting for transfers between devices, receive(): lax.ppermute(values, axis, [((i + distance) % size, i) for i in range(siz...  141 us
    pallas_call x2, Pallas kernels, gather_rows(): pl.pallas_call(functools.partial(gather_kernel, size, pieces, arrays, sha...  104 us
    pallas_call x1, Pallas kernels, expert_gradients(): pl.pallas_call(functools.partial(expert_kernel, group, tall, hidden), gri...  54.7 us
    ppermute x26, starting transfers between devices, receive(): lax.ppermute(values, axis, [((i + distance) % size, i) for i in range(siz...  39.8 us
    unnamed x327, local copies, waits for them, and re-layouts  33.1 us
    ppermute x10, waiting for transfers between devices, swap(): return lax.ppermute(values, axis, [(i, i ^ bit) for i in range(size)])  32.7 us
  transfers between devices with their start and end apart: 49, of which 18 were waited for; matrix products, arithmetic and copies ran while one was open for 33% of the time, Pallas kernels for 39%

profile of v3, /device:TPU:0, one launch (start us, length us, event | category | flops | bytes accessed | tf_op | source)
XLA Modules:
  0.0 1005.7 jit_solution(358938196722272247)
XLA Ops:
  25.9 64.6 %gather_rows.2 = (bf16[4,4,96,2048]{3,2,1,0:T(8,128)(2,1)}, bf16[4,4,96,2048]{3,2,1,0:T(8,128)(2,1)}) custom-call(bf16[384,2048]{1,0:T(8,128)(2,1)} %bitcast.347, bf16[384,2048]{1,0:T(8,128)(2,1)} %bitcast.360, bf16[1024,512]{1,0:T(8,128)(2,1)} %bitcast.341, bf16[1024,256]{1,0:T(8,128)(2,1)} %bitcast.361), custom_call_target="tpu_custom_call" | custom-call | tf_op jit(solution)/shard_map/gather_rows/pallas_call | solution.py:231
  173.8 39.1 %gather_rows.3 = bf16[4,4,96,2048]{3,2,1,0:T(8,128)(2,1)} custom-call(bf16[96,2048]{1,0:T(8,128)(2,1)} %multiply_convert_fusion.14.refs_0_), custom_call_target="tpu_custom_call" | custom-call | tf_op jit(solution)/shard_map/gather_rows/pallas_call | solution.py:231
  218.2 9.0 fusion.274
  250.3 46.8 %collective-permute-done.11 = bf16[1024,768]{1,0:T(8,128)(2,1)S(1)} collective-permute-done((bf16[1024,768]{1,0:T(8,128)(2,1)S(1)}, bf16[1024,768]{1,0:T(8,128)(2,1)S(1)}, u32[]{:S(2)}, u32[]{:S(2)}) %collective-permute-start.11) | collective-permute-done | bytes 1572896 | tf_op jit(solution)/shard_map/ppermute | solution.py:29
  299.0 7.0 fusion.1
  306.2 8.6 fusion.276
  314.7 8.8 fusion.275
  325.5 7.2 multiply_convert_fusion.7
  351.7 22.8 %collective-permute-done.35 = bf16[1024,768]{0,1:T(8,128)(2,1)S(1)} collective-permute-done((bf16[1024,768]{0,1:T(8,128)(2,1)S(1)}, bf16[1024,768]{0,1:T(8,128)(2,1)S(1)}, u32[]{:S(2)}, u32[]{:S(2)}) %collective-permute-start.35) | collective-permute-done | bytes 1572896 | tf_op jit(solution)/shard_map/ppermute | solution.py:29
  432.1 7.1 fusion.176
  445.6 17.6 %add_convert_fusion = bf16[1536,2048]{1,0:T(8,128)(2,1)} fusion(f32[1536,2048]{1,0:T(8,128)} %fusion.176, f32[1536,2048]{1,0:T(8,128)} %fusion.178, f32[1536,2048]{1,0:T(8,128)} %fusion.177, bf16[2048,512]{1,0:T(8,128)(2,1)S(1)} %copy-done.18, bf16[1536,256]{0,1:T(8,128)(2,1)} %copy-done.49, bf16[1536,256]{0,1:T(8,128)(2,1)} %copy-done.47), kind=kOutput, calls=%fused_computation.3 | convolution fusion | flops 3236954112 | bytes 47710208 | tf_op jit(solution)/shard_map/dot_general | solution.py:23
  469.6 16.2 %add_convert_fusion.1 = bf16[1536,2048]{1,0:T(8,128)(2,1)} fusion(f32[1536,2048]{1,0:T(8,128)} %fusion.109, f32[1536,2048]{1,0:T(8,128)} %fusion.101, f32[1536,2048]{1,0:T(8,128)} %fusion.113, bf16[2048,768]{0,1:T(8,128)(2,1)} %all-gather.27.cloned.1.call-done, bf16[1536,256]{0,1:T(8,128)(2,1)S(1)} %copy-done.51, f32[1536]{0:T(1024)S(1)} %copy-done.85), kind=kOutput, calls=%fused_computation.4 | convolution fusion | flops 1624375296 | bytes 45881344 | tf_op jit(solution)/shard_map/dot_general | solution.py:23
  491.4 69.5 %scatter_rows.3.refs_0_ = f32[96,2176]{1,0:T(8,128)S(1)} custom-call(bf16[4,4,96,2176]{3,2,1,0:T(8,128)(2,1)S(1)} %pad_maximum_fusion.parts, bf16[1024,768]{1,0:T(8,128)(2,1)S(1)} %copy-done.5), custom_call_target="tpu_custom_call" | custom-call | tf_op jit(solution)/shard_map/scatter_rows/pallas_call | solution.py:365
  561.0 87.9 %scatter_rows.4 = f32[96,2048]{1,0:T(8,128)S(1)} custom-call(bf16[4,4,96,2048]{3,2,1,0:T(8,128)(2,1)S(1)} %bitcast.306, f32[96,2176]{1,0:T(8,128)S(1)} %scatter_rows.3.refs_0_), custom_call_target="tpu_custom_call" | custom-call | tf_op jit(solution)/shard_map/scatter_rows/pallas_call | solution.py:365
  654.4 8.5 collective-permute-done.15
  668.5 7.4 collective-permute-done.13
  691.9 12.1 %collective-permute-done.18 = bf16[4,96,128]{2,1,0:T(8,128)(2,1)S(1)} collective-permute-done((bf16[4,96,128]{2,1,0:T(8,128)(2,1)S(1)}, bf16[4,96,128]{2,1,0:T(8,128)(2,1)S(1)}, u32[]{:S(2)}, u32[]{:S(2)}) %collective-permute-start.18) | collective-permute-done | bytes 98336 | tf_op jit(solution)/shard_map/ppermute | solution.py:29
  710.4 8.6 copy.181
  725.2 7.8 multiply_convert_fusion.1
  753.6 80.7 %scatter_rows.5 = f32[96,2048]{1,0:T(8,128)S(1)} custom-call(bf16[4,4,96,2048]{3,2,1,0:T(8,128)(2,1)S(1)} %bitcast.309, bf16[1024,768]{1,0:T(8,128)(2,1)S(1)} %get-tuple-element.38.refs_0_), custom_call_target="tpu_custom_call" | custom-call | tf_op jit(solution)/shard_map/scatter_rows/pallas_call | solution.py:365
  855.9 22.0 %collective-permute-done.33 = bf16[1024,128]{0,1:T(8,128)(2,1)S(1)} collective-permute-done((bf16[1024,128]{0,1:T(8,128)(2,1)S(1)}, bf16[1024,128]{0,1:T(8,128)(2,1)S(1)}, u32[]{:S(2)}, u32[]{:S(2)}) %collective-permute-start.33) | collective-permute-done | bytes 262176 | tf_op jit(solution)/shard_map/ppermute | solution.py:29
  903.1 16.3 %collective-permute-done.26 = f32[19,2048]{1,0:T(8,128)S(1)} collective-permute-done((f32[19,2048]{1,0:T(8,128)S(1)}, f32[19,2048]{1,0:T(8,128)S(1)}, u32[]{:S(2)}, u32[]{:S(2)}) %collective-permute-start.26) | collective-permute-done | bytes 155680 | tf_op jit(solution)/shard_map/ppermute | solution.py:29
  936.8 54.7 %expert_gradients.1 = (f32[1024,64,128]{2,1,0:T(8,128)}, f32[1024,32,128]{2,1,0:T(8,128)}) custom-call(bf16[4,1024,768]{2,1,0:T(8,128)(2,1)S(1)} %bitcast.311, bf16[4,1024,768]{2,1,0:T(8,128)(2,1)S(1)} %bitcast.308, bf16[4,1024,768]{2,1,0:T(8,128)(2,1)S(1)} %bitcast.313, bf16[4,1024,768]{2,1,0:T(8,128)(2,1)} %bitcast.346), custom_call_target="tpu_custom_call" | custom-call | tf_op jit(solution)/shard_map/expert_gradients/pallas_call | solution.py:514
  991.4 7.5 attention_gradients.1
  (615 shorter events, 345.1 us)
Async XLA Ops:
  7.2 95.0 %all-gather.19.cloned.1.call-start = ((), (), s32[]{:S(2)}) async-start(), calls=%async_computation | async-start | bytes 2359296 | tf_op jit(solution)/shard_map/all_gather | solution.py:431
  12.5 138.1 %all-gather.21.cloned.1.call-start = ((), (), s32[]{:S(2)}) async-start(), calls=%async_computation.1 | async-start | bytes 3145728 | tf_op jit(solution)/shard_map/all_gather | solution.py:431
  13.9 204.2 %all-gather.23.cloned.1.call-start = ((), (), s32[]{:S(2)}) async-start(), calls=%async_computation.2 | async-start | bytes 3145728 | tf_op jit(solution)/shard_map/all_gather | solution.py:431
  17.2 209.9 %all-gather.35.cloned.1.call-start = ((), (), s32[]{:S(2)}) async-start(), calls=%async_computation.8 | async-start | bytes 1572864 | tf_op jit(solution)/shard_map/all_gather | solution.py:431
  17.3 77.7 %collective-permute-start = (bf16[2,1024]{1,0:T(2,128)(2,1)S(1)}, bf16[2,1024]{1,0:T(2,128)(2,1)S(1)}, u32[]{:S(2)}, u32[]{:S(2)}) collective-permute-start(bf16[2,1024]{1,0:T(2,128)(2,1)S(1)} %pad_maximum_fusion.39), channel_id=1, source_target_pairs={{16,0},{0,16},{17,1},{1,17},{18,2},{2,18},{19,3},{3,19},{20,4},{4,... | collective-permute-start | bytes 12296 | tf_op jit(solution)/shard_map/ppermute | solution.py:29
  20.4 74.6 %collective-permute-start.1 = (bf16[1,128]{1,0:T(2,128)(2,1)S(1)}, bf16[1,128]{1,0:T(2,128)(2,1)S(1)}, u32[]{:S(2)}, u32[]{:S(2)}) collective-permute-start(bf16[1,128]{1,0:T(2,128)(2,1)S(1)} %bitcast.413), channel_id=1, source_target_pairs={{16,0},{0,16},{17,1},{1,17},{18,2},{2,18},{19,3},{3,19},{20,4},{4,... | collective-permute-start | bytes 776 | tf_op jit(solution)/shard_map/ppermute | solution.py:29
  25.0 281.2 %all-gather.29.cloned.1.call-start = ((), (), s32[]{:S(2)}) async-start(), calls=%async_computation.5 | async-start | bytes 3145728 | tf_op jit(solution)/shard_map/all_gather | solution.py:431
  125.9 188.8 %all-gather.25.cloned.1.call-start = ((), (), s32[]{:S(2)}) async-start(), calls=%async_computation.3 | async-start | bytes 3145728 | tf_op jit(solution)/shard_map/all_gather | solution.py:431
  127.2 198.2 %all-gather.27.cloned.1.call-start = ((), (), s32[]{:S(2)}) async-start(), calls=%async_computation.4 | async-start | bytes 4718592 | tf_op jit(solution)/shard_map/all_gather | solution.py:431
  139.9 251.8 %all-gather.31.cloned.1.call-start = ((), (), s32[]{:S(2)}) async-start(), calls=%async_computation.6 | async-start | bytes 3145728 | tf_op jit(solution)/shard_map/all_gather | solution.py:431
  163.9 299.3 %all-gather.37.cloned.1.call-start = ((), (), s32[]{:S(2)}) async-start(), calls=%async_computation.9 | async-start | bytes 7864320 | tf_op jit(solution)/shard_map/all_gather | solution.py:665
  240.6 56.5 %collective-permute-start.11 = (bf16[1024,768]{1,0:T(8,128)(2,1)S(1)}, bf16[1024,768]{1,0:T(8,128)(2,1)S(1)}, u32[]{:S(2)}, u32[]{:S(2)}) collective-permute-start(bf16[1024,768]{1,0:T(8,128)(2,1)S(1)} %pad_maximum_fusion.2), channel_id=1, source_target_pairs={{16,0},{0,16},{17,1},{1,17},{18,2},{2,18},{19,3},{3,19},{20,4},{4,... | collective-permute-start | bytes 4718600 | tf_op jit(solution)/shard_map/ppermute | solution.py:29
  298.8 411.6 %all-gather.41.cloned.1.call-start = ((), (), s32[]{:S(2)}) async-start(), calls=%async_computation.11 | async-start | bytes 7864320 | tf_op jit(solution)/shard_map/all_gather | solution.py:665
  338.6 35.9 %collective-permute-start.35 = (bf16[1024,768]{0,1:T(8,128)(2,1)S(1)}, bf16[1024,768]{0,1:T(8,128)(2,1)S(1)}, u32[]{:S(2)}, u32[]{:S(2)}) collective-permute-start(bf16[1024,768]{0,1:T(8,128)(2,1)S(1)} %pad_maximum_fusion.11), channel_id=1, source_target_pairs={{16,0},{0,16},{17,1},{1,17},{18,2},{2,18},{19,3},{3,19},{20,4},{4,... | collective-permute-start | bytes 4718600 | tf_op jit(solution)/shard_map/ppermute | solution.py:29
  376.3 507.0 %all-gather.39.cloned.1.call-start = ((), (), s32[]{:S(2)}) async-start(), calls=%async_computation.10 | async-start | bytes 7864320 | tf_op jit(solution)/shard_map/all_gather | solution.py:665
  402.7 62.3 %collective-permute-start.12 = (bf16[1024,768]{1,0:T(8,128)(2,1)}, bf16[1024,768]{1,0:T(8,128)(2,1)}, u32[]{:S(2)}, u32[]{:S(2)}) collective-permute-start(bf16[1024,768]{1,0:T(8,128)(2,1)} %pad_maximum_fusion.6), channel_id=1, source_target_pairs={{16,0},{0,16},{17,1},{1,17},{18,2},{2,18},{19,3},{3,19},{20,4},{4,... | collective-permute-start | bytes 4718600 | tf_op jit(solution)/shard_map/ppermute | solution.py:29
  469.5 458.9 %all-gather.43.cloned.1.call-start = ((), (), s32[]{:S(2)}) async-start(), calls=%async_computation.12 | async-start | bytes 7864320 | tf_op jit(solution)/shard_map/all_gather | solution.py:665
  664.8 56.1 %collective-permute-start.20 = (bf16[1024,768]{1,0:T(8,128)(2,1)}, bf16[1024,768]{1,0:T(8,128)(2,1)}, u32[]{:S(2)}, u32[]{:S(2)}) collective-permute-start(bf16[1024,768]{1,0:T(8,128)(2,1)} %pad_maximum_fusion.9), channel_id=1, source_target_pairs={{16,0},{0,16},{17,1},{1,17},{18,2},{2,18},{19,3},{3,19},{20,4},{4,... | collective-permute-start | bytes 4718600 | tf_op jit(solution)/shard_map/ppermute | solution.py:29
  687.5 151.6 %collective-permute-start.31 = (bf16[1024,512]{0,1:T(8,128)(2,1)}, bf16[1024,512]{0,1:T(8,128)(2,1)}, u32[]{:S(2)}, u32[]{:S(2)}) collective-permute-start(bf16[1024,512]{0,1:T(8,128)(2,1)} %convolution_convert_fusion.3), channel_id=1, source_target_pairs={{16,0},{0,16},{17,1},{1,17},{18,2},{2,18},{19,3},{3,19},{20,4},{4,... | collective-permute-start | bytes 3145736 | tf_op jit(solution)/shard_map/ppermute | solution.py:29
  725.0 266.4 %all-gather.33.cloned.1.call-start = ((), (), s32[]{:S(2)}) async-start(), calls=%async_computation.7 | async-start | bytes 5242880 | tf_op jit(solution)/shard_map/all_gather | solution.py:736
  744.1 105.1 %collective-permute-start.30 = (bf16[1024,384]{0,1:T(8,128)(2,1)}, bf16[1024,384]{0,1:T(8,128)(2,1)S(1)}, u32[]{:S(2)}, u32[]{:S(2)}) collective-permute-start(bf16[1024,384]{0,1:T(8,128)(2,1)} %fusion.83), channel_id=1, source_target_pairs={{16,0},{0,16},{17,1},{1,17},{18,2},{2,18},{19,3},{3,19},{20,4},{4,... | collective-permute-start | bytes 2359304 | tf_op jit(solution)/shard_map/ppermute | solution.py:29
  837.4 52.7 %collective-permute-start.24 = (f32[19,2048]{1,0:T(8,128)S(1)}, f32[19,2048]{1,0:T(8,128)}, u32[]{:S(2)}, u32[]{:S(2)}) collective-permute-start(f32[19,2048]{1,0:T(8,128)S(1)} %fusion.256), channel_id=1, source_target_pairs={{0,2},{1,3},{2,0},{3,1},{4,6},{5,7},{6,4},{7,5},{8,10},{9,11},{10,... | collective-permute-start | bytes 466952 | tf_op jit(solution)/shard_map/ppermute | solution.py:34
  843.6 34.3 %collective-permute-start.33 = (bf16[1024,128]{0,1:T(8,128)(2,1)S(1)}, bf16[1024,128]{0,1:T(8,128)(2,1)S(1)}, u32[]{:S(2)}, u32[]{:S(2)}) collective-permute-start(bf16[1024,128]{0,1:T(8,128)(2,1)S(1)} %get-tuple-element.91), channel_id=1, source_target_pairs={{8,0},{12,4},{0,8},{4,12},{9,1},{13,5},{1,9},{5,13},{10,2},{14,6},... | collective-permute-start | bytes 786440 | tf_op jit(solution)/shard_map/ppermute | solution.py:29
  847.0 36.1 %collective-permute-start.32 = (bf16[1024,128]{0,1:T(8,128)(2,1)S(1)}, bf16[1024,128]{0,1:T(8,128)(2,1)S(1)}, u32[]{:S(2)}, u32[]{:S(2)}) collective-permute-start(bf16[1024,128]{0,1:T(8,128)(2,1)S(1)} %get-tuple-element.89), channel_id=1, source_target_pairs={{12,0},{0,4},{4,8},{8,12},{13,1},{1,5},{5,9},{9,13},{14,2},{2,6},{... | collective-permute-start | bytes 786440 | tf_op jit(solution)/shard_map/ppermute | solution.py:29
  (173 other events, 3258.7 us)
Sparse Core Ops, SparseCore 0:
  12.6 29.8 all-gather.18
  44.7 33.1 all-gather.20
  80.0 33.1 all-gather.22
  114.5 22.0 all-gather.34
  138.5 33.1 all-gather.28
  173.1 33.1 all-gather.24
  208.3 54.3 all-gather.26
  264.9 44.5 all-gather.30
  311.6 115.3 all-gather.36
  428.4 136.1 all-gather.40
  566.7 142.6 all-gather.38
  725.1 154.2 all-gather.42
  888.0 86.8 all-gather.32

commit v4 on v3

--- a/solution.py
+++ b/solution.py
@@ -243,8 +243,11 @@
     )(*values, *earlier)
 
 
-def scatter_kernel(size, earlier, parts, *refs):
-    out, held, core_in, x_in, z_in, local, z_sent, z_here, x_sent, x_here, core_sent, core_here = refs[earlier:]
+def scatter_kernel(size, arrays, earlier, *refs):
+    parts = refs[:arrays]
+    outs, refs = refs[arrays + earlier : 2 * arrays + earlier], refs[2 * arrays + earlier :]
+    helds, core_ins, x_ins, z_ins = [refs[k * arrays : (k + 1) * arrays] for k in range(4)]
+    local, z_sent, z_here, x_sent, x_here, core_sent, core_here = refs[4 * arrays :]
     c, t = lax.axis_index("ctx"), lax.axis_index("tp")
     x_peer, core_peer = {"tp": t ^ 2}, {"tp": t ^ 1}
     first, last = c == 0, c == size - 1
@@ -252,41 +255,51 @@
     spot = [size - 1 - k + upper * (2 * k - size + 1) for k in range(size)]
     before, behind = {"ctx": lax.max(c - 1, 0)}, {"ctx": lax.min(c + 1, size - 1)}
     greet([x_peer, core_peer], ((jnp.logical_not(first), before), (jnp.logical_not(last), behind)))
-    keep = pltpu.make_async_copy(parts.at[pl.ds(0, 2)], held, local)
-    keep.start()
-    core = {
-        (m, k): remote(parts.at[2 + m, spot[k]], core_in.at[m, k], core_sent, core_here, m * size + k, core_peer)
-        for m in (1, 0)
-        for k in range(size)
-    }
-    x = [remote(held.at[1, spot[k]], x_in.at[k], x_sent, x_here, k, x_peer) for k in range(size)]
-    rising = [remote(held.at[0, spot[k]], z_in.at[0, spot[k]], z_sent, z_here, spot[k], behind) for k in range(size)]
-    falling = [
-        remote(held.at[0, spot[k]], z_in.at[1, spot[k]], z_sent, z_here, size + spot[k], before) for k in range(size)
-    ]
+    keeps, core, x, rising, falling, finals = [], {}, {}, {}, {}, {}
+    for n in range(arrays):
+        part, held, core_in, x_in, z_in = parts[n], helds[n], core_ins[n], x_ins[n], z_ins[n]
+        keeps.append(pltpu.make_async_copy(part.at[pl.ds(0, 2)], held, local.at[n]))
+        for m in (1, 0):
+            for k in range(size):
+                core[n, m, k] = remote(
+                    part.at[2 + m, spot[k]], core_in.at[m, k], core_sent, core_here, (n * 2 + m) * size + k, core_peer
+                )
+        for k in range(size):
+            a = spot[k]
+            x[n, k] = remote(held.at[1, a], x_in.at[k], x_sent, x_here, n * size + k, x_peer)
+            rising[n, k] = remote(held.at[0, a], z_in.at[0, a], z_sent, z_here, 2 * n * size + a, behind)
+            falling[n, k] = remote(held.at[0, a], z_in.at[1, a], z_sent, z_here, (2 * n + 1) * size + a, before)
+        finals[n] = [
+            remote(held.at[0, c], z_in.at[0, c], z_sent, z_here, 2 * n * size + c, behind),
+            remote(held.at[0, c], z_in.at[1, c], z_sent, z_here, (2 * n + 1) * size + c, before),
+        ]
     for copy in core.values():
         copy.start()
-    keep.wait()
+    for keep in keeps:
+        keep.start()
+    for keep in keeps:
+        keep.wait()
     tall = 16
 
     def each(body):
-        @pl.loop(0, out.shape[0] // tall)
+        @pl.loop(0, outs[0].shape[0] // tall)
         def _(i):
             body(pl.ds(pl.multiple_of(i * tall, tall), tall))
 
-    for k in range(size):
-        a = spot[k]
-        core[1, k].wait_recv()
+    order = [(n, k) for n in range(arrays) for k in range(size)]
+    for n, k in order:
+        a, held, core_in = spot[k], helds[n], core_ins[n]
+        core[n, 1, k].wait_recv()
 
         def add_core(rows):
             held[1, a, rows] = (held[1, a, rows].astype(F32) + core_in[1, k, rows].astype(F32)).astype(BF16)
 
         each(add_core)
-        x[k].start()
-    for k in range(size):
-        a = spot[k]
-        core[0, k].wait_recv()
-        x[k].wait_recv()
+        x[n, k].start()
+    for n, k in order:
+        a, held, core_in, x_in, z_in, out = spot[k], helds[n], core_ins[n], x_ins[n], z_ins[n], outs[n]
+        core[n, 0, k].wait_recv()
+        x[n, k].wait_recv()
 
         def total(rows):
             return held[0, a, rows].astype(F32) + core_in[0, k, rows].astype(F32) + x_in[k, rows].astype(F32)
@@ -315,10 +328,10 @@
 
             @pl.when(jnp.logical_not(first))
             def _():
-                rising[k].wait_recv()
+                rising[n, k].wait_recv()
                 each(add_rising)
 
-            rising[k].start()
+            rising[n, k].start()
 
         @pl.when(a < c)
         def _():
@@ -328,58 +341,57 @@
 
             @pl.when(jnp.logical_not(last))
             def _():
-                falling[k].wait_recv()
+                falling[n, k].wait_recv()
                 each(add_falling)
 
-            falling[k].start()
-
-    for side, edge in enumerate((first, last)):
-
-        @pl.when(jnp.logical_not(edge))
-        def _():
-            remote(
-                held.at[0, c], z_in.at[side, c], z_sent, z_here, side * size + c, before if side else behind
-            ).wait_recv()
-
-            def add_side(rows):
-                out[rows] = out[rows] + z_in[side, c, rows].astype(F32)
-
-            each(add_side)
-
-    for copy in list(core.values()) + x:
+            falling[n, k].start()
+
+    for n in range(arrays):
+        for side, edge in enumerate((first, last)):
+            z_in, out = z_ins[n], outs[n]
+
+            @pl.when(jnp.logical_not(edge))
+            def _():
+                finals[n][side].wait_recv()
+
+                def add_side(rows):
+                    out[rows] = out[rows] + z_in[side, c, rows].astype(F32)
+
+                each(add_side)
+
+    for copy in list(core.values()) + list(x.values()):
         copy.wait_send()
-    for k in range(size):
+    for n, k in order:
 
         @pl.when(spot[k] > c)
         def _():
-            rising[k].wait_send()
+            rising[n, k].wait_send()
 
         @pl.when(spot[k] < c)
         def _():
-            falling[k].wait_send()
+            falling[n, k].wait_send()
 
 
 def scatter_rows(parts, collective, *earlier):
-    size = lax.axis_size("ctx")
-    rows, width = parts.shape[2:]
+    size, arrays = lax.axis_size("ctx"), len(parts)
+    rows, width = parts[0].shape[2:]
     return pl.pallas_call(
-        functools.partial(scatter_kernel, size, len(earlier)),
-        out_shape=jax.ShapeDtypeStruct((rows, width), F32),
-        in_specs=[pl.BlockSpec(memory_space=pl.ANY)] * (1 + len(earlier)),
-        out_specs=pl.BlockSpec(memory_space=pltpu.VMEM),
-        scratch_shapes=[
-            pltpu.VMEM((2, size, rows, width), BF16),
-            pltpu.VMEM((2, size, rows, width), BF16),
-            pltpu.VMEM((size, rows, width), BF16),
-            pltpu.VMEM((2, size, rows, width), BF16),
-            pltpu.SemaphoreType.DMA(()),
-        ]
-        + [pltpu.SemaphoreType.DMA((n,)) for n in (2 * size, 2 * size, size, size, 2 * size, 2 * size)],
+        functools.partial(scatter_kernel, size, arrays, len(earlier)),
+        out_shape=[jax.ShapeDtypeStruct((rows, width), F32)] * arrays,
+        in_specs=[pl.BlockSpec(memory_space=pl.ANY)] * (arrays + len(earlier)),
+        out_specs=[pl.BlockSpec(memory_space=pltpu.VMEM)] * arrays,
+        scratch_shapes=[pltpu.VMEM((2, size, rows, width), BF16)] * (2 * arrays)
+        + [pltpu.VMEM((size, rows, width), BF16)] * arrays
+        + [pltpu.VMEM((2, size, rows, width), BF16)] * arrays
+        + [
+            pltpu.SemaphoreType.DMA((arrays * n,))
+            for n in (1, 2 * size, 2 * size, size, size, 2 * size, 2 * size)
+        ],
         compiler_params=pltpu.CompilerParams(
-            collective_id=collective, has_side_effects=True, vmem_limit_bytes=40 * 1024 * 1024
+            collective_id=collective, has_side_effects=True, vmem_limit_bytes=48 * 1024 * 1024
         ),
         name="scatter_rows",
-    )(parts, *earlier)
+    )(*parts, *earlier)
 
 
 def sum_tokens(values):
@@ -471,17 +483,286 @@
     return lax.rsqrt(jnp.mean(values * values, axis=-1, keepdims=True) + NORM_EPSILON)
 
 
-def turn(values, cosine, sine):
-    half = values.shape[-1] // 2
-    front, back = values[..., :half], values[..., half:]
-    return jnp.concatenate([front * cosine - back * sine, back * cosine + front * sine], axis=-1)
-
-
 def norm_back(grad, values, gain):
     scale = inverse_scale(values)
     weighted = grad * gain
     middle = jnp.mean(values * weighted, axis=-1, keepdims=True)
     return scale * weighted - values * (scale * scale * scale) * middle, grad * values * scale
+
+
+def weights_kernel(ctxs, group, pieces, index, inward, outward, entry, *refs):
+    exits, (first, others, head, leave) = refs[:ctxs], refs[ctxs:]
+    c = index[0]
+    tall = first.shape[0]
+    deep = 16
+    in_rows, out_rows = inward.shape[1], outward.shape[1]
+    out_experts = 8
+    half = lax.rem(c, out_experts // group) * group
+
+    def picker(rows, kept, place):
+        count = kept * deep
+        to = lax.broadcasted_iota(jnp.int32, (count, rows * deep), 0)
+        source = lax.broadcasted_iota(jnp.int32, (count, rows * deep), 1)
+        return (source == to % deep * rows + place(to // deep)).astype(BF16)
+
+    in_pick = picker(in_rows, in_rows, lambda row: row)
+    kept = group * pieces
+    out_pick = picker(out_rows, kept, lambda row: row // group * out_experts + half + row % group)
+
+    def put(i, column, rows, value):
+        if i:
+            column = column + (i - 1) * 3 * pieces * 128
+        (others if i else first)[rows, column : column + 128] = value
+
+    for step in range(tall // deep):
+        rows = slice(step * deep, (step + 1) * deep)
+        moved = matmul(in_pick, inward[rows].reshape(deep * in_rows, 128)).astype(BF16)
+        for row in range(in_rows):
+            i, piece, side = row // (2 * pieces), row // 2 % pieces, row % 2
+            put(i, (side * pieces + piece) * 128, rows, moved[row * deep : (row + 1) * deep])
+        moved = matmul(out_pick, outward[rows].reshape(deep * out_rows, 128)).astype(BF16)
+        for row in range(kept):
+            i, piece = row % group, row // group
+            put(i, (2 * pieces + piece) * 128, rows, moved[row * deep : (row + 1) * deep])
+    for k in range(3):
+        head[:, k * HEAD_DIM : (k + 1) * HEAD_DIM] = entry[k]
+    for j in range(ctxs):
+        leave[:, j * HEAD_DIM : (j + 1) * HEAD_DIM] = exits[j][...]
+
+
+def own_weights(expert_in, expert_out, attention_in, attention_out):
+    c, ctxs = lax.axis_index("ctx"), lax.axis_size("ctx")
+    rows, experts, _, hidden = expert_in.shape
+    group, pieces = experts // ctxs, hidden // 128
+    assert group in (1, 2, 4, 8) and group * 2 * pieces % 16 == 0 and 8 * pieces % 16 == 0
+    inward = expert_in.reshape(rows, experts, 2, pieces, 128).transpose(0, 1, 3, 2, 4).reshape(rows, -1, 128)
+    outward = expert_out.reshape(rows, experts // 8, 8, pieces, 128).transpose(0, 1, 3, 2, 4).reshape(rows, -1, 128)
+    entry = attention_in.transpose(1, 0, 2)
+    tall = 64
+    wide = 3 * hidden
+    grid_spec = pltpu.PrefetchScalarGridSpec(
+        num_scalar_prefetch=1,
+        grid=(rows // tall,),
+        in_specs=[
+            pl.BlockSpec((tall, group * 2 * pieces, 128), lambda b, c: (b, c[0], 0)),
+            pl.BlockSpec((tall, 8 * pieces, 128), lambda b, c: (b, c[0] * group // 8, 0)),
+            pl.BlockSpec((3, tall, HEAD_DIM), lambda b, c: (0, b, c[0])),
+        ]
+        + [
+            pl.BlockSpec((tall, HEAD_DIM), functools.partial(lambda j, b, c: (b, lax.rem(c[0] + j, ctxs)), j))
+            for j in range(ctxs)
+        ],
+        out_specs=[
+            pl.BlockSpec((tall, n), lambda b, c: (b, 0))
+            for n in (wide, (group - 1) * wide, 3 * HEAD_DIM, ctxs * HEAD_DIM)
+        ],
+    )
+    return pl.pallas_call(
+        functools.partial(weights_kernel, ctxs, group, pieces),
+        grid_spec=grid_spec,
+        out_shape=[
+            jax.ShapeDtypeStruct((rows, n), BF16)
+            for n in (wide, (group - 1) * wide, 3 * HEAD_DIM, ctxs * HEAD_DIM)
+        ],
+        compiler_params=pltpu.CompilerParams(vmem_limit_bytes=48 * 1024 * 1024),
+        name="own_weights",
+    )(c.astype(jnp.int32)[None], inward, outward, entry, *([attention_out] * ctxs))
+
+
+def matmul(left, right, over=(1, 0)):
+    return lax.dot_general(left, right, (((over[0],), (over[1],)), ((), ())), preferred_element_type=F32)
+
+
+def head_norm(values):
+    return lax.rsqrt(jnp.mean(values * values, axis=-1, keepdims=True) + NORM_EPSILON)
+
+
+def turned(values, cosine, sine):
+    return values * cosine + pltpu.roll(values, values.shape[-1] // 2, 1) * sine
+
+
+def project_kernel(tokens, gain, weight, gains, cosine, sine, normed, raw, query, key, value):
+    values = tokens[...].astype(F32)
+    low = (values * head_norm(values) * gain[...]).astype(BF16)
+    normed[...] = low
+    projected = matmul(low, weight[...])
+    raw[...] = projected[:, : 2 * HEAD_DIM]
+    for k, out in enumerate((query, key)):
+        part = projected[:, k * HEAD_DIM : (k + 1) * HEAD_DIM]
+        part = part * head_norm(part) * gains[k : k + 1, :]
+        out[...] = turned(part, cosine[...], sine[...]).astype(BF16)
+    value[...] = projected[:, 2 * HEAD_DIM :].astype(BF16)
+
+
+def project(tokens, gain, weight, gains, cosine, sine):
+    rows, width = tokens.shape
+    tall = 256
+    block = lambda n: pl.BlockSpec((tall, n), lambda b: (b, 0))
+    whole = lambda v: pl.BlockSpec(v.shape, lambda b: (0, 0))
+    head = jax.ShapeDtypeStruct((rows, HEAD_DIM), BF16)
+    return pl.pallas_call(
+        project_kernel,
+        grid=(rows // tall,),
+        in_specs=[block(width), whole(gain), whole(weight), whole(gains), block(HEAD_DIM), block(HEAD_DIM)],
+        out_specs=[block(width), block(2 * HEAD_DIM)] + [block(HEAD_DIM)] * 3,
+        out_shape=[
+            jax.ShapeDtypeStruct((rows, width), BF16),
+            jax.ShapeDtypeStruct((rows, 2 * HEAD_DIM), F32),
+            head,
+            head,
+            head,
+        ],
+        compiler_params=pltpu.CompilerParams(vmem_limit_bytes=48 * 1024 * 1024),
+        name="project",
+    )(tokens, gain, weight, gains, cosine, sine)
+
+
+def chances_of(query, key, row_doc, column_doc):
+    scores = matmul(query, key, (1, 1)) * (HEAD_DIM**-0.5)
+    scores = jnp.where(row_doc == column_doc, scores, MASKED)
+    grown = jnp.exp(scores - jnp.max(scores, axis=-1, keepdims=True))
+    return grown / jnp.sum(grown, axis=-1, keepdims=True)
+
+
+def attend_kernel(query, key, value, row_doc, column_doc, mixed):
+    chances = chances_of(query[...], key[...], row_doc[...], column_doc[...])
+    mixed[...] = matmul(chances.astype(BF16), value[...]).astype(BF16)
+
+
+def attend(query, key, value, row_doc, column_doc):
+    rows = query.shape[0]
+    tall = 256
+    block = pl.BlockSpec((tall, HEAD_DIM), lambda b: (b, 0))
+    whole = pl.BlockSpec((rows, HEAD_DIM), lambda b: (0, 0))
+    return pl.pallas_call(
+        attend_kernel,
+        grid=(rows // tall,),
+        in_specs=[
+            block,
+            whole,
+            whole,
+            pl.BlockSpec((tall, 1), lambda b: (b, 0)),
+            pl.BlockSpec((1, rows), lambda b: (0, 0)),
+        ],
+        out_specs=block,
+        out_shape=jax.ShapeDtypeStruct((rows, HEAD_DIM), BF16),
+        compiler_params=pltpu.CompilerParams(vmem_limit_bytes=48 * 1024 * 1024),
+        name="attend",
+    )(query, key, value, row_doc, column_doc)
+
+
+def attend_back_kernel(
+    tall, query, key, value, raw, cosine, sine, gains, row_doc, column_doc, mixed_grad, grad, gain_grad, key_grad, value_grad
+):
+    step = pl.program_id(0)
+    rows = pl.ds(pl.multiple_of(step * tall, tall), tall)
+
+    def projected_back(turned_grad, k, where):
+        values = raw[where, k * HEAD_DIM : (k + 1) * HEAD_DIM]
+        grown = turned(turned_grad, cosine[where], -sine[where])
+        scale = head_norm(values)
+        weighted = grown * gains[k : k + 1, :]
+        middle = jnp.mean(values * weighted, axis=-1, keepdims=True)
+        part = jnp.sum(grown * values * scale, axis=0, keepdims=True)
+        return scale * weighted - values * (scale * scale * scale) * middle, part
+
+    @pl.when(step == 0)
+    def _():
+        key_grad[...] = jnp.zeros_like(key_grad)
+        value_grad[...] = jnp.zeros_like(value_grad)
+        gain_grad[...] = jnp.zeros_like(gain_grad)
+
+    here = query[...]
+    chances = chances_of(here, key[...], row_doc[...], column_doc[...])
+    upstream = mixed_grad[...]
+    weight_grad = matmul(upstream, value[...], (1, 1))
+    score_grad = chances * (weight_grad - jnp.sum(chances * weight_grad, axis=-1, keepdims=True))
+    score_grad = score_grad.astype(BF16)
+    scale = HEAD_DIM**-0.5
+    query_grad, part = projected_back(matmul(score_grad, key[...]) * scale, 0, rows)
+    grad[rows, :HEAD_DIM] = query_grad.astype(BF16)
+    gain_grad[0:1, :] += part
+    key_grad[...] += matmul(score_grad, here, (0, 0)) * scale
+    value_grad[...] += matmul(chances.astype(BF16), upstream, (0, 0))
+
+    @pl.when(step == pl.num_programs(0) - 1)
+    def _():
+        back, part = projected_back(key_grad[...], 1, slice(None))
+        grad[:, HEAD_DIM : 2 * HEAD_DIM] = back.astype(BF16)
+        gain_grad[1:2, :] += part
+        grad[:, 2 * HEAD_DIM :] = value_grad[...].astype(BF16)
+
+
+def attend_back(query, key, value, raw, cosine, sine, gains, row_doc, column_doc, mixed_grad):
+    rows = query.shape[0]
+    tall = 256
+    block = pl.BlockSpec((tall, HEAD_DIM), lambda b: (b, 0))
+    whole = lambda v: pl.BlockSpec(v.shape, lambda b: (0, 0))
+    return pl.pallas_call(
+        functools.partial(attend_back_kernel, tall),
+        grid=(rows // tall,),
+        in_specs=[
+            block,
+            whole(key),
+            whole(value),
+            whole(raw),
+            whole(cosine),
+            whole(sine),
+            whole(gains),
+            pl.BlockSpec((tall, 1), lambda b: (b, 0)),
+            whole(column_doc),
+            block,
+        ],
+        out_specs=[
+            pl.BlockSpec((rows, 3 * HEAD_DIM), lambda b: (0, 0)),
+            pl.BlockSpec((8, HEAD_DIM), lambda b: (0, 0)),
+        ],
+        out_shape=[
+            jax.ShapeDtypeStruct((rows, 3 * HEAD_DIM), BF16),
+            jax.ShapeDtypeStruct((8, HEAD_DIM), F32),
+        ],
+        scratch_shapes=[pltpu.VMEM((rows, HEAD_DIM), F32)] * 2,
+        compiler_params=pltpu.CompilerParams(vmem_limit_bytes=48 * 1024 * 1024),
+        name="attend_back",
+    )(query, key, value, raw, cosine, sine, gains, row_doc, column_doc, mixed_grad)
+
+
+def expert_step_kernel(index, earlier, rows, upstream, gate_in, up_in, outward, gates, *refs):
+    scaled, inner_grad, gate_part = refs[earlier:]
+    hidden_size = outward.shape[1]
+    gate, up = matmul(rows[...], gate_in[...]), matmul(rows[...], up_in[...])
+    back = matmul(upstream[...], outward[...])
+    sigmoid = 1.0 / (1.0 + jnp.exp(-gate))
+    silu = gate * sigmoid
+    hidden = (silu * up).astype(BF16).astype(F32)
+    weight = gates[:, index : index + 1]
+    scaled[...] = (hidden * weight).astype(BF16)
+    lane = lax.broadcasted_iota(jnp.int32, gate_part.shape, 1)
+    gate_part[...] = jnp.where(lane == index, jnp.sum(hidden * back, axis=1, keepdims=True), 0.0)
+    hidden_grad = back * weight
+    inner_grad[:, :hidden_size] = (hidden_grad * up * sigmoid * (1.0 + gate * (1.0 - sigmoid))).astype(BF16)
+    inner_grad[:, hidden_size:] = (hidden_grad * silu).astype(BF16)
+
+
+def expert_step(index, place, rows, upstream, weights, hidden_size, gates, *earlier):
+    count, width = rows.shape
+    tall = 256
+    block = lambda n: pl.BlockSpec((tall, n), lambda b: (b, 0))
+    column = lambda k: pl.BlockSpec((width, hidden_size), lambda b: (0, 3 * place + k))
+    return pl.pallas_call(
+        functools.partial(expert_step_kernel, index, len(earlier)),
+        grid=(count // tall,),
+        in_specs=[block(width), block(width), column(0), column(1), column(2), block(gates.shape[1])]
+        + [pl.BlockSpec(memory_space=pl.ANY)] * len(earlier),
+        out_specs=[block(hidden_size), block(2 * hidden_size), block(128)],
+        out_shape=[
+            jax.ShapeDtypeStruct((count, hidden_size), BF16),
+            jax.ShapeDtypeStruct((count, 2 * hidden_size), BF16),
+            jax.ShapeDtypeStruct((count, 128), F32),
+        ],
+        compiler_params=pltpu.CompilerParams(vmem_limit_bytes=48 * 1024 * 1024),
+        name="expert_step",
+    )(rows, upstream, weights, weights, weights, gates, *earlier)
 
 
 def expert_kernel(group, tall, hidden, *refs):
@@ -583,7 +864,6 @@
     hidden_size = expert_out.shape[2]
     local_width = attention_out.shape[1]
     head_size = local_width // ctxs
-    heads = head_size // HEAD_DIM
 
     group = experts // ctxs
     base = c * group
@@ -591,25 +871,20 @@
     gains = gather_small(jnp.stack([first_gain, second_gain]), 1).astype(F32)
     gain_one, gain_two = gains[0], gains[1]
     head_gains = gather_small(head_gain[None], 1)[0].astype(F32)
-    head_in = lax.dynamic_slice_in_dim(attention_in, c * head_size, head_size, axis=2)
-    head_in = gather_natural(head_in.reshape(block, 3 * head_size), "shard")
-    exit_weight = gather_natural(ahead_first(attention_out, c * head_size, 1), "shard")
-
-    def expert_weights(start, count):
-        inward = lax.dynamic_slice_in_dim(expert_in, start, count, axis=1)
-        outward = lax.dynamic_slice_in_dim(expert_out, start, count, axis=1)
-        inward = [inward[:, i].reshape(block, 2 * hidden_size) for i in range(count)]
-        outward = outward.reshape(block, count * hidden_size)
-        return inward, outward
-
+    first_weights, others, head_in, exit_weight = own_weights(expert_in, expert_out, attention_in, attention_out)
+    tokens_all, cot_all = gather_rows([tokens[0], cotangent[0]], 3, head_in, shared=True)
+    tokens_all, cot_all = tokens_all.reshape(every, width), cot_all.reshape(every, width)
+    head_in = gather_natural(head_in, "shard")
+    first_weights, others = gather_natural(first_weights, "shard"), gather_natural(others, "shard")
+    exit_weight = gather_small(exit_weight, 0)
+    columns = lambda i, start, count: (others if i else first_weights)[
+        :, (3 * max(i - 1, 0) + start) * hidden_size : (3 * max(i - 1, 0) + start + count) * hidden_size
+    ]
+    in_weights = [columns(i, 0, 2) for i in range(group)]
+    out_weights = [columns(i, 2, 1) for i in range(group)]
     first = t * own
     tokens_own = lax.dynamic_slice_in_dim(tokens[0], first, own)
     cot_own = lax.dynamic_slice_in_dim(cotangent[0], first, own)
-    inward, outward = expert_weights(base, 1)
-    tokens_all, cot_all = gather_rows([tokens[0], cotangent[0]], 3, inward[0], outward, shared=True)
-    tokens_all, cot_all = tokens_all.reshape(every, width), cot_all.reshape(every, width)
-    in_weights = [gather_natural(inward[0], "shard")]
-    out_weights = [gather_natural(outward, "shard")]
 
     layer_in = tokens_own.astype(F32)
     upstream = cot_own.astype(F32)
@@ -619,34 +894,23 @@
     picks_all = picks_all.reshape(every, experts)
     router = gather_small(router_weight, 0)
 
-    tokens_wide = tokens_all.astype(F32)
-    normed_one_all = lower(tokens_wide * inverse_scale(tokens_wide) * gain_one)
+    assert head_size == HEAD_DIM
     spot = part_order(jnp.arange(every, dtype=jnp.int32).reshape(ctxs, tps, own)).reshape(-1)
     documents = part_order(segments[0].reshape(ctxs, tps, own)).reshape(-1)
+    row_doc, column_doc = documents[:, None], documents[None, :]
     steps = jnp.arange(HEAD_DIM // 2).astype(F32)
     frequency = ROTARY_BASE ** (-2.0 * steps / HEAD_DIM)
     angles = spot.astype(F32)[:, None] * frequency[None, :]
-    cosine, sine = jnp.cos(angles)[:, None], jnp.sin(angles)[:, None]
-    projected = dot(normed_one_all, head_in, (1, 0)).reshape(every, 3, heads, HEAD_DIM)
-    query_raw, key_raw = projected[:, 0], projected[:, 1]
-    gain_q, gain_k = head_gains[:HEAD_DIM], head_gains[HEAD_DIM:]
-    queries = lower(turn(query_raw * inverse_scale(query_raw) * gain_q, cosine, sine))
-    keys = lower(turn(key_raw * inverse_scale(key_raw) * gain_k, cosine, sine))
-    values = lower(projected[:, 2])
-    scale = HEAD_DIM ** (-0.5)
-    scores = jnp.einsum("qhd,khd->hqk", queries, keys, preferred_element_type=F32) * scale
-    same = documents[:, None] == documents[None, :]
-    chances = jax.nn.softmax(jnp.where(same[None], scores, MASKED), axis=-1)
-    chances_low = lower(chances)
-    mixed_head = lower(jnp.einsum("hqk,khd->qhd", chances_low, values, preferred_element_type=F32))
+    cosine, sine = jnp.cos(angles), jnp.sin(angles)
+    cosine, sine = jnp.concatenate([cosine, cosine], axis=1), jnp.concatenate([-sine, sine], axis=1)
+    head_gains = head_gains.reshape(2, HEAD_DIM)
+    normed_one_all, raw, queries, keys, values = project(
+        tokens_all, gain_one[None], head_in, head_gains, cosine, sine
+    )
+    mixed_head = attend(queries, keys, values, row_doc, column_doc)
     blocks = ahead_first(mixed_head.reshape(tps, ctxs, own, head_size), c, 1)
     mixed = [blocks[:, 0]] + [receive(blocks[:, ctxs - j], "ctx", j) for j in range(1, ctxs)]
     mixed = jnp.concatenate([m.reshape(rows, head_size) for m in mixed], axis=1)
-    inward, outward = expert_weights(base + 1 + start_after(mixed), group - 1)
-    in_weights.append(gather_natural(inward[0], "shard"))
-    outward = gather_natural(outward, "shard")
-    out_weights += [outward[:, i * hidden_size : (i + 1) * hidden_size] for i in range(group - 1)]
-    in_weights += [gather_natural(inward[i], "shard") for i in range(1, group - 1)]
     residual = layer_in + scatter_tp(dot(mixed, exit_weight, (1, 1)))
 
     normed_two = lower(residual * inverse_scale(residual) * gain_two)
@@ -658,45 +922,32 @@
     cot_blocks = [own_block(cot_all, r, 1) for r in range(shards)]
     scaled, gate_parts, inner_grads, products, chunks, gathered = [], [], [], [], [], []
 
-    def finish(i):
+    def finish(i, later):
         own_part, others = products[i]
-        chunks.append(lower(product_sum(tie(own_part, products[-1][1][0]), others)))
+        chunks.append(lower(product_sum(tie(own_part, later), others)))
         chunk = chunks[i] if i < 2 else tie(chunks[i], gathered[i - 2])
         gathered.append(lax.all_gather(chunk, "ctx", axis=0, tiled=False))
 
     for i in range(group):
-        gate_up = dot(normed_two_all, in_weights[i], (1, 0))
-        gate, up = gate_up[:, :hidden_size], gate_up[:, hidden_size:]
-        back = dot(cot_all, out_weights[i], (1, 0))
-        sigmoid = jax.nn.sigmoid(gate)
-        silu = gate * sigmoid
-        hidden = lower(silu * up).astype(F32)
-        weight = gates[:, i : i + 1]
-        if i >= 2:
-            weight = tie(weight, chunks[max(i - 3, 0)])
-        scaled.append(lower(hidden * weight))
-        gate_parts.append(jnp.sum(hidden * back, axis=1))
-        hidden_grad = back * weight
-        inner_grads.append(
-            lower(
-                jnp.concatenate(
-                    [hidden_grad * up * sigmoid * (1.0 + gate * (1.0 - sigmoid)), hidden_grad * silu], axis=1
-                )
-            )
+        before = [] if i == 0 else list(products[i - 1][1])
+        step = expert_step(
+            i, max(i - 1, 0), normed_two_all, cot_all, others if i else first_weights, hidden_size, gates, *before
         )
+        scaled.append(step[0])
+        inner_grads.append(step[1])
+        gate_parts.append(step[2])
         products.append(product_parts([(normed_blocks, inner_grads[i]), (cot_blocks, scaled[i])]))
-        if i != 1:
-            finish(max(i - 1, 0))
-    finish(group - 1)
-
+    early = min(2, group)
+    for i in range(early):
+        finish(i, products[min(2 * i + 1, group - 1)][1][0])
     normed_part = sum(dot(inner_grads[i], in_weights[i], (1, 1)) for i in range(group))
     gate_part = lax.dynamic_update_slice(
-        jnp.zeros((every, 128), F32), jnp.stack(gate_parts, axis=1), (0, base)
+        jnp.zeros((every, 128), F32), sum(gate_parts)[:, :group], (0, base)
     )
     normed_part = lower(jnp.concatenate([normed_part, gate_part], axis=1))
-    normed_sum = scatter_rows(normed_part.reshape(tps, ctxs, own, -1), 1, chunks[-2])
-    result_part = lower(sum(dot(scaled[i], out_weights[i], (1, 1)) for i in range(group)))
-    result_sum = scatter_rows(result_part.reshape(tps, ctxs, own, width), 2, normed_sum)
+    (normed_sum,) = scatter_rows([normed_part.reshape(tps, ctxs, own, -1)], 1, *chunks)
+    for i in range(early, group):
+        finish(i, normed_sum)
     normed_sum, gate_grad = normed_sum[:, :width], normed_sum[:, width : width + experts]
 
     router_chances = jax.nn.softmax(dot(normed_two, router, (1, 0)), axis=-1)
@@ -719,30 +970,26 @@
     mixed_grad = lower(dot(attend_grad, exit_weight, (1, 0))).reshape(tps, own, ctxs, head_size)
     parts = [mixed_grad[:, :, 0]] + [receive(mixed_grad[:, :, ctxs - j], "ctx", j) for j in range(1, ctxs)]
     mixed_grad = ahead_first(jnp.stack(parts, axis=1), lax.rem(ctxs - c, ctxs), 1)
-    mixed_grad = mixed_grad.reshape(every, heads, HEAD_DIM)
-    weight_grad = jnp.einsum("qhd,khd->hqk", mixed_grad, values, preferred_element_type=F32)
-    score_grad = lower(chances * (weight_grad - jnp.sum(chances * weight_grad, axis=-1, keepdims=True)))
-    query_grad = jnp.einsum("hqk,khd->qhd", score_grad, keys, preferred_element_type=F32) * scale
-    key_grad = jnp.einsum("hqk,qhd->khd", score_grad, queries, preferred_element_type=F32) * scale
-    value_grad = jnp.einsum("hqk,qhd->khd", chances_low, mixed_grad, preferred_element_type=F32)
-    query_raw_grad, gain_q_part = norm_back(turn(query_grad, cosine, -sine), query_raw, gain_q)
-    key_raw_grad, gain_k_part = norm_back(turn(key_grad, cosine, -sine), key_raw, gain_k)
-    projected_grad = lower(
-        jnp.stack([query_raw_grad, key_raw_grad, value_grad], axis=1).reshape(every, 3 * head_size)
+    mixed_grad = mixed_grad.reshape(every, HEAD_DIM)
+    projected_grad, gain_part = attend_back(
+        queries, keys, values, raw, cosine, sine, head_gains, row_doc, column_doc, mixed_grad
     )
     entry_blocks = [own_block(normed_one_all, r, 1) for r in range(shards)]
     entry_head = product_sum(*product_parts([(entry_blocks, projected_grad)]))
-    attention_chunk = tie(lower(jnp.concatenate([entry_head, exit_head], axis=1)), gathered[-2])
-    attention_chunk = lax.all_gather(attention_chunk, "ctx", axis=0, tiled=False)
+    attention_chunk = lower(jnp.concatenate([entry_head, exit_head], axis=1))
+    attention_gathered = lax.all_gather(tie(attention_chunk, gathered[-2]), "ctx", axis=0, tiled=False)
+
+    result_part = lower(sum(dot(tie(scaled[i], projected_grad), out_weights[i], (1, 1)) for i in range(group)))
     first_part = dot(projected_grad, head_in, (1, 1), BF16)
-    first_normed_grad = scatter_rows(first_part.reshape(tps, ctxs, own, width), 4, chunks[-1])
-
+    first_normed_grad, result_sum = scatter_rows(
+        [part.reshape(tps, ctxs, own, width) for part in (first_part, result_part)], 2, attention_chunk
+    )
     layer_output = natural_rows(gather_tp(lower(residual + result_sum)))[None]
 
     input_back, first_part = norm_back(first_normed_grad, layer_in, gain_one)
     input_gradient = natural_rows(gather_tp(lower(residual_grad + input_back))).astype(F32)[None]
 
-    head_part = jnp.concatenate([jnp.sum(gain_q_part, axis=(0, 1)), jnp.sum(gain_k_part, axis=(0, 1))])
+    head_part = gain_part[:2].reshape(-1)
     small_part = jnp.concatenate(
         [jnp.sum(second_part, axis=0)[None], jnp.sum(first_part, axis=0)[None], router_part], axis=0
     )
@@ -752,7 +999,7 @@
     small_sum = sum_shard(small_sum[:-1], 1)
 
     upward_gradient, downward_gradient = expert_gradients(gathered)
-    entry_gradient, exit_gradient = attention_gradients(attention_chunk)
+    entry_gradient, exit_gradient = attention_gradients(attention_gathered)
     return (
         layer_output,
         input_gradient,

time: 1020 us -> 950 us (0.931)
  Pallas kernels: 404 us -> 459 us
  matrix products: 214 us -> 166 us
  local copies, waits for them, and re-layouts: 73.5 us -> 46.7 us
  waiting for transfers between devices: 174 us -> 150 us
  other arithmetic: 72.8 us -> 50.2 us
    pallas_call x3 -> x10, Pallas kernels: 238 us -> 294 us  [the longest x2 208 us: scatter_rows(): pl.pallas_call(functools.partial(scatter_kernel, size, arrays, len(earlie...]
    ppermute x26 -> x27, waiting for transfers between devices: 141 us -> 95.6 us  [receive(): lax.ppermute(values, axis, [((i + distance) % size, i) for i in range(siz...]
    dot_general x44 -> x35, matrix products: 199 us -> 166 us  [dot(): lax.dot_general(left, right, (((over[0],), (over[1],)), ((), ())), prefer...]
    convert_element_type x8 -> x6, other arithmetic: 28.9 us -> 9.74 us  [lower(): return values.astype(BF16)]
    all_gather x1, waiting for transfers between devices: 0.01 us -> 18.3 us  [local(): lax.all_gather(tie(attention_chunk, gathered[-2]), 'ctx', axis=0, tiled=F...]
    dot_general x6 -> x0, matrix products: 14.4 us -> none  [the longest x1 6.06 us: local(): jnp.einsum('qhd,khd->hqk', mixed_grad, values, preferred_element_type=F32)]
    dynamic_slice x4 -> x0, local copies, waits for them, and re-layouts: 11.3 us -> none  [the longest x2 8.35 us: expert_weights(): outward = lax.dynamic_slice_in_dim(expert_out, start, count, axis=1)]
    ppermute x10, waiting for transfers between devices: 32.7 us -> 21.9 us  [swap(): return lax.ppermute(values, axis, [(i, i ^ bit) for i in range(size)])]
  transfers between devices with their start and end apart: 49 -> 45, of which waited for: 18 -> 19; matrix products, arithmetic and copies ran while one was open for 33% -> 26% of each run, Pallas kernels for 39% -> 46%
where the time goes in v4:
time: 950 us; the launch traced here: 942 us
  Pallas kernels  459 us (48%)
  matrix products  166 us (17%)
  waiting for transfers between devices  150 us (16%)
  other arithmetic  50.2 us (5%)
  starting transfers between devices  49.3 us (5%)
  local copies, waits for them, and re-layouts  46.7 us (5%)
  between operations  21.3 us (2%)
    pallas_call x2, Pallas kernels, scatter_rows(): pl.pallas_call(functools.partial(scatter_kernel, size, arrays, len(earlie...  208 us
    dot_general x35, matrix products, dot(): lax.dot_general(left, right, (((over[0],), (over[1],)), ((), ())), prefer...  166 us
    pallas_call x2, Pallas kernels, gather_rows(): pl.pallas_call(functools.partial(gather_kernel, size, pieces, arrays, sha...  103 us
    ppermute x27, waiting for transfers between devices, receive(): lax.ppermute(values, axis, [((i + distance) % size, i) for i in range(siz...  95.6 us
    pallas_call x1, Pallas kernels, expert_gradients(): pl.pallas_call(functools.partial(expert_kernel, group, tall, hidden), gri...  54.6 us
    pallas_call x4, Pallas kernels, expert_step(): pl.pallas_call(functools.partial(expert_step_kernel, index, len(earlier))...  42.4 us
    ppermute x27, starting transfers between devices, receive(): lax.ppermute(values, axis, [((i + distance) % size, i) for i in range(siz...  41.9 us
    unnamed x241, local copies, waits for them, and re-layouts  28.6 us
  transfers between devices with their start and end apart: 45, of which 19 were waited for; matrix products, arithmetic and copies ran while one was open for 26% of the time, Pallas kernels for 46%

profile of v4, /device:TPU:0, one launch (start us, length us, event | category | flops | bytes accessed | tf_op | source)
XLA Modules:
  0.0 942.2 jit_solution(15452078002948323229)
XLA Ops:
  8.5 14.1 %own_weights.1 = (bf16[1024,768]{1,0:T(8,128)(2,1)}, bf16[1024,2304]{1,0:T(8,128)(2,1)}, bf16[1024,384]{1,0:T(8,128)(2,1)}, bf16[1024,512]{1,0:T(8,128)(2,1)S(1)}) custom-call(s32[1]{0:T(128)} %bitcast.3.index, bf16[1024,64,128]{2,1,0:T(8,128)(2,1)} %bitcast.240, bf16[1024,32,128]{2,1,0:T(8,128)(2,1)} %bitcast.241, bf16[3,1024,512]{2,1,0:T(8,128)(2,1)} %bitcast.246, ...), custom_call_target="tpu_custom_call" | custom-call | tf_op jit(solution)/shard_map/own_weights/pallas_call | solution.py:560
  37.0 64.1 %gather_rows.2 = (bf16[4,4,96,2048]{3,2,1,0:T(8,128)(2,1)}, bf16[4,4,96,2048]{3,2,1,0:T(8,128)(2,1)}) custom-call(bf16[384,2048]{1,0:T(8,128)(2,1)} %bitcast.245, bf16[384,2048]{1,0:T(8,128)(2,1)} %bitcast.248, bf16[1024,384]{1,0:T(8,128)(2,1)} %get-tuple-element.41.refs_2_), custom_call_target="tpu_custom_call" | custom-call | tf_op jit(solution)/shard_map/gather_rows/pallas_call | solution.py:231
  115.0 9.9 %project.1 = (bf16[1536,2048]{1,0:T(8,128)(2,1)}, f32[1536,256]{1,0:T(8,128)S(1)}, bf16[1536,128]{1,0:T(8,128)(2,1)S(1)}, bf16[1536,128]{1,0:T(8,128)(2,1)S(1)}, bf16[1536,128]{1,0:T(8,128)(2,1)S(1)}) custom-call(bf16[1536,2048]{1,0:T(8,128)(2,1)} %bitcast.242, f32[1,2048]{1,0:T(1,128)S(1)} %get-tuple-element.111.gain, bf16[2048,384]{1,0:T(8,128)(2,1)S(1)} %copy-done.21, ...), custom_call_target="tpu_custom_call" | custom-call | tf_op jit(solution)/shard_map/project/pallas_call | solution.py:603
  153.8 8.3 collective-permute-done.7
  165.5 39.0 %gather_rows.3 = bf16[4,4,96,2048]{3,2,1,0:T(8,128)(2,1)} custom-call(bf16[96,2048]{1,0:T(8,128)(2,1)} %multiply_convert_fusion.refs_0_), custom_call_target="tpu_custom_call" | custom-call | tf_op jit(solution)/shard_map/gather_rows/pallas_call | solution.py:231
  210.5 10.3 %expert_step.4 = (bf16[1536,256]{1,0:T(8,128)(2,1)S(1)}, bf16[1536,512]{1,0:T(8,128)(2,1)S(1)}, f32[1536,128]{1,0:T(8,128)S(1)}) custom-call(bf16[1536,2048]{1,0:T(8,128)(2,1)} %bitcast.206, bf16[1536,2048]{1,0:T(8,128)(2,1)} %bitcast.224, bf16[2048,768]{1,0:T(8,128)(2,1)} %all-gather.15.cloned.1.call-done.gate_in.up_in.outward, ...), custom_call_target="tpu_custom_call" | custom-call | tf_op jit(solution)/shard_map/expert_step/pallas_call | solution.py:752
  243.3 10.3 %expert_step.5 = (bf16[1536,256]{1,0:T(8,128)(2,1)S(1)}, bf16[1536,512]{1,0:T(8,128)(2,1)S(1)}, f32[1536,128]{1,0:T(8,128)S(1)}) custom-call(bf16[1536,2048]{1,0:T(8,128)(2,1)} %bitcast.209, bf16[1536,2048]{1,0:T(8,128)(2,1)} %bitcast.227, bf16[2048,2304]{1,0:T(8,128)(2,1)} %all-gather.17.cloned.1.call-done.gate_in.up_in.outward, ...), custom_call_target="tpu_custom_call" | custom-call | tf_op jit(solution)/shard_map/expert_step/pallas_call | solution.py:752
  259.7 11.5 %collective-permute-done.12 = bf16[1024,768]{1,0:T(8,128)(2,1)} collective-permute-done((bf16[1024,768]{1,0:T(8,128)(2,1)S(1)}, bf16[1024,768]{1,0:T(8,128)(2,1)}, u32[]{:S(2)}, u32[]{:S(2)}) %collective-permute-start.12) | collective-permute-done | bytes 1572896 | tf_op jit(solution)/shard_map/ppermute | solution.py:29
  278.1 11.2 %expert_step.6 = (bf16[1536,256]{1,0:T(8,128)(2,1)S(1)}, bf16[1536,512]{1,0:T(8,128)(2,1)S(1)}, f32[1536,128]{1,0:T(8,128)S(1)}) custom-call(bf16[1536,2048]{1,0:T(8,128)(2,1)} %bitcast.211, bf16[1536,2048]{1,0:T(8,128)(2,1)} %bitcast.229, bf16[2048,2304]{1,0:T(8,128)(2,1)} %all-gather.17.cloned.1.call-done.gate_in.up_in.outward, ...), custom_call_target="tpu_custom_call" | custom-call | tf_op jit(solution)/shard_map/expert_step/pallas_call | solution.py:752
  294.3 10.6 %expert_step.7 = (bf16[1536,256]{1,0:T(8,128)(2,1)S(1)}, bf16[1536,512]{1,0:T(8,128)(2,1)S(1)}, f32[1536,128]{1,0:T(8,128)S(1)}) custom-call(bf16[1536,2048]{1,0:T(8,128)(2,1)} %bitcast.212, bf16[1536,2048]{1,0:T(8,128)(2,1)} %bitcast.231, bf16[2048,2304]{1,0:T(8,128)(2,1)} %all-gather.17.cloned.1.call-done.gate_in.up_in.outward, ...), custom_call_target="tpu_custom_call" | custom-call | tf_op jit(solution)/shard_map/expert_step/pallas_call | solution.py:752
  317.6 10.4 %fusion.20 = f32[1536,2048]{1,0:T(8,128)} fusion(bf16[1536,512]{1,0:T(8,128)(2,1)} %copy-done.44, bf16[2048,768]{1,0:T(8,128)(2,1)} %all-gather.15.cloned.1.call-done.gate_in.up_in.outward), kind=kOutput, calls=%fused_computation.32 | convolution fusion | flops 3221225472 | bytes 16252928 | tf_op jit(solution)/shard_map/dot_general | solution.py:23
  328.4 8.3 fusion.16
  344.8 18.0 %add_convert_fusion.1 = bf16[1536,2048]{1,0:T(8,128)(2,1)} fusion(f32[1536,2048]{1,0:T(8,128)} %fusion.16, f32[1536,2048]{1,0:T(8,128)} %fusion.20, f32[1536,2048]{1,0:T(8,128)} %fusion.18, bf16[1536,512]{1,0:T(8,128)(2,1)} %copy-done.12, bf16[2048,2304]{1,0:T(8,128)(2,1)} %all-gather.17.cloned.1.call-done.gate_in.up_in.outward), kind=kOutput, calls=%fused_computation.1 | convolution fusion | flops 3233808384 | bytes 47710208 | tf_op jit(solution)/shard_map/dot_general | solution.py:23
  381.9 90.0 %scatter_rows.2 = f32[96,2176]{1,0:T(8,128)S(1)} custom-call(bf16[4,4,96,2176]{3,2,1,0:T(8,128)(2,1)} %pad_maximum_fusion.refs_0_, bf16[1024,768]{1,0:T(8,128)(2,1)S(1)} %copy-done.2, bf16[1024,768]{1,0:T(8,128)(2,1)S(1)} %copy-done.1), custom_call_target="tpu_custom_call" | custom-call | tf_op jit(solution)/shard_map/scatter_rows/pallas_call | solution.py:378
  514.0 11.8 %collective-permute-done.17 = bf16[4,96,128]{2,1,0:T(8,128)(2,1)S(1)} collective-permute-done((bf16[4,96,128]{2,1,0:T(8,128)(2,1)S(1)}, bf16[4,96,128]{2,1,0:T(8,128)(2,1)S(1)}, u32[]{:S(2)}, u32[]{:S(2)}) %collective-permute-start.17) | collective-permute-done | bytes 98336 | tf_op jit(solution)/shard_map/ppermute | solution.py:29
  544.7 13.0 %attend_back.1 = (bf16[1536,384]{1,0:T(8,128)(2,1)S(1)}, f32[8,128]{1,0:T(8,128)S(1)}) custom-call(bf16[1536,128]{1,0:T(8,128)(2,1)S(1)} %copy-done.16, bf16[1536,128]{1,0:T(8,128)(2,1)S(1)} %copy-done.18, bf16[1536,128]{1,0:T(8,128)(2,1)S(1)} %copy-done.20, f32[1536,256]{1,0:T(8,128)} %copy-done.14, f32[1536,128]{1,0:T(8,128)S(1)} %copy-done.4, ...), custom_call_target="tpu_custom_call" | custom-call | tf_op jit(solution)/shard_map/attend_back/pallas_call | solution.py:701
  588.7 15.1 %add_convert_fusion = bf16[1536,2048]{1,0:T(8,128)(2,1)} fusion(f32[1536,2048]{1,0:T(8,128)} %fusion.84, f32[1536,2048]{1,0:T(8,128)} %fusion.88, f32[1536,2048]{1,0:T(8,128)} %fusion.86, bf16[2048,2304]{1,0:T(8,128)(2,1)} %all-gather.17.cloned.1.call-done.gate_in.up_in.outward, bf16[1536,256]{1,0:T(8,128)(2,1)S(1)} %copy-done.37, bf16[]{:T(256)} %bitcast.54), kind=kOutput, calls=%fused_computation | convolution fusion | flops 1623588864 | bytes 45875712 | tf_op jit(solution)/shard_map/dot_general | solution.py:23
  621.4 11.0 %collective-permute-done.23 = bf16[1024,128]{1,0:T(8,128)(2,1)S(1)} collective-permute-done((bf16[1024,128]{1,0:T(8,128)(2,1)S(1)}, bf16[1024,128]{1,0:T(8,128)(2,1)S(1)}, u32[]{:S(2)}, u32[]{:S(2)}) %collective-permute-start.23) | collective-permute-done | bytes 262176 | tf_op jit(solution)/shard_map/ppermute | solution.py:29
  632.4 34.4 %collective-permute-done.22 = bf16[1024,128]{1,0:T(8,128)(2,1)S(1)} collective-permute-done((bf16[1024,128]{1,0:T(8,128)(2,1)S(1)}, bf16[1024,128]{1,0:T(8,128)(2,1)S(1)}, u32[]{:S(2)}, u32[]{:S(2)}) %collective-permute-start.22) | collective-permute-done | bytes 262176 | tf_op jit(solution)/shard_map/ppermute | solution.py:29
  667.1 118.1 %scatter_rows.3 = (f32[96,2048]{1,0:T(8,128)S(1)}, f32[96,2048]{1,0:T(8,128)S(1)}) custom-call(bf16[4,4,96,2048]{3,2,1,0:T(8,128)(2,1)} %bitcast.244, bf16[4,4,96,2048]{3,2,1,0:T(8,128)(2,1)} %bitcast.236, bf16[1024,512]{1,0:T(8,128)(2,1)S(1)} %pad_maximum_fusion.8.refs_2_), custom_call_target="tpu_custom_call" | custom-call | tf_op jit(solution)/shard_map/scatter_rows/pallas_call | solution.py:378
  790.3 9.7 %collective-permute-done.29 = f32[19,2048]{1,0:T(8,128)S(1)} collective-permute-done((f32[19,2048]{1,0:T(8,128)S(1)}, f32[19,2048]{1,0:T(8,128)S(1)}, u32[]{:S(2)}, u32[]{:S(2)}) %collective-permute-start.29) | collective-permute-done | bytes 155680 | tf_op jit(solution)/shard_map/ppermute | solution.py:34
  813.3 16.3 %collective-permute-done.31 = f32[19,2048]{1,0:T(8,128)S(1)} collective-permute-done((f32[19,2048]{1,0:T(8,128)S(1)}, f32[19,2048]{1,0:T(8,128)S(1)}, u32[]{:S(2)}, u32[]{:S(2)}) %collective-permute-start.31) | collective-permute-done | bytes 155680 | tf_op jit(solution)/shard_map/ppermute | solution.py:29
  854.5 54.6 %expert_gradients.1 = (f32[1024,64,128]{2,1,0:T(8,128)}, f32[1024,32,128]{2,1,0:T(8,128)}) custom-call(bf16[4,1024,768]{2,1,0:T(8,128)(2,1)S(1)} %bitcast.194, bf16[4,1024,768]{2,1,0:T(8,128)(2,1)S(1)} %bitcast.196, bf16[4,1024,768]{2,1,0:T(8,128)(2,1)S(1)} %bitcast.198, bf16[4,1024,768]{2,1,0:T(8,128)(2,1)} %bitcast.243), custom_call_target="tpu_custom_call" | custom-call | tf_op jit(solution)/shard_map/expert_gradients/pallas_call | solution.py:795
  909.1 18.3 %all-gather.19.cloned.1.call-done.chunk = bf16[4,1024,512]{2,1,0:T(8,128)(2,1)} async-done(((bf16[1,1024,512]{2,1,0:T(8,128)(2,1)}), bf16[4,1024,512]{2,1,0:T(8,128)(2,1)}) %all-gather.19.cloned.1.call-update) | async-done | bytes 4194320 | tf_op jit(solution)/shard_map/all_gather | solution.py:980
  (473 shorter events, 302.7 us)
Async XLA Ops:
  7.2 106.5 %all-gather.13.cloned.1.call-start = ((), (), s32[]{:S(2)}) async-start(), calls=%async_computation | async-start | bytes 2359296 | tf_op jit(solution)/shard_map/all_gather | solution.py:443
  22.5 188.0 %all-gather.15.cloned.1.call-start = ((), (), s32[]{:S(2)}) async-start(), calls=%async_computation.1 | async-start | bytes 4718592 | tf_op jit(solution)/shard_map/all_gather | solution.py:443
  23.3 220.0 %all-gather.17.cloned.1.call-start = ((), (), s32[]{:S(2)}) async-start(), calls=%async_computation.2 | async-start | bytes 14155776 | tf_op jit(solution)/shard_map/all_gather | solution.py:443
  23.3 86.1 %collective-permute-start.8 = (s32[384,8]{0,1:T(8,128)S(1)}, s32[384,8]{0,1:T(8,128)S(1)}, u32[]{:S(2)}, u32[]{:S(2)}) collective-permute-start(s32[384,8]{0,1:T(8,128)S(1)} %bitcast.276), channel_id=1, source_target_pairs={{4,0},{8,4},{12,8},{0,12},{5,1},{9,5},{13,9},{1,13},{6,2},{10,6},{... | collective-permute-start | bytes 36872 | tf_op jit(solution)/shard_map/ppermute | solution.py:29
  28.4 81.6 %collective-permute-start.9 = (s32[384,8]{0,1:T(8,128)S(1)}, s32[384,8]{0,1:T(8,128)S(1)}, u32[]{:S(2)}, u32[]{:S(2)}) collective-permute-start(s32[384,8]{0,1:T(8,128)S(1)} %bitcast.277), channel_id=1, source_target_pairs={{8,0},{12,4},{0,8},{4,12},{9,1},{13,5},{1,9},{5,13},{10,2},{14,6},... | collective-permute-start | bytes 36872 | tf_op jit(solution)/shard_map/ppermute | solution.py:29
  28.5 82.2 %collective-permute-start.10 = (s32[384,8]{0,1:T(8,128)S(1)}, s32[384,8]{0,1:T(8,128)S(1)}, u32[]{:S(2)}, u32[]{:S(2)}) collective-permute-start(s32[384,8]{0,1:T(8,128)S(1)} %bitcast.278), channel_id=1, source_target_pairs={{12,0},{0,4},{4,8},{8,12},{13,1},{1,5},{5,9},{9,13},{14,2},{2,6},{... | collective-permute-start | bytes 36872 | tf_op jit(solution)/shard_map/ppermute | solution.py:29
  29.5 108.2 %collective-permute-start.5 = (bf16[1024,512]{1,0:T(8,128)(2,1)S(1)}, bf16[1024,512]{1,0:T(8,128)(2,1)}, u32[]{:S(2)}, u32[]{:S(2)}) collective-permute-start(bf16[1024,512]{1,0:T(8,128)(2,1)S(1)} %get-tuple-element.46), channel_id=1, source_target_pairs={{16,0},{0,16},{17,1},{1,17},{18,2},{2,18},{19,3},{3,19},{20,4},{4,... | collective-permute-start | bytes 3145736 | tf_op jit(solution)/shard_map/ppermute | solution.py:29
  31.0 72.9 %collective-permute-start.1 = (bf16[1,128]{1,0:T(2,128)(2,1)S(1)}, bf16[1,128]{1,0:T(2,128)(2,1)S(1)}, u32[]{:S(2)}, u32[]{:S(2)}) collective-permute-start(bf16[1,128]{1,0:T(2,128)(2,1)S(1)} %bitcast.291), channel_id=1, source_target_pairs={{16,0},{0,16},{17,1},{1,17},{18,2},{2,18},{19,3},{3,19},{20,4},{4,... | collective-permute-start | bytes 776 | tf_op jit(solution)/shard_map/ppermute | solution.py:29
  31.5 441.5 %all-gather.21.cloned.1.call-start = ((), (), s32[]{:S(2)}) async-start(), calls=%async_computation.4 | async-start | bytes 7864320 | tf_op jit(solution)/shard_map/all_gather | solution.py:929
  107.7 45.2 %collective-permute-start.11 = (bf16[1024,16]{0,1:T(8,128)(2,1)S(1)}, bf16[1024,16]{0,1:T(8,128)(2,1)}, u32[]{:S(2)}, u32[]{:S(2)}) collective-permute-start(bf16[1024,16]{0,1:T(8,128)(2,1)S(1)} %copy-done.94), channel_id=1, source_target_pairs={{16,0},{0,16},{17,1},{1,17},{18,2},{2,18},{19,3},{3,19},{20,4},{4,... | collective-permute-start | bytes 98312 | tf_op jit(solution)/shard_map/ppermute | solution.py:29
  228.7 42.5 %collective-permute-start.12 = (bf16[1024,768]{1,0:T(8,128)(2,1)S(1)}, bf16[1024,768]{1,0:T(8,128)(2,1)}, u32[]{:S(2)}, u32[]{:S(2)}) collective-permute-start(bf16[1024,768]{1,0:T(8,128)(2,1)S(1)} %pad_maximum_fusion.1.refs_0_), channel_id=1, source_target_pairs={{16,0},{0,16},{17,1},{1,17},{18,2},{2,18},{19,3},{3,19},{20,4},{4,... | collective-permute-start | bytes 4718600 | tf_op jit(solution)/shard_map/ppermute | solution.py:29
  274.3 258.2 %all-gather.25.cloned.1.call-start = ((), (), s32[]{:S(2)}) async-start(), calls=%async_computation.6 | async-start | bytes 7864320 | tf_op jit(solution)/shard_map/all_gather | solution.py:929
  277.7 36.4 %collective-permute-start.13 = (bf16[1024,768]{1,0:T(8,128)(2,1)S(1)}, bf16[1024,768]{1,0:T(8,128)(2,1)}, u32[]{:S(2)}, u32[]{:S(2)}) collective-permute-start(bf16[1024,768]{1,0:T(8,128)(2,1)S(1)} %pad_maximum_fusion.2.refs_0_), channel_id=1, source_target_pairs={{16,0},{0,16},{17,1},{1,17},{18,2},{2,18},{19,3},{3,19},{20,4},{4,... | collective-permute-start | bytes 4718600 | tf_op jit(solution)/shard_map/ppermute | solution.py:29
  317.2 489.3 %all-gather.23.cloned.1.call-start = ((), (), s32[]{:S(2)}) async-start(), calls=%async_computation.5 | async-start | bytes 7864320 | tf_op jit(solution)/shard_map/all_gather | solution.py:929
  328.1 146.8 %collective-permute-start.35 = (bf16[1024,768]{1,0:T(8,128)(2,1)S(1)}, bf16[1024,768]{1,0:T(8,128)(2,1)}, u32[]{:S(2)}, u32[]{:S(2)}) collective-permute-start(bf16[1024,768]{1,0:T(8,128)(2,1)S(1)} %pad_maximum_fusion.3.refs_0_), channel_id=1, source_target_pairs={{16,0},{0,16},{17,1},{1,17},{18,2},{2,18},{19,3},{3,19},{20,4},{4,... | collective-permute-start | bytes 4718600 | tf_op jit(solution)/shard_map/ppermute | solution.py:29
  479.1 366.7 %all-gather.27.cloned.1.call-start = ((), (), s32[]{:S(2)}) async-start(), calls=%async_computation.7 | async-start | bytes 7864320 | tf_op jit(solution)/shard_map/all_gather | solution.py:929
  492.8 41.6 %collective-permute-start.36 = (bf16[1024,768]{1,0:T(8,128)(2,1)S(1)}, bf16[1024,768]{1,0:T(8,128)(2,1)}, u32[]{:S(2)}, u32[]{:S(2)}) collective-permute-start(bf16[1024,768]{1,0:T(8,128)(2,1)S(1)} %pad_maximum_fusion.7), channel_id=1, source_target_pairs={{16,0},{0,16},{17,1},{1,17},{18,2},{2,18},{19,3},{3,19},{20,4},{4,... | collective-permute-start | bytes 4718600 | tf_op jit(solution)/shard_map/ppermute | solution.py:29
  511.7 97.8 %collective-permute-start.20 = (bf16[1024,512]{1,0:T(8,128)(2,1)}, bf16[1024,512]{1,0:T(8,128)(2,1)}, u32[]{:S(2)}, u32[]{:S(2)}) collective-permute-start(bf16[1024,512]{1,0:T(8,128)(2,1)} %convolution_convert_fusion.1), channel_id=1, source_target_pairs={{16,0},{0,16},{17,1},{1,17},{18,2},{2,18},{19,3},{3,19},{20,4},{4,... | collective-permute-start | bytes 3145736 | tf_op jit(solution)/shard_map/ppermute | solution.py:29
  538.6 388.8 %all-gather.19.cloned.1.call-start = ((), (), s32[]{:S(2)}) async-start(), calls=%async_computation.3 | async-start | bytes 5242880 | tf_op jit(solution)/shard_map/all_gather | solution.py:980
  563.7 53.8 %collective-permute-start.19 = (bf16[1024,384]{1,0:T(8,128)(2,1)}, bf16[1024,384]{1,0:T(8,128)(2,1)}, u32[]{:S(2)}, u32[]{:S(2)}) collective-permute-start(bf16[1024,384]{1,0:T(8,128)(2,1)} %fusion.68), channel_id=1, source_target_pairs={{16,0},{0,16},{17,1},{1,17},{18,2},{2,18},{19,3},{3,19},{20,4},{4,... | collective-permute-start | bytes 2359304 | tf_op jit(solution)/shard_map/ppermute | solution.py:29
  614.3 52.6 %collective-permute-start.22 = (bf16[1024,128]{1,0:T(8,128)(2,1)S(1)}, bf16[1024,128]{1,0:T(8,128)(2,1)S(1)}, u32[]{:S(2)}, u32[]{:S(2)}) collective-permute-start(bf16[1024,128]{1,0:T(8,128)(2,1)S(1)} %get-tuple-element.95), channel_id=1, source_target_pairs={{8,0},{12,4},{0,8},{4,12},{9,1},{13,5},{1,9},{5,13},{10,2},{14,6},... | collective-permute-start | bytes 786440 | tf_op jit(solution)/shard_map/ppermute | solution.py:29
  615.9 51.0 %collective-permute-start.21 = (bf16[1024,128]{1,0:T(8,128)(2,1)S(1)}, bf16[1024,128]{1,0:T(8,128)(2,1)S(1)}, u32[]{:S(2)}, u32[]{:S(2)}) collective-permute-start(bf16[1024,128]{1,0:T(8,128)(2,1)S(1)} %get-tuple-element.93), channel_id=1, source_target_pairs={{12,0},{0,4},{4,8},{8,12},{13,1},{1,5},{5,9},{9,13},{14,2},{2,6},{... | collective-permute-start | bytes 786440 | tf_op jit(solution)/shard_map/ppermute | solution.py:29
  800.7 28.8 %collective-permute-start.31 = (f32[19,2048]{1,0:T(8,128)S(1)}, f32[19,2048]{1,0:T(8,128)S(1)}, u32[]{:S(2)}, u32[]{:S(2)}) collective-permute-start(f32[19,2048]{1,0:T(8,128)S(1)} %get-tuple-element.77), channel_id=1, source_target_pairs={{8,0},{12,4},{0,8},{4,12},{9,1},{13,5},{1,9},{5,13},{10,2},{14,6},... | collective-permute-start | bytes 466952 | tf_op jit(solution)/shard_map/ppermute | solution.py:29
  809.8 28.7 %collective-permute-start.27 = (bf16[192,2048]{1,0:T(8,128)(2,1)S(1)}, bf16[192,2048]{1,0:T(8,128)(2,1)S(1)}, u32[]{:S(2)}, u32[]{:S(2)}) collective-permute-start(bf16[192,2048]{1,0:T(8,128)(2,1)S(1)} %pad_maximum_fusion.13), channel_id=1, source_target_pairs={{0,1},{1,0},{2,3},{3,2},{4,5},{5,4},{6,7},{7,6},{8,9},{9,8},{10,11... | collective-permute-start | bytes 2359304 | tf_op jit(solution)/shard_map/ppermute | solution.py:34
  (130 other events, 2152.7 us)
Sparse Core Ops, SparseCore 0:
  22.7 46.3 all-gather.12
  71.2 46.1 all-gather.14
  119.6 123.6 all-gather.16
  274.4 115.3 all-gather.20
  391.2 141.2 all-gather.24
  533.9 138.8 all-gather.22
  675.0 170.8 all-gather.26
  848.0 79.4 all-gather.18

commit v5 on v4

--- a/solution.py
+++ b/solution.py
@@ -13,6 +13,7 @@
 MASKED = -1e30
 F32 = jnp.float32
 BF16 = jnp.bfloat16
+COST = pl.CostEstimate(flops=1024, bytes_accessed=1024, transcendentals=0)
 
 
 def lower(values):
@@ -48,9 +49,10 @@
     return order
 
 
-def gather_tp(values):
-    for bit in reversed(bits("tp")):
-        values = jnp.concatenate([values, swap(values, "tp", bit)], axis=0)
+def gather_tp(values, beside=()):
+    for k, bit in enumerate(reversed(bits("tp"))):
+        far = swap(values, "tp", bit)
+        values = jnp.concatenate([tie(values, beside[k]) if beside else values, far], axis=0)
     return values
 
 
@@ -240,22 +242,44 @@
         ],
         compiler_params=pltpu.CompilerParams(collective_id=collective, has_side_effects=True),
         name="gather_rows",
+        cost_estimate=COST,
     )(*values, *earlier)
 
 
-def scatter_kernel(size, arrays, earlier, *refs):
-    parts = refs[:arrays]
-    outs, refs = refs[arrays + earlier : 2 * arrays + earlier], refs[2 * arrays + earlier :]
+def scatter_kernel(size, arrays, aheads, small, earlier, *refs):
+    parts, swaps = refs[:arrays], refs[arrays : arrays + len(aheads)]
+    given, refs = refs[arrays + len(aheads) :][:small], refs[arrays + len(aheads) + small + earlier :]
+    outs, swapped, refs = refs[:arrays], refs[arrays : arrays + len(aheads)], refs[arrays + len(aheads) :]
+    summed, refs = refs[:small], refs[small:]
+    if small:
+        (given,), (summed,), (near, pair, blocks, small_sent, small_here) = given, summed, refs[-5:]
+        refs = refs[:-5]
     helds, core_ins, x_ins, z_ins = [refs[k * arrays : (k + 1) * arrays] for k in range(4)]
-    local, z_sent, z_here, x_sent, x_here, core_sent, core_here = refs[4 * arrays :]
-    c, t = lax.axis_index("ctx"), lax.axis_index("tp")
+    local, z_sent, z_here, x_sent, x_here, core_sent, core_here, y_sent, y_here = refs[4 * arrays :]
+    c, t, s = lax.axis_index("ctx"), lax.axis_index("tp"), lax.axis_index("shard")
+    shards = lax.axis_size("shard")
+    rings = [{"shard": lax.rem(s + r, shards)} for r in range(1, shards)] if aheads else []
     x_peer, core_peer = {"tp": t ^ 2}, {"tp": t ^ 1}
     first, last = c == 0, c == size - 1
     upper = c // (size // 2)
     spot = [size - 1 - k + upper * (2 * k - size + 1) for k in range(size)]
     before, behind = {"ctx": lax.max(c - 1, 0)}, {"ctx": lax.min(c + 1, size - 1)}
-    greet([x_peer, core_peer], ((jnp.logical_not(first), before), (jnp.logical_not(last), behind)))
+    line = ((jnp.logical_not(first), before), (jnp.logical_not(last), behind))
+    around = [{"ctx": lax.rem(c + r, size)} for r in range(1, size)] if small else []
+    greet([x_peer, core_peer] + rings + around, () if small else line)
+    if small:
+        small_core = remote(given, near.at[0], small_sent, small_here, 0, core_peer)
+        small_x = remote(pair, near.at[1], small_sent, small_here, 1, x_peer)
+        small_ctx = [
+            remote(blocks.at[c], blocks.at[c], small_sent, small_here, 1 + r, around[r - 1]) for r in range(1, size)
+        ]
+        small_from = [
+            remote(blocks.at[b], blocks.at[b], small_sent, small_here, 1 + r, around[r - 1])
+            for r, b in [(r, lax.rem(c + size - r, size)) for r in range(1, size)]
+        ]
+        small_core.start()
     keeps, core, x, rising, falling, finals = [], {}, {}, {}, {}, {}
+    y = [remote(swaps[k], swapped[k], y_sent, y_here, k, rings[ahead - 1]) for k, ahead in enumerate(aheads)]
     for n in range(arrays):
         part, held, core_in, x_in, z_in = parts[n], helds[n], core_ins[n], x_ins[n], z_ins[n]
         keeps.append(pltpu.make_async_copy(part.at[pl.ds(0, 2)], held, local.at[n]))
@@ -273,7 +297,7 @@
             remote(held.at[0, c], z_in.at[0, c], z_sent, z_here, 2 * n * size + c, behind),
             remote(held.at[0, c], z_in.at[1, c], z_sent, z_here, (2 * n + 1) * size + c, before),
         ]
-    for copy in core.values():
+    for copy in list(core.values()) + y:
         copy.start()
     for keep in keeps:
         keep.start()
@@ -296,6 +320,10 @@
 
         each(add_core)
         x[n, k].start()
+    if small:
+        small_core.wait_recv()
+        pair[...] = given[...] + near[0]
+        small_x.start()
     for n, k in order:
         a, held, core_in, x_in, z_in, out = spot[k], helds[n], core_ins[n], x_ins[n], z_ins[n], outs[n]
         core[n, 0, k].wait_recv()
@@ -346,6 +374,11 @@
 
             falling[n, k].start()
 
+    if small:
+        small_x.wait_recv()
+        blocks[c] = pair[...] + near[1]
+        for copy in small_ctx:
+            copy.start()
     for n in range(arrays):
         for side, edge in enumerate((first, last)):
             z_in, out = z_ins[n], outs[n]
@@ -359,6 +392,14 @@
 
                 each(add_side)
 
+    for copy in y:
+        copy.wait()
+    if small:
+        for copy in small_from:
+            copy.wait_recv()
+        summed[...] = sum(blocks[b] for b in range(1, size)) + blocks[0]
+        for copy in [small_core, small_x] + small_ctx:
+            copy.wait_send()
     for copy in list(core.values()) + list(x.values()):
         copy.wait_send()
     for n, k in order:
@@ -372,34 +413,37 @@
             falling[n, k].wait_send()
 
 
-def scatter_rows(parts, collective, *earlier):
+def scatter_rows(parts, collective, swaps, *earlier, small=None):
     size, arrays = lax.axis_size("ctx"), len(parts)
     rows, width = parts[0].shape[2:]
-    return pl.pallas_call(
-        functools.partial(scatter_kernel, size, arrays, len(earlier)),
-        out_shape=[jax.ShapeDtypeStruct((rows, width), F32)] * arrays,
-        in_specs=[pl.BlockSpec(memory_space=pl.ANY)] * (arrays + len(earlier)),
-        out_specs=[pl.BlockSpec(memory_space=pltpu.VMEM)] * arrays,
+    moved = [v for v, _ in swaps]
+    smalls = [] if small is None else [small]
+    anywhere, held = pl.BlockSpec(memory_space=pl.ANY), pl.BlockSpec(memory_space=pltpu.VMEM)
+    found = pl.pallas_call(
+        functools.partial(
+            scatter_kernel, size, arrays, tuple(ahead for _, ahead in swaps), len(smalls), len(earlier)
+        ),
+        out_shape=[jax.ShapeDtypeStruct((rows, width), F32)] * arrays
+        + [jax.ShapeDtypeStruct(v.shape, v.dtype) for v in moved + smalls],
+        in_specs=[anywhere] * (arrays + len(moved)) + [held] * len(smalls) + [anywhere] * len(earlier),
+        out_specs=[held] * arrays + [anywhere] * len(moved) + [held] * len(smalls),
         scratch_shapes=[pltpu.VMEM((2, size, rows, width), BF16)] * (2 * arrays)
         + [pltpu.VMEM((size, rows, width), BF16)] * arrays
         + [pltpu.VMEM((2, size, rows, width), BF16)] * arrays
         + [
             pltpu.SemaphoreType.DMA((arrays * n,))
             for n in (1, 2 * size, 2 * size, size, size, 2 * size, 2 * size)
-        ],
+        ]
+        + [pltpu.SemaphoreType.DMA((max(len(moved), 1),))] * 2
+        + [pltpu.VMEM((n,) + v.shape, F32) if n else pltpu.VMEM(v.shape, F32) for v in smalls for n in (2, 0, size)]
+        + [pltpu.SemaphoreType.DMA((1 + size,))] * (2 * len(smalls)),
         compiler_params=pltpu.CompilerParams(
             collective_id=collective, has_side_effects=True, vmem_limit_bytes=48 * 1024 * 1024
         ),
         name="scatter_rows",
-    )(*parts, *earlier)
-
-
-def sum_tokens(values):
-    size = lax.axis_size("ctx")
-    for bit in bits("tp"):
-        values = values + swap(values, "tp", bit)
-    found = jnp.stack([values] + [receive(values, "ctx", r) for r in range(1, size)])
-    return jnp.sum(ahead_first(found, lax.rem(size - lax.axis_index("ctx"), size)), axis=0)
+        cost_estimate=COST,
+    )(*parts, *moved, *smalls, *earlier)
+    return found[:arrays], found[arrays:]
 
 
 def own_block(values, ahead=0, axis=0):
@@ -424,6 +468,14 @@
         for r in range(1, lax.axis_size("shard"))
     )
     return own, others
+
+
+def product_swaps(others):
+    return [(part, r) for r, part in enumerate(others, 1)]
+
+
+def product_add(own, arrived):
+    return own + sum(part.astype(F32) for part in arrived)
 
 
 def product_sum(own, others):
@@ -514,16 +566,21 @@
             column = column + (i - 1) * 3 * pieces * 128
         (others if i else first)[rows, column : column + 128] = value
 
-    for step in range(tall // deep):
-        rows = slice(step * deep, (step + 1) * deep)
-        moved = matmul(in_pick, inward[rows].reshape(deep * in_rows, 128)).astype(BF16)
-        for row in range(in_rows):
-            i, piece, side = row // (2 * pieces), row // 2 % pieces, row % 2
-            put(i, (side * pieces + piece) * 128, rows, moved[row * deep : (row + 1) * deep])
-        moved = matmul(out_pick, outward[rows].reshape(deep * out_rows, 128)).astype(BF16)
-        for row in range(kept):
-            i, piece = row % group, row // group
-            put(i, (2 * pieces + piece) * 128, rows, moved[row * deep : (row + 1) * deep])
+    def two(ref, step, rows):
+        parts = [ref[slice((step + n) * deep, (step + n + 1) * deep)].reshape(deep * rows, 128) for n in range(2)]
+        return jnp.concatenate(parts, axis=1)
+
+    for step in range(0, tall // deep, 2):
+        moved_in = matmul(in_pick, two(inward, step, in_rows)).astype(BF16)
+        moved_out = matmul(out_pick, two(outward, step, out_rows)).astype(BF16)
+        for n in range(2):
+            rows, lanes = slice((step + n) * deep, (step + n + 1) * deep), slice(n * 128, (n + 1) * 128)
+            for row in range(in_rows):
+                i, piece, side = row // (2 * pieces), row // 2 % pieces, row % 2
+                put(i, (side * pieces + piece) * 128, rows, moved_in[row * deep : (row + 1) * deep, lanes])
+            for row in range(kept):
+                i, piece = row % group, row // group
+                put(i, (2 * pieces + piece) * 128, rows, moved_out[row * deep : (row + 1) * deep, lanes])
     for k in range(3):
         head[:, k * HEAD_DIM : (k + 1) * HEAD_DIM] = entry[k]
     for j in range(ctxs):
@@ -566,6 +623,7 @@
         ],
         compiler_params=pltpu.CompilerParams(vmem_limit_bytes=48 * 1024 * 1024),
         name="own_weights",
+        cost_estimate=COST,
     )(c.astype(jnp.int32)[None], inward, outward, entry, *([attention_out] * ctxs))
 
 
@@ -579,6 +637,77 @@
 
 def turned(values, cosine, sine):
     return values * cosine + pltpu.roll(values, values.shape[-1] // 2, 1) * sine
+
+
+def shared_weights_kernel(ctxs, group, pieces, index, *refs):
+    others = ctxs - 1
+    inwards, outwards, outs = refs[:others], refs[others : 2 * others], refs[-others:]
+    deep, hidden = 16, pieces * 128
+    kinds, out_kinds = group * 2 * pieces, 8 * pieces
+
+    def picker(rows, kept, place):
+        to = lax.broadcasted_iota(jnp.int32, (kept * deep, rows * deep), 0)
+        source = lax.broadcasted_iota(jnp.int32, (kept * deep, rows * deep), 1)
+        return (source == to % deep * rows + place(to // deep)).astype(BF16)
+
+    in_pick = picker(kinds, 2 * pieces, lambda r: (group - 1) * 2 * pieces + r)
+
+    def two(ref, step, rows):
+        parts = [ref[(step + n) * deep : (step + n + 1) * deep].reshape(deep * rows, 128) for n in range(2)]
+        return jnp.concatenate(parts, axis=1)
+
+    for k in range(others):
+        inward, outward, out = inwards[k], outwards[k], outs[k]
+        at = lax.rem(lax.rem(index[0] + k + 1, ctxs), 8 // group) * group + group - 1
+        out_pick = picker(out_kinds, pieces, lambda r: r * 8 + at)
+
+        def put(moved, step, r, column):
+            for n in range(2):
+                rows = slice((step + n) * deep, (step + n + 1) * deep)
+                out[rows, column : column + 128] = moved[r * deep : (r + 1) * deep, n * 128 : (n + 1) * 128]
+
+        for step in range(0, out.shape[0] // deep, 2):
+            moved = matmul(in_pick, two(inward, step, kinds)).astype(BF16)
+            for r in range(2 * pieces):
+                put(moved, step, r, (r % 2 * pieces + r // 2) * 128)
+            moved = matmul(out_pick, two(outward, step, out_kinds)).astype(BF16)
+            for r in range(pieces):
+                put(moved, step, r, (2 * pieces + r) * 128)
+
+
+def shared_weights(expert_in, expert_out, *earlier):
+    ctxs = lax.axis_size("ctx")
+    rows, experts, _, hidden = expert_in.shape
+    group, pieces = experts // ctxs, hidden // 128
+    inward = expert_in.reshape(rows, experts, 2, pieces, 128).transpose(0, 1, 3, 2, 4).reshape(rows, -1, 128)
+    outward = expert_out.reshape(rows, experts // 8, 8, pieces, 128).transpose(0, 1, 3, 2, 4).reshape(rows, -1, 128)
+    tall, others = 64, ctxs - 1
+    after = lambda k, c: lax.rem(c[0] + k + 1, ctxs)
+    return pl.pallas_call(
+        functools.partial(shared_weights_kernel, ctxs, group, pieces),
+        grid_spec=pltpu.PrefetchScalarGridSpec(
+            num_scalar_prefetch=1,
+            grid=(rows // tall,),
+            in_specs=[
+                pl.BlockSpec(
+                    (tall, group * 2 * pieces, 128), functools.partial(lambda k, b, c: (b, after(k, c), 0), k)
+                )
+                for k in range(others)
+            ]
+            + [
+                pl.BlockSpec(
+                    (tall, 8 * pieces, 128), functools.partial(lambda k, b, c: (b, after(k, c) * group // 8, 0), k)
+                )
+                for k in range(others)
+            ]
+            + [pl.BlockSpec(memory_space=pl.ANY)] * len(earlier),
+            out_specs=[pl.BlockSpec((tall, 3 * hidden), lambda b, c: (b, 0))] * others,
+        ),
+        out_shape=[jax.ShapeDtypeStruct((rows, 3 * hidden), BF16)] * others,
+        compiler_params=pltpu.CompilerParams(vmem_limit_bytes=48 * 1024 * 1024),
+        name="shared_weights",
+        cost_estimate=COST,
+    )(lax.axis_index("ctx").astype(jnp.int32)[None], *([inward] * others), *([outward] * others), *earlier)
 
 
 def project_kernel(tokens, gain, weight, gains, cosine, sine, normed, raw, query, key, value):
@@ -614,6 +743,7 @@
         ],
         compiler_params=pltpu.CompilerParams(vmem_limit_bytes=48 * 1024 * 1024),
         name="project",
+        cost_estimate=COST,
     )(tokens, gain, weight, gains, cosine, sine)
 
 
@@ -648,12 +778,14 @@
         out_shape=jax.ShapeDtypeStruct((rows, HEAD_DIM), BF16),
         compiler_params=pltpu.CompilerParams(vmem_limit_bytes=48 * 1024 * 1024),
         name="attend",
+        cost_estimate=COST,
     )(query, key, value, row_doc, column_doc)
 
 
 def attend_back_kernel(
-    tall, query, key, value, raw, cosine, sine, gains, row_doc, column_doc, mixed_grad, grad, gain_grad, key_grad, value_grad
+    tall, query, key, value, raw, cosine, sine, gains, row_doc, column_doc, mixed_grad, *refs
 ):
+    grad, gain_grad, key_grad, value_grad = refs[-4:]
     step = pl.program_id(0)
     rows = pl.ds(pl.multiple_of(step * tall, tall), tall)
 
@@ -693,7 +825,7 @@
         grad[:, 2 * HEAD_DIM :] = value_grad[...].astype(BF16)
 
 
-def attend_back(query, key, value, raw, cosine, sine, gains, row_doc, column_doc, mixed_grad):
+def attend_back(query, key, value, raw, cosine, sine, gains, row_doc, column_doc, mixed_grad, *earlier):
     rows = query.shape[0]
     tall = 256
     block = pl.BlockSpec((tall, HEAD_DIM), lambda b: (b, 0))
@@ -712,7 +844,8 @@
             pl.BlockSpec((tall, 1), lambda b: (b, 0)),
             whole(column_doc),
             block,
-        ],
+        ]
+        + [pl.BlockSpec(memory_space=pl.ANY)] * len(earlier),
         out_specs=[
             pl.BlockSpec((rows, 3 * HEAD_DIM), lambda b: (0, 0)),
             pl.BlockSpec((8, HEAD_DIM), lambda b: (0, 0)),
@@ -724,37 +857,60 @@
         scratch_shapes=[pltpu.VMEM((rows, HEAD_DIM), F32)] * 2,
         compiler_params=pltpu.CompilerParams(vmem_limit_bytes=48 * 1024 * 1024),
         name="attend_back",
-    )(query, key, value, raw, cosine, sine, gains, row_doc, column_doc, mixed_grad)
-
-
-def expert_step_kernel(index, earlier, rows, upstream, gate_in, up_in, outward, gates, *refs):
-    scaled, inner_grad, gate_part = refs[earlier:]
-    hidden_size = outward.shape[1]
-    gate, up = matmul(rows[...], gate_in[...]), matmul(rows[...], up_in[...])
-    back = matmul(upstream[...], outward[...])
+        cost_estimate=COST,
+    )(query, key, value, raw, cosine, sine, gains, row_doc, column_doc, mixed_grad, *earlier)
+
+
+def expert_step_kernel(index, count, earlier, shard, rows, upstream, *refs):
+    gate_in, up_in, outward = [refs[k * count : (k + 1) * count] for k in range(3)]
+    gates, lanes, scaled, inner_grad, gate_part = refs[3 * count], refs[3 * count + 1], *refs[3 * count + 2 + earlier :]
+    hidden_size = outward[0].shape[1]
+    deep = outward[0].shape[0]
+
+    def product(left, parts):
+        total = 0.0
+        for r, part in enumerate(parts):
+            start = pl.multiple_of(lax.rem(shard[0] + r, count) * deep, deep) if count > 1 else 0
+            total = total + matmul(left[:, pl.ds(start, deep)], part[...])
+        return total
+
+    gate, up, back = product(rows, gate_in), product(rows, up_in), product(upstream, outward)
     sigmoid = 1.0 / (1.0 + jnp.exp(-gate))
     silu = gate * sigmoid
     hidden = (silu * up).astype(BF16).astype(F32)
     weight = gates[:, index : index + 1]
     scaled[...] = (hidden * weight).astype(BF16)
-    lane = lax.broadcasted_iota(jnp.int32, gate_part.shape, 1)
-    gate_part[...] = jnp.where(lane == index, jnp.sum(hidden * back, axis=1, keepdims=True), 0.0)
+    gate_part[...] = jnp.sum(hidden * back, axis=1, keepdims=True) * lanes[index : index + 1, :]
     hidden_grad = back * weight
     inner_grad[:, :hidden_size] = (hidden_grad * up * sigmoid * (1.0 + gate * (1.0 - sigmoid))).astype(BF16)
     inner_grad[:, hidden_size:] = (hidden_grad * silu).astype(BF16)
 
 
-def expert_step(index, place, rows, upstream, weights, hidden_size, gates, *earlier):
+def expert_step(index, place, rows, upstream, weights, hidden_size, gates, lanes, *earlier):
     count, width = rows.shape
-    tall = 256
-    block = lambda n: pl.BlockSpec((tall, n), lambda b: (b, 0))
-    column = lambda k: pl.BlockSpec((width, hidden_size), lambda b: (0, 3 * place + k))
+    tall, parts = 256, len(weights)
+    block = lambda n: pl.BlockSpec((tall, n), lambda b, s: (b, 0))
+    whole = weights[0].shape[0] == width
+
+    def column(k, r, b, s):
+        return (lax.rem(s[0] + r, parts) if whole else 0, 3 * place + k)
+
+    columns = [
+        pl.BlockSpec((width // parts, hidden_size), functools.partial(column, k, r))
+        for k in range(3)
+        for r in range(parts)
+    ]
     return pl.pallas_call(
-        functools.partial(expert_step_kernel, index, len(earlier)),
-        grid=(count // tall,),
-        in_specs=[block(width), block(width), column(0), column(1), column(2), block(gates.shape[1])]
-        + [pl.BlockSpec(memory_space=pl.ANY)] * len(earlier),
-        out_specs=[block(hidden_size), block(2 * hidden_size), block(128)],
+        functools.partial(expert_step_kernel, index, parts, len(earlier)),
+        grid_spec=pltpu.PrefetchScalarGridSpec(
+            num_scalar_prefetch=1,
+            grid=(count // tall,),
+            in_specs=[block(width), block(width)]
+            + columns
+            + [block(gates.shape[1]), pl.BlockSpec(lanes.shape, lambda b, s: (0, 0))]
+            + [pl.BlockSpec(memory_space=pl.ANY)] * len(earlier),
+            out_specs=[block(hidden_size), block(2 * hidden_size), block(128)],
+        ),
         out_shape=[
             jax.ShapeDtypeStruct((count, hidden_size), BF16),
             jax.ShapeDtypeStruct((count, 2 * hidden_size), BF16),
@@ -762,55 +918,151 @@
         ],
         compiler_params=pltpu.CompilerParams(vmem_limit_bytes=48 * 1024 * 1024),
         name="expert_step",
-    )(rows, upstream, weights, weights, weights, gates, *earlier)
-
-
-def expert_kernel(group, tall, hidden, *refs):
-    chunks, up, down, up_rows, down_rows = refs[:group], *refs[group:]
+        cost_estimate=COST,
+    )(lax.axis_index("shard").astype(jnp.int32)[None], rows, upstream, *(list(weights) * 3), gates, lanes, *earlier)
+
+
+def combine_kernel(count, extras, *refs):
+    lefts, rights, lanes, out = refs[:count], refs[count : 2 * count], refs[2 * count : 2 * count + extras], refs[-1]
+    width = rights[0].shape[0]
+    total = matmul(lefts[0][...], rights[0][...], (1, 1))
+    for left, right in zip(lefts[1:], rights[1:]):
+        total = total + matmul(left[...], right[...], (1, 1))
+    out[:, :width] = total.astype(BF16)
+    if extras:
+        out[:, width:] = sum(lane[...] for lane in lanes).astype(BF16)
+
+
+def combine(lefts, rights, lanes, *earlier):
+    (rows, _), (width, _) = lefts[0][0].shape, rights[0][0].shape
+    tall, deep = 256, 256
+    total = width + (lanes[0].shape[1] if lanes else 0)
+    return pl.pallas_call(
+        lambda *refs: combine_kernel(len(lefts), len(lanes), *refs[: len(refs) - 1 - len(earlier)], refs[-1]),
+        grid=(rows // tall,),
+        in_specs=[pl.BlockSpec((tall, deep), functools.partial(lambda k, b: (b, k), k)) for _, k in lefts]
+        + [
+            pl.BlockSpec((width, deep), functools.partial(lambda k, b: (0, k), k), pipeline_mode=pl.Buffered(1))
+            for _, k in rights
+        ]
+        + [pl.BlockSpec((tall, lane.shape[1]), lambda b: (b, 0)) for lane in lanes]
+        + [pl.BlockSpec(memory_space=pl.ANY)] * len(earlier),
+        out_specs=pl.BlockSpec((tall, total), lambda b: (b, 0)),
+        out_shape=jax.ShapeDtypeStruct((rows, total), BF16),
+        compiler_params=pltpu.CompilerParams(vmem_limit_bytes=56 * 1024 * 1024),
+        name="combine",
+        cost_estimate=COST,
+    )(*[v for v, _ in lefts], *[v for v, _ in rights], *lanes, *earlier)
+
+
+def gradient_kernel(steps, index, rows, upstream, inner_grad, scaled, own, others):
+    step = pl.program_id(0)
+    wide = inner_grad.shape[1]
+
+    def put(out):
+        out[:, :wide] = matmul(rows[...], inner_grad[...], (0, 0)).astype(out.dtype)
+        out[:, wide:] = matmul(upstream[...], scaled[...], (0, 0)).astype(out.dtype)
+
+    @pl.when(step < steps)
+    def _():
+        put(own)
+
+    @pl.when(step >= steps)
+    def _():
+        put(others)
+
+
+def gradient_parts(rows, upstream, inner_grad, scaled):
+    s, shards = lax.axis_index("shard"), lax.axis_size("shard")
+    count, width = rows.shape
+    deep = 256
+    steps = width // shards // deep
+    wide = inner_grad.shape[1] + scaled.shape[1]
+    feature = pl.BlockSpec((count, deep), lambda b, s: (0, lax.rem(s[0] * steps + b, steps * shards)))
+    whole = lambda v: pl.BlockSpec(v.shape, lambda b, s: (0, 0))
+    return pl.pallas_call(
+        functools.partial(gradient_kernel, steps),
+        grid_spec=pltpu.PrefetchScalarGridSpec(
+            num_scalar_prefetch=1,
+            grid=(steps * shards,),
+            in_specs=[feature, feature, whole(inner_grad), whole(scaled)],
+            out_specs=[
+                pl.BlockSpec((deep, wide), lambda b, s: (lax.min(b, steps - 1), 0)),
+                pl.BlockSpec((deep, wide), lambda b, s: (lax.max(b - steps, 0), 0)),
+            ],
+        ),
+        out_shape=[
+            jax.ShapeDtypeStruct((steps * deep, wide), F32),
+            jax.ShapeDtypeStruct((steps * deep * (shards - 1), wide), BF16),
+        ],
+        compiler_params=pltpu.CompilerParams(vmem_limit_bytes=48 * 1024 * 1024),
+        name="gradient_parts",
+        cost_estimate=COST,
+    )(s.astype(jnp.int32)[None], rows, upstream, inner_grad, scaled)
+
+
+def expert_kernel(group, ctxs, tall, hidden, index, *refs):
+    gathered, shared, (up, down) = refs[: group - 1], refs[group - 1 : group - 1 + ctxs], refs[group - 1 + ctxs :]
     pieces = hidden // 128
-    ctxs = chunks[0].shape[0]
     experts = group * ctxs
-    for i in range(group):
-        for j in range(ctxs):
-            e = j * group + i
-            for p in range(2 * pieces):
-                side, piece = p // pieces, p % pieces
-                value = chunks[i][j, :, p * 128 : p * 128 + 128].astype(F32)
-                up_rows[pl.ds((e * pieces + piece) * 2 + side, tall, stride=experts * pieces * 2), :] = value
-            for piece in range(pieces):
-                value = chunks[i][j, :, (2 * pieces + piece) * 128 : (2 * pieces + piece) * 128 + 128].astype(F32)
-                row = (e // 8 * pieces + piece) * 8 + e % 8
-                down_rows[pl.ds(row, tall, stride=experts * pieces), :] = value
-    up[...] = up_rows[...].reshape(up.shape)
-    down[...] = down_rows[...].reshape(down.shape)
-
-
-def expert_gradients(chunks):
-    group = len(chunks)
-    ctxs, rows, width = chunks[0].shape
+    deep = 16
+    to = lax.broadcasted_iota(jnp.int32, (deep * deep, deep * deep), 0)
+    source = lax.broadcasted_iota(jnp.int32, (deep * deep, deep * deep), 1)
+    turn = (source == to % deep * deep + to // deep).astype(BF16)
+
+    def tile(e, column, start):
+        rows, columns = slice(start, start + deep), slice(column, column + 128)
+        if e % group == group - 1:
+            return shared[e // group][0, rows, columns]
+        return gathered[e % group][e // group, rows, columns]
+
+    def place(out, kinds, start):
+        blocks = [jnp.concatenate([tile(e, column, start) for e, column in kinds[k : k + deep]], axis=0) for k in range(0, len(kinds), deep)]
+        for k in range(0, len(blocks), 2):
+            pair = blocks[k : k + 2]
+            moved = matmul(turn, jnp.concatenate(pair, axis=1))
+            for n in range(len(pair)):
+                for d in range(deep):
+                    row = (start + d) * len(kinds) + (k + n) * deep
+                    out[row : row + deep, :] = moved[d * deep : (d + 1) * deep, n * 128 : (n + 1) * 128]
+
+    ups = [(e, (side * pieces + piece) * 128) for e in range(experts) for piece in range(pieces) for side in range(2)]
+    downs = [
+        (part * 8 + e, (2 * pieces + piece) * 128)
+        for part in range(experts // 8)
+        for piece in range(pieces)
+        for e in range(8)
+    ]
+    for start in range(0, tall, deep):
+        place(up, ups, start)
+        place(down, downs, start)
+
+
+def expert_gradients(gathered, shared):
+    (ctxs, rows, width), group = shared.shape, len(gathered) + 1
     hidden, experts = width // 3, group * ctxs
     pieces = hidden // 128
     assert experts % 8 == 0 and hidden % 128 == 0
-    tall = 32
+    tall = 64
     up, down = pl.pallas_call(
-        functools.partial(expert_kernel, group, tall, hidden),
-        grid=(rows // tall,),
-        in_specs=[pl.BlockSpec((ctxs, tall, width), lambda b: (0, b, 0))] * group,
-        out_specs=[
-            pl.BlockSpec((tall, experts * pieces * 2, 128), lambda b: (b, 0, 0)),
-            pl.BlockSpec((tall, experts * pieces, 128), lambda b: (b, 0, 0)),
-        ],
-        out_shape=[
-            jax.ShapeDtypeStruct((rows, experts * pieces * 2, 128), F32),
-            jax.ShapeDtypeStruct((rows, experts * pieces, 128), F32),
-        ],
-        scratch_shapes=[
-            pltpu.VMEM((tall * experts * pieces * 2, 128), F32),
-            pltpu.VMEM((tall * experts * pieces, 128), F32),
-        ],
-        compiler_params=pltpu.CompilerParams(vmem_limit_bytes=32 * 1024 * 1024),
+        functools.partial(expert_kernel, group, ctxs, tall, hidden),
+        grid_spec=pltpu.PrefetchScalarGridSpec(
+            num_scalar_prefetch=1,
+            grid=(rows // tall,),
+            in_specs=[pl.BlockSpec((ctxs, tall, width), lambda b, c: (0, b, 0))] * len(gathered)
+            + [
+                pl.BlockSpec(
+                    (1, tall, width), functools.partial(lambda j, b, c: (lax.rem(ctxs + j - c[0], ctxs), b, 0), j)
+                )
+                for j in range(ctxs)
+            ],
+            out_specs=[pl.BlockSpec((tall * experts * pieces * k, 128), lambda b, c: (b, 0)) for k in (2, 1)],
+        ),
+        out_shape=[jax.ShapeDtypeStruct((rows * experts * pieces * k, 128), F32) for k in (2, 1)],
+        compiler_params=pltpu.CompilerParams(vmem_limit_bytes=48 * 1024 * 1024),
         name="expert_gradients",
-    )(*chunks)
+        cost_estimate=COST,
+    )(lax.axis_index("ctx").astype(jnp.int32)[None], *gathered, *([shared] * ctxs))
     up = up.reshape(rows, experts, pieces, 2, 128).transpose(0, 1, 3, 2, 4).reshape(rows, experts, 2, hidden)
     down = down.reshape(rows, experts // 8, pieces, 8, 128).transpose(0, 1, 3, 2, 4).reshape(rows, experts, hidden)
     return up, down
@@ -836,6 +1088,7 @@
         out_specs=[pl.BlockSpec((3, tall, wide), lambda b: (0, b, 0)), pl.BlockSpec((tall, wide), lambda b: (b, 0))],
         out_shape=[jax.ShapeDtypeStruct((3, rows, wide), F32), jax.ShapeDtypeStruct((rows, wide), F32)],
         name="attention_gradients",
+        cost_estimate=COST,
     )(chunk)
     return entry.transpose(1, 0, 2), exit_out
 
@@ -877,11 +1130,6 @@
     head_in = gather_natural(head_in, "shard")
     first_weights, others = gather_natural(first_weights, "shard"), gather_natural(others, "shard")
     exit_weight = gather_small(exit_weight, 0)
-    columns = lambda i, start, count: (others if i else first_weights)[
-        :, (3 * max(i - 1, 0) + start) * hidden_size : (3 * max(i - 1, 0) + start + count) * hidden_size
-    ]
-    in_weights = [columns(i, 0, 2) for i in range(group)]
-    out_weights = [columns(i, 2, 1) for i in range(group)]
     first = t * own
     tokens_own = lax.dynamic_slice_in_dim(tokens[0], first, own)
     cot_own = lax.dynamic_slice_in_dim(cotangent[0], first, own)
@@ -916,38 +1164,43 @@
     normed_two = lower(residual * inverse_scale(residual) * gain_two)
     normed_two_all = gather_rows([normed_two], 0)[0].reshape(every, width)
     chances_all = jax.nn.softmax(dot(normed_two_all, router, (1, 0)), axis=-1)
-    gates = jnp.where(picks_all, chances_all, 0.0)
-    gates = lax.dynamic_slice_in_dim(gates, base, group, axis=1)
-    normed_blocks = [own_block(normed_two_all, r, 1) for r in range(shards)]
-    cot_blocks = [own_block(cot_all, r, 1) for r in range(shards)]
-    scaled, gate_parts, inner_grads, products, chunks, gathered = [], [], [], [], [], []
-
-    def finish(i, later):
-        own_part, others = products[i]
-        chunks.append(lower(product_sum(tie(own_part, later), others)))
-        chunk = chunks[i] if i < 2 else tie(chunks[i], gathered[i - 2])
-        gathered.append(lax.all_gather(chunk, "ctx", axis=0, tiled=False))
-
+    gates_all = jnp.where(picks_all, chances_all, 0.0)
+    gates = lax.dynamic_slice_in_dim(gates_all, base, group, axis=1)
+    lanes = (jnp.arange(128)[None] == base + jnp.arange(group)[:, None]).astype(F32)
+    scaled, gate_parts, inner_grads, products = [], [], [], []
+
+    def gradient_blocks(inner_grad, gated):
+        own_part, far = gradient_parts(normed_two_all, cot_all, inner_grad, gated)
+        return own_part, tuple(far[r * block : (r + 1) * block] for r in range(shards - 1))
+
+    last = group - 1
+    before = []
     for i in range(group):
-        before = [] if i == 0 else list(products[i - 1][1])
+        weights = [others] * shards if i == last else [others] if i else [first_weights]
         step = expert_step(
-            i, max(i - 1, 0), normed_two_all, cot_all, others if i else first_weights, hidden_size, gates, *before
+            i, max(i - 1, 0), normed_two_all, cot_all, weights, hidden_size, gates, lanes, *before
         )
         scaled.append(step[0])
         inner_grads.append(step[1])
         gate_parts.append(step[2])
-        products.append(product_parts([(normed_blocks, inner_grads[i]), (cot_blocks, scaled[i])]))
-    early = min(2, group)
-    for i in range(early):
-        finish(i, products[min(2 * i + 1, group - 1)][1][0])
-    normed_part = sum(dot(inner_grads[i], in_weights[i], (1, 1)) for i in range(group))
-    gate_part = lax.dynamic_update_slice(
-        jnp.zeros((every, 128), F32), sum(gate_parts)[:, :group], (0, base)
+        products.append(gradient_blocks(inner_grads[i], scaled[i]))
+        before = list(products[i][1])
+        if i == 1:
+            shared = shared_weights(expert_in, expert_out, *before)
+            before += shared
+    chunks, gathered = [], []
+    for i in range(last):
+        own_part, far = products[i]
+        chunks.append(lower(product_sum(tie(own_part, inner_grads[last] if i else products[1][1][0]), far)))
+        gathered.append(lax.all_gather(chunks[i], "ctx", axis=0, tiled=False))
+    columns = lambda k: [(others if i else first_weights, 3 * max(i - 1, 0) + k) for i in range(group)]
+    normed_part = combine(
+        [(v, k) for k in range(2) for v in inner_grads], columns(0) + columns(1), gate_parts, *before
     )
-    normed_part = lower(jnp.concatenate([normed_part, gate_part], axis=1))
-    (normed_sum,) = scatter_rows([normed_part.reshape(tps, ctxs, own, -1)], 1, *chunks)
-    for i in range(early, group):
-        finish(i, normed_sum)
+    weight_swaps = lambda weights: [(w, shards - r) for w in weights for r in range(1, shards)]
+    (normed_sum,), arrived = scatter_rows([normed_part.reshape(tps, ctxs, own, -1)], 1, weight_swaps(shared[:-1]))
+    shared_all = [[w] + list(arrived[k * (shards - 1) : (k + 1) * (shards - 1)]) for k, w in enumerate(shared[:-1])]
+    normed_sum = tie(normed_sum, gathered[0])
     normed_sum, gate_grad = normed_sum[:, :width], normed_sum[:, width : width + experts]
 
     router_chances = jax.nn.softmax(dot(normed_two, router, (1, 0)), axis=-1)
@@ -961,12 +1214,7 @@
     residual_grad = upstream + residual_back
 
     attend_grad = gather_tp(lower(residual_grad))
-    exit_part = product_sum(*product_parts([([own_block(attend_grad, r, 1) for r in range(shards)], mixed)]))
-    exit_head = exit_part[:, :head_size]
-    for r in range(1, ctxs):
-        exit_head = exit_head + receive(
-            lower(exit_part[:, r * head_size : (r + 1) * head_size]), "ctx", ctxs - r
-        ).astype(F32)
+    exit_parts = product_parts([([own_block(attend_grad, r, 1) for r in range(shards)], mixed)])
     mixed_grad = lower(dot(attend_grad, exit_weight, (1, 0))).reshape(tps, own, ctxs, head_size)
     parts = [mixed_grad[:, :, 0]] + [receive(mixed_grad[:, :, ctxs - j], "ctx", j) for j in range(1, ctxs)]
     mixed_grad = ahead_first(jnp.stack(parts, axis=1), lax.rem(ctxs - c, ctxs), 1)
@@ -975,40 +1223,69 @@
         queries, keys, values, raw, cosine, sine, head_gains, row_doc, column_doc, mixed_grad
     )
     entry_blocks = [own_block(normed_one_all, r, 1) for r in range(shards)]
-    entry_head = product_sum(*product_parts([(entry_blocks, projected_grad)]))
-    attention_chunk = lower(jnp.concatenate([entry_head, exit_head], axis=1))
-    attention_gathered = lax.all_gather(tie(attention_chunk, gathered[-2]), "ctx", axis=0, tiled=False)
-
-    result_part = lower(sum(dot(tie(scaled[i], projected_grad), out_weights[i], (1, 1)) for i in range(group)))
+    entry_parts = product_parts([(entry_blocks, projected_grad)])
+    shared_gates = ahead_first(gates_all[:, last::group], c, 1)
+    shared_all += [[w] + [receive(w, "shard", r) for r in range(1, shards)] for w in shared[len(shared_all) :]]
+    exit_part = product_sum(*exit_parts)
+    shared_products = [products[last]]
+    shared_chunks = [lower(product_sum(*products[last]))]
+    earlier = [exit_part, *entry_parts[1], *chunks]
+    for j in range(1, ctxs):
+        step = expert_step(
+            j, 0, normed_two_all, cot_all, shared_all[j - 1], hidden_size, shared_gates, lanes, *earlier
+        )
+        parts = gradient_blocks(step[1], step[0])
+        shared_products.append(parts)
+        earlier = list(parts[1])
+        if j == 1:
+            exit_head = tie(exit_part[:, :head_size], parts[1][0])
+            for r in range(1, ctxs):
+                exit_head = exit_head + receive(
+                    lower(exit_part[:, r * head_size : (r + 1) * head_size]), "ctx", ctxs - r
+                ).astype(F32)
+            earlier += [shared_chunks[0], gathered[1], *shared_all[-1][1:]]
+        if j == 2:
+            entry_head = product_sum(tie(entry_parts[0], parts[1][0]), entry_parts[1])
+            attention_chunk = lower(jnp.concatenate([entry_head, exit_head], axis=1))
+            attention_gathered = lax.all_gather(attention_chunk, "ctx", axis=0, tiled=False)
+
+    result_part = combine([(v, 0) for v in scaled], columns(2), [], *earlier, attention_chunk)
     first_part = dot(projected_grad, head_in, (1, 1), BF16)
-    first_normed_grad, result_sum = scatter_rows(
-        [part.reshape(tps, ctxs, own, width) for part in (first_part, result_part)], 2, attention_chunk
+    tokens_wide = tokens_all.astype(F32)
+    first_sum = jnp.sum(first_part.astype(F32) * tokens_wide * inverse_scale(tokens_wide), axis=0)
+    head_part = gain_part[:2].reshape(1, -1)
+    small_part = [jnp.sum(second_part, axis=0)[None], first_sum[None], jnp.pad(head_part, ((0, 0), (0, width - head_part.shape[1])))]
+    small_part = jnp.concatenate([router_part] + small_part, axis=0)
+    small_part = jnp.pad(small_part, ((0, -small_part.shape[0] % 8), (0, 0)))
+    shared_chunks.append(lower(product_sum(*shared_products[1])))
+    (first_normed_grad, result_sum), arrived = scatter_rows(
+        [part.reshape(tps, ctxs, own, width) for part in (first_part, result_part)],
+        2,
+        sum([product_swaps(p[1]) for p in shared_products[2:]], []),
+        shared_chunks[1],
+        small=small_part,
     )
+    head_gradient = sum_shard(arrived[-1][experts + 2 : experts + 3, : head_part.shape[1]], 1)[0]
+    small_sum = sum_shard(arrived[-1][: experts + 2], 1)
+    for k, p in enumerate(shared_products[2:]):
+        shared_chunks.append(lower(product_add(p[0], arrived[k * (shards - 1) : (k + 1) * (shards - 1)])))
     layer_output = natural_rows(gather_tp(lower(residual + result_sum)))[None]
-
-    input_back, first_part = norm_back(first_normed_grad, layer_in, gain_one)
+    input_back, _ = norm_back(first_normed_grad, layer_in, gain_one)
     input_gradient = natural_rows(gather_tp(lower(residual_grad + input_back))).astype(F32)[None]
 
-    head_part = gain_part[:2].reshape(-1)
-    small_part = jnp.concatenate(
-        [jnp.sum(second_part, axis=0)[None], jnp.sum(first_part, axis=0)[None], router_part], axis=0
+    upward_gradient, downward_gradient = expert_gradients(
+        gathered, jnp.stack(shared_chunks)
     )
-    small_part = jnp.concatenate([small_part, jnp.pad(head_part, (0, width - head_part.shape[0]))[None]], axis=0)
-    small_sum = sum_tokens(small_part)
-    head_gradient = sum_shard(small_sum[-1:, : head_part.shape[0]], 1)[0]
-    small_sum = sum_shard(small_sum[:-1], 1)
-
-    upward_gradient, downward_gradient = expert_gradients(gathered)
     entry_gradient, exit_gradient = attention_gradients(attention_gathered)
     return (
         layer_output,
         input_gradient,
-        small_sum[1],
+        small_sum[experts + 1],
         head_gradient,
         entry_gradient,
         exit_gradient,
-        small_sum[0],
-        small_sum[2:].T,
+        small_sum[experts],
+        small_sum[:experts].T,
         upward_gradient,
         downward_gradient,
     )

time: 950 us -> 878 us (0.924)
  Pallas kernels: 459 us -> 628 us
  matrix products: 166 us -> 27 us
  waiting for transfers between devices: 150 us -> 54 us
    pallas_call x7 -> x20, Pallas kernels: 305 us -> 475 us  [the longest x2 241 us: scatter_rows(): pl.pallas_call(functools.partial(scatter_kernel, size, arrays, tuple((ahe...]
    dot_general x35 -> x11, matrix products: 166 us -> 27 us  [dot(): lax.dot_general(left, right, (((over[0],), (over[1],)), ((), ())), prefer...]
    ppermute x27 -> x26, waiting for transfers between devices: 95.6 us -> 41.9 us  [receive(): lax.ppermute(values, axis, [((i + distance) % size, i) for i in range(siz...]
    all_gather x5 -> x4, waiting for transfers between devices: 26.9 us -> 0.02 us  [the longest x3 0.02 us: local(): gathered.append(lax.all_gather(chunks[i], 'ctx', axis=0, tiled=False))]
    ppermute x10 -> x8, waiting for transfers between devices: 21.9 us -> 11.2 us  [swap(): return lax.ppermute(values, axis, [(i, i ^ bit) for i in range(size)])]
    ppermute x27 -> x26, starting transfers between devices: 41.9 us -> 34.4 us  [receive(): lax.ppermute(values, axis, [((i + distance) % size, i) for i in range(siz...]
    unnamed x241 -> x257, local copies, waits for them, and re-layouts: 28.6 us -> 25.2 us
  transfers between devices with their start and end apart: 45 -> 41, of which waited for: 19 -> 9; matrix products, arithmetic and copies ran while one was open for 26% -> 11% of each run, Pallas kernels for 46% -> 70%
where the time goes in v5:
time: 878 us; the launch traced here: 866 us
  Pallas kernels  628 us (72%)
  waiting for transfers between devices  54 us (6%)
  other arithmetic  49.9 us (6%)
  local copies, waits for them, and re-layouts  46.3 us (5%)
  starting transfers between devices  40.4 us (5%)
  matrix products  27 us (3%)
  between operations  19.6 us (2%)
    pallas_call x2, Pallas kernels, scatter_rows(): pl.pallas_call(functools.partial(scatter_kernel, size, arrays, tuple((ahe...  241 us
    pallas_call x2, Pallas kernels, gather_rows(): pl.pallas_call(functools.partial(gather_kernel, size, pieces, arrays, sha...  103 us
    pallas_call x7, Pallas kernels, gradient_parts(): pl.pallas_call(functools.partial(gradient_kernel, steps), grid_spec=pltpu...  83.9 us
    pallas_call x7, Pallas kernels, expert_step(): pl.pallas_call(functools.partial(expert_step_kernel, index, parts, len(ea...  74.6 us
    ppermute x26, waiting for transfers between devices, receive(): lax.ppermute(values, axis, [((i + distance) % size, i) for i in range(siz...  41.9 us
    ppermute x26, starting transfers between devices, receive(): lax.ppermute(values, axis, [((i + distance) % size, i) for i in range(siz...  34.4 us
    pallas_call x2, Pallas kernels, combine(): pl.pallas_call(lambda *refs: combine_kernel(len(lefts), len(lanes), *refs...  31.7 us
    pallas_call x1, Pallas kernels, expert_gradients(): pl.pallas_call(functools.partial(expert_kernel, group, ctxs, tall, hidden...  27.7 us
  transfers between devices with their start and end apart: 41, of which 9 were waited for; matrix products, arithmetic and copies ran while one was open for 11% of the time, Pallas kernels for 70%

profile of v5, /device:TPU:0, one launch (start us, length us, event | category | flops | bytes accessed | tf_op | source)
XLA Modules:
  0.0 865.7 jit_solution(12149055245362768577)
XLA Ops:
  8.5 13.2 %own_weights.1 = (bf16[1024,768]{1,0:T(8,128)(2,1)}, bf16[1024,2304]{1,0:T(8,128)(2,1)}, bf16[1024,384]{1,0:T(8,128)(2,1)}, bf16[1024,512]{1,0:T(8,128)(2,1)S(1)}) custom-call(s32[1]{0:T(128)} %bitcast.3.index, bf16[1024,64,128]{2,1,0:T(8,128)(2,1)} %bitcast.200, bf16[1024,32,128]{2,1,0:T(8,128)(2,1)} %bitcast.204, bf16[3,1024,512]{2,1,0:T(8,128)(2,1)} %bitcast.222, ...), custom_call_target="tpu_custom_call" | custom-call | flops 1024 | bytes 1024 | tf_op jit(solution)/shard_map/own_weights/pallas_call | solution.py:617
  36.9 64.1 %gather_rows.2 = (bf16[4,4,96,2048]{3,2,1,0:T(8,128)(2,1)}, bf16[4,4,96,2048]{3,2,1,0:T(8,128)(2,1)}) custom-call(bf16[384,2048]{1,0:T(8,128)(2,1)} %bitcast.221, bf16[384,2048]{1,0:T(8,128)(2,1)} %bitcast.224, bf16[1024,384]{1,0:T(8,128)(2,1)} %get-tuple-element.70.refs_2_), custom_call_target="tpu_custom_call" | custom-call | flops 1024 | bytes 1024 | tf_op jit(solution)/shard_map/gather_rows/pallas_call | solution.py:233
  165.4 38.8 %gather_rows.3 = bf16[4,4,96,2048]{3,2,1,0:T(8,128)(2,1)} custom-call(bf16[96,2048]{1,0:T(8,128)(2,1)} %multiply_convert_fusion.refs_0_), custom_call_target="tpu_custom_call" | custom-call | flops 1024 | bytes 1024 | tf_op jit(solution)/shard_map/gather_rows/pallas_call | solution.py:233
  211.2 10.3 %expert_step.7 = (bf16[1536,256]{1,0:T(8,128)(2,1)S(1)}, bf16[1536,512]{1,0:T(8,128)(2,1)S(1)}, f32[1536,128]{1,0:T(8,128)S(1)}) custom-call(s32[1]{0:T(128)} %bitcast.31.shard.index, bf16[1536,2048]{1,0:T(8,128)(2,1)} %bitcast.172, bf16[1536,2048]{1,0:T(8,128)(2,1)} %bitcast.186, ...), custom_call_target="tpu_custom_call" | custom-call | flops 1024 | bytes 1024 | tf_op jit(solution)/shard_map/expert_step/pallas_call | solution.py:903
  222.4 12.5 %gradient_parts.7 = (f32[1024,768]{1,0:T(8,128)}, bf16[1024,768]{1,0:T(8,128)(2,1)}) custom-call(s32[1]{0:T(128)} %bitcast.31.shard.index, bf16[1536,2048]{1,0:T(8,128)(2,1)} %bitcast.173, bf16[1536,2048]{1,0:T(8,128)(2,1)} %bitcast.187, bf16[1536,512]{1,0:T(8,128)(2,1)S(1)} %get-tuple-element.79.inner_grad.refs_0_.refs_4_, ...), custom_call_target="tpu_custom_call" | custom-call | flops 1024 | bytes 1024 | tf_op jit(solution)/shard_map/gradient_parts/pallas_call | solution.py:983
  248.7 12.5 %gradient_parts.8 = (f32[1024,768]{1,0:T(8,128)}, bf16[1024,768]{1,0:T(8,128)(2,1)}) custom-call(s32[1]{0:T(128)} %bitcast.31.shard.index, bf16[1536,2048]{1,0:T(8,128)(2,1)} %bitcast.175, bf16[1536,2048]{1,0:T(8,128)(2,1)} %bitcast.189, bf16[1536,512]{1,0:T(8,128)(2,1)S(1)} %get-tuple-element.83.inner_grad.refs_1_.refs_5_, ...), custom_call_target="tpu_custom_call" | custom-call | flops 1024 | bytes 1024 | tf_op jit(solution)/shard_map/gradient_parts/pallas_call | solution.py:983
  276.6 16.3 %shared_weights.1 = (bf16[1024,768]{1,0:T(8,128)(2,1)S(1)}, bf16[1024,768]{1,0:T(8,128)(2,1)S(1)}, bf16[1024,768]{1,0:T(8,128)(2,1)S(1)}) custom-call(s32[1]{0:T(128)} %bitcast.3.index, bf16[1024,64,128]{2,1,0:T(8,128)(2,1)} %bitcast.201, bf16[1024,64,128]{2,1,0:T(8,128)(2,1)} %bitcast.202, bf16[1024,64,128]{2,1,0:T(8,128)(2,1)} %bitcast.203, ...), custom_call_target="tpu_custom_call" | custom-call | flops 1024 | bytes 1024 | tf_op jit(solution)/shard_map/shared_weights/pallas_call | solution.py:686
  296.4 10.3 %expert_step.9 = (bf16[1536,256]{1,0:T(8,128)(2,1)S(1)}, bf16[1536,512]{1,0:T(8,128)(2,1)S(1)}, f32[1536,128]{1,0:T(8,128)S(1)}) custom-call(s32[1]{0:T(128)} %bitcast.31.shard.index, bf16[1536,2048]{1,0:T(8,128)(2,1)} %bitcast.176, bf16[1536,2048]{1,0:T(8,128)(2,1)} %bitcast.190, ...), custom_call_target="tpu_custom_call" | custom-call | flops 1024 | bytes 1024 | tf_op jit(solution)/shard_map/expert_step/pallas_call | solution.py:903
  307.7 12.2 %gradient_parts.9 = (f32[1024,768]{1,0:T(8,128)}, bf16[1024,768]{1,0:T(8,128)(2,1)S(1)}) custom-call(s32[1]{0:T(128)} %bitcast.31.shard.index, bf16[1536,2048]{1,0:T(8,128)(2,1)} %bitcast.177, bf16[1536,2048]{1,0:T(8,128)(2,1)} %bitcast.191, bf16[1536,512]{1,0:T(8,128)(2,1)S(1)} %get-tuple-element.89.inner_grad.refs_2_.refs_6_, ...), custom_call_target="tpu_custom_call" | custom-call | flops 1024 | bytes 1024 | tf_op jit(solution)/shard_map/gradient_parts/pallas_call | solution.py:983
  320.0 11.1 %expert_step.10 = (bf16[1536,256]{1,0:T(8,128)(2,1)S(1)}, bf16[1536,512]{1,0:T(8,128)(2,1)S(1)}, f32[1536,128]{1,0:T(8,128)S(1)}) custom-call(s32[1]{0:T(128)} %bitcast.31.shard.index, bf16[1536,2048]{1,0:T(8,128)(2,1)} %bitcast.178, bf16[1536,2048]{1,0:T(8,128)(2,1)} %bitcast.192, ...), custom_call_target="tpu_custom_call" | custom-call | flops 1024 | bytes 1024 | tf_op jit(solution)/shard_map/expert_step/pallas_call | solution.py:903
  337.4 11.7 %gradient_parts.10 = (f32[1024,768]{1,0:T(8,128)}, bf16[1024,768]{1,0:T(8,128)(2,1)}) custom-call(s32[1]{0:T(128)} %bitcast.31.shard.index, bf16[1536,2048]{1,0:T(8,128)(2,1)} %bitcast.179, bf16[1536,2048]{1,0:T(8,128)(2,1)} %bitcast.193, bf16[1536,512]{1,0:T(8,128)(2,1)S(1)} %get-tuple-element.92.inner_grad.refs_3_.refs_7_, ...), custom_call_target="tpu_custom_call" | custom-call | flops 1024 | bytes 1024 | tf_op jit(solution)/shard_map/gradient_parts/pallas_call | solution.py:983
  351.0 19.9 %combine.2 = bf16[1536,2176]{1,0:T(8,128)(2,1)} custom-call(bf16[1536,512]{1,0:T(8,128)(2,1)} %copy-done.9, bf16[1536,512]{1,0:T(8,128)(2,1)} %copy-done.10, bf16[1536,512]{1,0:T(8,128)(2,1)} %copy-done.11, bf16[1536,512]{1,0:T(8,128)(2,1)} %copy-done.12, bf16[1536,512]{1,0:T(8,128)(2,1)} %copy-done.9, bf16[1536,512]{1,0:T(8,128)(2,1)} %copy-done.10, ...), custom_call_target="tpu_custom_call" | custom-call | flops 1024 | bytes 1024 | tf_op jit(solution)/shard_map/combine/pallas_call | solution.py:940
  371.0 101.1 %scatter_rows.2 = (f32[96,2176]{1,0:T(8,128)S(1)}, bf16[1024,768]{1,0:T(8,128)(2,1)S(1)}, bf16[1024,768]{1,0:T(8,128)(2,1)S(1)}) custom-call(bf16[4,4,96,2176]{3,2,1,0:T(8,128)(2,1)} %bitcast.208, bf16[1024,768]{1,0:T(8,128)(2,1)S(1)} %copy-done.3, bf16[1024,768]{1,0:T(8,128)(2,1)} %copy-done), custom_call_target="tpu_custom_call" | custom-call | flops 1024 | bytes 1024 | tf_op jit(solution)/shard_map/scatter_rows/pallas_call | solution.py:422
  511.5 13.7 %collective-permute-done.16 = bf16[4,96,128]{2,1,0:T(8,128)(2,1)S(1)} collective-permute-done((bf16[4,96,128]{2,1,0:T(8,128)(2,1)S(1)}, bf16[4,96,128]{2,1,0:T(8,128)(2,1)S(1)}, u32[]{:S(2)}, u32[]{:S(2)}) %collective-permute-start.16) | collective-permute-done | bytes 98336 | tf_op jit(solution)/shard_map/ppermute | solution.py:30
  525.4 13.2 %attend_back.1 = (bf16[1536,384]{1,0:T(8,128)(2,1)S(1)}, f32[8,128]{1,0:T(8,128)S(1)}) custom-call(bf16[1536,128]{1,0:T(8,128)(2,1)S(1)} %get-tuple-element.72.query, bf16[1536,128]{1,0:T(8,128)(2,1)S(1)} %copy-done.30, bf16[1536,128]{1,0:T(8,128)(2,1)S(1)} %copy-done.32, f32[1536,256]{1,0:T(8,128)} %copy-done.28, f32[1536,128]{1,0:T(8,128)S(1)} %copy-done.17, ...), custom_call_target="tpu_custom_call" | custom-call | flops 1024 | bytes 1024 | tf_op jit(solution)/shard_map/attend_back/pallas_call | solution.py:833
  556.9 11.3 %expert_step.11 = (bf16[1536,256]{1,0:T(8,128)(2,1)S(1)}, bf16[1536,512]{1,0:T(8,128)(2,1)S(1)}, f32[1536,128]{1,0:T(8,128)}) custom-call(s32[1]{0:T(128)} %bitcast.31.shard.index, bf16[1536,2048]{1,0:T(8,128)(2,1)} %bitcast.180, bf16[1536,2048]{1,0:T(8,128)(2,1)} %bitcast.194, bf16[1024,768]{1,0:T(8,128)(2,1)} %copy-done.2, bf16[1024,768]{1,0:T(8,128)(2,1)} %copy-done.8, ...), custom_call_target="tpu_custom_call" | custom-call | flops 1024 | bytes 1024 | tf_op jit(solution)/shard_map/expert_step/pallas_call | solution.py:903
  568.1 11.9 %gradient_parts.11 = (f32[1024,768]{1,0:T(8,128)}, bf16[1024,768]{1,0:T(8,128)(2,1)}) custom-call(s32[1]{0:T(128)} %bitcast.31.shard.index, bf16[1536,2048]{1,0:T(8,128)(2,1)} %bitcast.181, bf16[1536,2048]{1,0:T(8,128)(2,1)} %bitcast.195, bf16[1536,512]{1,0:T(8,128)(2,1)S(1)} %get-tuple-element.107.inner_grad, bf16[1536,256]{1,0:T(8,128)(2,1)S(1)} %get-tuple-element.108.scaled), custom_call_target="tpu_custom_call" | custom-call | flops 1024 | bytes 1024 | tf_op jit(solution)/shard_map/gradient_parts/pallas_call | solution.py:983
  593.1 10.6 %expert_step.12 = (bf16[1536,256]{1,0:T(8,128)(2,1)S(1)}, bf16[1536,512]{1,0:T(8,128)(2,1)S(1)}, f32[1536,128]{1,0:T(8,128)}) custom-call(s32[1]{0:T(128)} %bitcast.31.shard.index, bf16[1536,2048]{1,0:T(8,128)(2,1)} %bitcast.182, bf16[1536,2048]{1,0:T(8,128)(2,1)} %bitcast.196, bf16[1024,768]{1,0:T(8,128)(2,1)S(1)} %copy-done.1, ...), custom_call_target="tpu_custom_call" | custom-call | flops 1024 | bytes 1024 | tf_op jit(solution)/shard_map/expert_step/pallas_call | solution.py:903
  603.7 11.6 %gradient_parts.12 = (f32[1024,768]{1,0:T(8,128)}, bf16[1024,768]{1,0:T(8,128)(2,1)S(1)}) custom-call(s32[1]{0:T(128)} %bitcast.31.shard.index, bf16[1536,2048]{1,0:T(8,128)(2,1)} %bitcast.183, bf16[1536,2048]{1,0:T(8,128)(2,1)} %bitcast.197, bf16[1536,512]{1,0:T(8,128)(2,1)S(1)} %get-tuple-element.111.inner_grad, ...), custom_call_target="tpu_custom_call" | custom-call | flops 1024 | bytes 1024 | tf_op jit(solution)/shard_map/gradient_parts/pallas_call | solution.py:983
  616.5 10.7 %expert_step.13 = (bf16[1536,256]{1,0:T(8,128)(2,1)S(1)}, bf16[1536,512]{1,0:T(8,128)(2,1)S(1)}, f32[1536,128]{1,0:T(8,128)}) custom-call(s32[1]{0:T(128)} %bitcast.31.shard.index, bf16[1536,2048]{1,0:T(8,128)(2,1)} %bitcast.184, bf16[1536,2048]{1,0:T(8,128)(2,1)} %bitcast.198, bf16[1024,768]{1,0:T(8,128)(2,1)S(1)} %copy-done.5, ...), custom_call_target="tpu_custom_call" | custom-call | flops 1024 | bytes 1024 | tf_op jit(solution)/shard_map/expert_step/pallas_call | solution.py:903
  627.2 11.5 %gradient_parts.13 = (f32[1024,768]{1,0:T(8,128)}, bf16[1024,768]{1,0:T(8,128)(2,1)S(1)}) custom-call(s32[1]{0:T(128)} %bitcast.31.shard.index, bf16[1536,2048]{1,0:T(8,128)(2,1)} %bitcast.185, bf16[1536,2048]{1,0:T(8,128)(2,1)} %bitcast.199, bf16[1536,512]{1,0:T(8,128)(2,1)S(1)} %get-tuple-element.114.inner_grad, ...), custom_call_target="tpu_custom_call" | custom-call | flops 1024 | bytes 1024 | tf_op jit(solution)/shard_map/gradient_parts/pallas_call | solution.py:983
  649.0 11.8 %combine.3 = bf16[1536,2048]{1,0:T(8,128)(2,1)} custom-call(bf16[1536,256]{1,0:T(8,128)(2,1)} %copy-done.24, bf16[1536,256]{1,0:T(8,128)(2,1)} %copy-done.25, bf16[1536,256]{1,0:T(8,128)(2,1)} %copy-done.26, bf16[1536,256]{1,0:T(8,128)(2,1)} %copy-done.27, bf16[2048,768]{1,0:T(8,128)(2,1)} %all-gather.13.cloned.1.call-done.refs_0_.refs_1_.refs_2_.refs_8_.refs_12_.refs_4_, ...), custom_call_target="tpu_custom_call" | custom-call | flops 1024 | bytes 1024 | tf_op jit(solution)/shard_map/combine/pallas_call | solution.py:940
  663.7 139.9 %scatter_rows.3 = (f32[96,2048]{1,0:T(8,128)S(1)}, f32[96,2048]{1,0:T(8,128)S(1)}, bf16[1024,768]{1,0:T(8,128)(2,1)S(1)}, bf16[1024,768]{1,0:T(8,128)(2,1)S(1)}, f32[24,2048]{1,0:T(8,128)S(1)}) custom-call(bf16[4,4,96,2048]{3,2,1,0:T(8,128)(2,1)} %bitcast.217, bf16[4,4,96,2048]{3,2,1,0:T(8,128)(2,1)} %bitcast.214, bf16[1024,768]{1,0:T(8,128)(2,1)} %copy-done.22, ...), custom_call_target="tpu_custom_call" | custom-call | flops 1024 | bytes 1024 | tf_op jit(solution)/shard_map/scatter_rows/pallas_call | solution.py:422
  815.6 27.7 %expert_gradients.1 = (f32[65536,128]{1,0:T(8,128)}, f32[32768,128]{1,0:T(8,128)}) custom-call(s32[1]{0:T(128)} %bitcast.3.index, bf16[4,1024,768]{2,1,0:T(8,128)(2,1)} %bitcast.219, bf16[4,1024,768]{2,1,0:T(8,128)(2,1)} %bitcast.213, bf16[4,1024,768]{2,1,0:T(8,128)(2,1)} %bitcast.220, bf16[4,1024,768]{2,1,0:T(8,128)(2,1)} %pad_maximum_fusion.refs_3_.refs_4_.refs_5_.refs_6_, ...), custom_call_target="tpu_custom_call" | custom-call | flops 1024 | bytes 1024 | tf_op jit(solution)/shard_map/expert_gradients/pallas_call | solution.py:1047
  (467 shorter events, 238.4 us)
Async XLA Ops:
  7.2 96.9 %all-gather.11.cloned.1.call-start = ((), (), s32[]{:S(2)}) async-start(), calls=%async_computation | async-start | bytes 2359296 | tf_op jit(solution)/shard_map/all_gather | solution.py:495
  22.6 188.6 %all-gather.13.cloned.1.call-start = ((), (), s32[]{:S(2)}) async-start(), calls=%async_computation.1 | async-start | bytes 4718592 | tf_op jit(solution)/shard_map/all_gather | solution.py:495
  23.4 214.1 %all-gather.15.cloned.1.call-start = ((), (), s32[]{:S(2)}) async-start(), calls=%async_computation.2 | async-start | bytes 14155776 | tf_op jit(solution)/shard_map/all_gather | solution.py:495
  23.4 80.5 %collective-permute-start.8 = (s32[384,8]{0,1:T(8,128)S(1)}, s32[384,8]{0,1:T(8,128)S(1)}, u32[]{:S(2)}, u32[]{:S(2)}) collective-permute-start(s32[384,8]{0,1:T(8,128)S(1)} %bitcast.244), channel_id=1, source_target_pairs={{4,0},{8,4},{12,8},{0,12},{5,1},{9,5},{13,9},{1,13},{6,2},{10,6},{... | collective-permute-start | bytes 36872 | tf_op jit(solution)/shard_map/ppermute | solution.py:30
  28.5 75.4 %collective-permute-start.9 = (s32[384,8]{0,1:T(8,128)S(1)}, s32[384,8]{0,1:T(8,128)S(1)}, u32[]{:S(2)}, u32[]{:S(2)}) collective-permute-start(s32[384,8]{0,1:T(8,128)S(1)} %bitcast.245), channel_id=1, source_target_pairs={{8,0},{12,4},{0,8},{4,12},{9,1},{13,5},{1,9},{5,13},{10,2},{14,6},... | collective-permute-start | bytes 36872 | tf_op jit(solution)/shard_map/ppermute | solution.py:30
  28.5 75.4 %collective-permute-start.10 = (s32[384,8]{0,1:T(8,128)S(1)}, s32[384,8]{0,1:T(8,128)S(1)}, u32[]{:S(2)}, u32[]{:S(2)}) collective-permute-start(s32[384,8]{0,1:T(8,128)S(1)} %bitcast.246), channel_id=1, source_target_pairs={{12,0},{0,4},{4,8},{8,12},{13,1},{1,5},{5,9},{9,13},{14,2},{2,6},{... | collective-permute-start | bytes 36872 | tf_op jit(solution)/shard_map/ppermute | solution.py:30
  29.6 73.0 %collective-permute-start = (bf16[2,1024]{1,0:T(2,128)(2,1)S(1)}, bf16[2,1024]{1,0:T(2,128)(2,1)S(1)}, u32[]{:S(2)}, u32[]{:S(2)}) collective-permute-start(bf16[2,1024]{1,0:T(2,128)(2,1)S(1)} %pad_maximum_fusion.12), channel_id=1, source_target_pairs={{16,0},{0,16},{17,1},{1,17},{18,2},{2,18},{19,3},{3,19},{20,4},{4,... | collective-permute-start | bytes 12296 | tf_op jit(solution)/shard_map/ppermute | solution.py:30
  31.2 69.8 %collective-permute-start.1 = (bf16[1,128]{1,0:T(2,128)(2,1)S(1)}, bf16[1,128]{1,0:T(2,128)(2,1)S(1)}, u32[]{:S(2)}, u32[]{:S(2)}) collective-permute-start(bf16[1,128]{1,0:T(2,128)(2,1)S(1)} %bitcast.260), channel_id=1, source_target_pairs={{16,0},{0,16},{17,1},{1,17},{18,2},{2,18},{19,3},{3,19},{20,4},{4,... | collective-permute-start | bytes 776 | tf_op jit(solution)/shard_map/ppermute | solution.py:30
  31.7 445.9 %all-gather.19.cloned.1.call-start = ((), (), s32[]{:S(2)}) async-start(), calls=%async_computation.4 | async-start | bytes 7864320 | tf_op jit(solution)/shard_map/all_gather | solution.py:1195
  102.6 62.0 %collective-permute-start.11 = (bf16[1024,16]{0,1:T(8,128)(2,1)}, bf16[1024,16]{0,1:T(8,128)(2,1)}, u32[]{:S(2)}, u32[]{:S(2)}) collective-permute-start(bf16[1024,16]{0,1:T(8,128)(2,1)} %param.21), channel_id=1, source_target_pairs={{16,0},{0,16},{17,1},{1,17},{18,2},{2,18},{19,3},{3,19},{20,4},{4,... | collective-permute-start | bytes 98312 | tf_op jit(solution)/shard_map/ppermute | solution.py:30
  274.3 317.7 %all-gather.21.cloned.1.call-start = ((), (), s32[]{:S(2)}) async-start(), calls=%async_computation.5 | async-start | bytes 7864320 | tf_op jit(solution)/shard_map/all_gather | solution.py:1195
  274.8 58.4 %collective-permute-start.20 = (bf16[1024,768]{1,0:T(8,128)(2,1)}, bf16[1024,768]{1,0:T(8,128)(2,1)S(1)}, u32[]{:S(2)}, u32[]{:S(2)}) collective-permute-start(bf16[1024,768]{1,0:T(8,128)(2,1)} %get-tuple-element.85.refs_6_.refs_5_), channel_id=1, source_target_pairs={{16,0},{0,16},{17,1},{1,17},{18,2},{2,18},{19,3},{3,19},{20,4},{4,... | collective-permute-start | bytes 4718600 | tf_op jit(solution)/shard_map/ppermute | solution.py:30
  334.8 480.9 %all-gather.23.cloned.1.call-start = ((), (), s32[]{:S(2)}) async-start(), calls=%async_computation.6 | async-start | bytes 7864320 | tf_op jit(solution)/shard_map/all_gather | solution.py:1195
  334.8 139.6 %collective-permute-start.21 = (bf16[1024,768]{1,0:T(8,128)(2,1)}, bf16[1024,768]{1,0:T(8,128)(2,1)}, u32[]{:S(2)}, u32[]{:S(2)}) collective-permute-start(bf16[1024,768]{1,0:T(8,128)(2,1)} %copy-done.35), channel_id=1, source_target_pairs={{16,0},{0,16},{17,1},{1,17},{18,2},{2,18},{19,3},{3,19},{20,4},{4,... | collective-permute-start | bytes 4718600 | tf_op jit(solution)/shard_map/ppermute | solution.py:30
  349.1 146.8 %collective-permute-start.22 = (bf16[1024,768]{1,0:T(8,128)(2,1)}, bf16[1024,768]{1,0:T(8,128)(2,1)}, u32[]{:S(2)}, u32[]{:S(2)}) collective-permute-start(bf16[1024,768]{1,0:T(8,128)(2,1)} %get-tuple-element.98.refs_20_), channel_id=1, source_target_pairs={{16,0},{0,16},{17,1},{1,17},{18,2},{2,18},{19,3},{3,19},{20,4},{4,... | collective-permute-start | bytes 4718600 | tf_op jit(solution)/shard_map/ppermute | solution.py:30
  477.4 373.5 %all-gather.17.cloned.1.call-start = ((), (), s32[]{:S(2)}) async-start(), calls=%async_computation.3 | async-start | bytes 5242880 | tf_op jit(solution)/shard_map/all_gather | solution.py:1250
  494.7 94.4 %collective-permute-start.18 = (bf16[1024,768]{1,0:T(8,128)(2,1)S(1)}, bf16[1024,768]{1,0:T(8,128)(2,1)}, u32[]{:S(2)}, u32[]{:S(2)}) collective-permute-start(bf16[1024,768]{1,0:T(8,128)(2,1)S(1)} %copy-done.5), channel_id=1, source_target_pairs={{16,0},{0,16},{17,1},{1,17},{18,2},{2,18},{19,3},{3,19},{20,4},{4,... | collective-permute-start | bytes 4718600 | tf_op jit(solution)/shard_map/ppermute | solution.py:30
  509.4 45.1 %collective-permute-start.19 = (bf16[1024,512]{1,0:T(8,128)(2,1)S(1)}, bf16[1024,512]{1,0:T(8,128)(2,1)S(1)}, u32[]{:S(2)}, u32[]{:S(2)}) collective-permute-start(bf16[1024,512]{1,0:T(8,128)(2,1)S(1)} %convolution_convert_fusion.1), channel_id=1, source_target_pairs={{16,0},{0,16},{17,1},{1,17},{18,2},{2,18},{19,3},{3,19},{20,4},{4,... | collective-permute-start | bytes 3145736 | tf_op jit(solution)/shard_map/ppermute | solution.py:30
  543.6 98.7 %collective-permute-start.23 = (bf16[1024,384]{1,0:T(8,128)(2,1)}, bf16[1024,384]{1,0:T(8,128)(2,1)}, u32[]{:S(2)}, u32[]{:S(2)}) collective-permute-start(bf16[1024,384]{1,0:T(8,128)(2,1)} %fusion.11.refs_9_), channel_id=1, source_target_pairs={{16,0},{0,16},{17,1},{1,17},{18,2},{2,18},{19,3},{3,19},{20,4},{4,... | collective-permute-start | bytes 2359304 | tf_op jit(solution)/shard_map/ppermute | solution.py:30
  580.0 80.8 %collective-permute-start.27 = (bf16[1024,768]{1,0:T(8,128)(2,1)}, bf16[1024,768]{1,0:T(8,128)(2,1)}, u32[]{:S(2)}, u32[]{:S(2)}) collective-permute-start(bf16[1024,768]{1,0:T(8,128)(2,1)} %get-tuple-element.109.refs_8_), channel_id=1, source_target_pairs={{16,0},{0,16},{17,1},{1,17},{18,2},{2,18},{19,3},{3,19},{20,4},{4,... | collective-permute-start | bytes 4718600 | tf_op jit(solution)/shard_map/ppermute | solution.py:30
  587.9 57.4 %collective-permute-start.24 = (bf16[1024,128]{1,0:T(8,128)(2,1)}, bf16[1024,128]{1,0:T(8,128)(2,1)}, u32[]{:S(2)}, u32[]{:S(2)}) collective-permute-start(bf16[1024,128]{1,0:T(8,128)(2,1)} %get-tuple-element.146), channel_id=1, source_target_pairs={{12,0},{0,4},{4,8},{8,12},{13,1},{1,5},{5,9},{9,13},{14,2},{2,6},{... | collective-permute-start | bytes 786440 | tf_op jit(solution)/shard_map/ppermute | solution.py:30
  588.9 56.5 %collective-permute-start.25 = (bf16[1024,128]{1,0:T(8,128)(2,1)}, bf16[1024,128]{1,0:T(8,128)(2,1)}, u32[]{:S(2)}, u32[]{:S(2)}) collective-permute-start(bf16[1024,128]{1,0:T(8,128)(2,1)} %get-tuple-element.148), channel_id=1, source_target_pairs={{8,0},{12,4},{0,8},{4,12},{9,1},{13,5},{1,9},{5,13},{10,2},{14,6},... | collective-permute-start | bytes 786440 | tf_op jit(solution)/shard_map/ppermute | solution.py:30
  589.1 56.2 %collective-permute-start.26 = (bf16[1024,128]{1,0:T(8,128)(2,1)}, bf16[1024,128]{1,0:T(8,128)(2,1)}, u32[]{:S(2)}, u32[]{:S(2)}) collective-permute-start(bf16[1024,128]{1,0:T(8,128)(2,1)} %get-tuple-element.147), channel_id=1, source_target_pairs={{4,0},{8,4},{12,8},{0,12},{5,1},{9,5},{13,9},{1,13},{6,2},{10,6},{... | collective-permute-start | bytes 786440 | tf_op jit(solution)/shard_map/ppermute | solution.py:30
  803.7 40.3 %collective-permute-start.32 = (f32[18,1024]{1,0:T(8,128)S(1)}, f32[18,1024]{1,0:T(8,128)S(1)}, u32[]{:S(2)}, u32[]{:S(2)}) collective-permute-start(f32[18,1024]{1,0:T(8,128)S(1)} %constant_dynamic-slice_fusion.5), channel_id=1, source_target_pairs={{16,0},{0,16},{17,1},{1,17},{18,2},{2,18},{19,3},{3,19},{20,4},{4,... | collective-permute-start | bytes 221192 | tf_op jit(solution)/shard_map/ppermute | solution.py:30
  (138 other events, 2021.8 us)
Sparse Core Ops, SparseCore 0:
  22.7 29.9 all-gather.10
  54.8 44.9 all-gather.12
  101.9 126.7 all-gather.14
  274.4 113.7 all-gather.18
  389.6 136.5 all-gather.20
  527.7 135.7 all-gather.22
  665.1 135.3 all-gather.16

commit v6 on v5

--- a/solution.py
+++ b/solution.py
@@ -1129,7 +1129,7 @@
     tokens_all, cot_all = tokens_all.reshape(every, width), cot_all.reshape(every, width)
     head_in = gather_natural(head_in, "shard")
     first_weights, others = gather_natural(first_weights, "shard"), gather_natural(others, "shard")
-    exit_weight = gather_small(exit_weight, 0)
+    exit_weights = [exit_weight] + [receive(exit_weight, "shard", r) for r in range(1, shards)]
     first = t * own
     tokens_own = lax.dynamic_slice_in_dim(tokens[0], first, own)
     cot_own = lax.dynamic_slice_in_dim(cotangent[0], first, own)
@@ -1159,7 +1159,8 @@
     blocks = ahead_first(mixed_head.reshape(tps, ctxs, own, head_size), c, 1)
     mixed = [blocks[:, 0]] + [receive(blocks[:, ctxs - j], "ctx", j) for j in range(1, ctxs)]
     mixed = jnp.concatenate([m.reshape(rows, head_size) for m in mixed], axis=1)
-    residual = layer_in + scatter_tp(dot(mixed, exit_weight, (1, 1)))
+    attended = scatter_tp(jnp.concatenate([dot(mixed, w, (1, 1)) for w in exit_weights], axis=1))
+    residual = layer_in + ahead_first(attended, lax.rem(shards - s, shards) * block, 1)
 
     normed_two = lower(residual * inverse_scale(residual) * gain_two)
     normed_two_all = gather_rows([normed_two], 0)[0].reshape(every, width)
@@ -1191,7 +1192,7 @@
     chunks, gathered = [], []
     for i in range(last):
         own_part, far = products[i]
-        chunks.append(lower(product_sum(tie(own_part, inner_grads[last] if i else products[1][1][0]), far)))
+        chunks.append(lower(product_sum(tie(own_part, inner_grads[i + 1] if i else products[1][1][0]), far)))
         gathered.append(lax.all_gather(chunks[i], "ctx", axis=0, tiled=False))
     columns = lambda k: [(others if i else first_weights, 3 * max(i - 1, 0) + k) for i in range(group)]
     normed_part = combine(
@@ -1214,8 +1215,10 @@
     residual_grad = upstream + residual_back
 
     attend_grad = gather_tp(lower(residual_grad))
-    exit_parts = product_parts([([own_block(attend_grad, r, 1) for r in range(shards)], mixed)])
-    mixed_grad = lower(dot(attend_grad, exit_weight, (1, 0))).reshape(tps, own, ctxs, head_size)
+    attend_blocks = [own_block(attend_grad, r, 1) for r in range(shards)]
+    exit_parts = product_parts([(attend_blocks, mixed)])
+    mixed_grad = lower(sum(dot(v, w, (1, 0)) for v, w in zip(attend_blocks, exit_weights)))
+    mixed_grad = mixed_grad.reshape(tps, own, ctxs, head_size)
     parts = [mixed_grad[:, :, 0]] + [receive(mixed_grad[:, :, ctxs - j], "ctx", j) for j in range(1, ctxs)]
     mixed_grad = ahead_first(jnp.stack(parts, axis=1), lax.rem(ctxs - c, ctxs), 1)
     mixed_grad = mixed_grad.reshape(every, HEAD_DIM)

time: 878 us -> 868 us (0.989)
    pallas_call x2, Pallas kernels: 241 us -> 230 us  [scatter_rows(): pl.pallas_call(functools.partial(scatter_kernel, size, arrays, tuple((ahe...]
    dot_general x11 -> x13, matrix products: 27 us -> 31.1 us  [dot(): lax.dot_general(left, right, (((over[0],), (over[1],)), ((), ())), prefer...]
    unnamed x257 -> x203, local copies, waits for them, and re-layouts: 25.2 us -> 24 us
  transfers between devices with their start and end apart: 41 -> 41, of which waited for: 9 -> 13; matrix products, arithmetic and copies ran while one was open for 11% -> 11% of each run, Pallas kernels for 70% -> 70%
where the time goes in v6:
time: 868 us; the launch traced here: 856 us
  Pallas kernels  620 us (71%)
  waiting for transfers between devices  59.4 us (7%)
  other arithmetic  46.8 us (5%)
  local copies, waits for them, and re-layouts  39.7 us (5%)
  starting transfers between devices  38.6 us (4%)
  matrix products  31.1 us (4%)
  between operations  20.1 us (2%)
    pallas_call x2, Pallas kernels, scatter_rows(): pl.pallas_call(functools.partial(scatter_kernel, size, arrays, tuple((ahe...  230 us
    pallas_call x2, Pallas kernels, gather_rows(): pl.pallas_call(functools.partial(gather_kernel, size, pieces, arrays, sha...  103 us
    pallas_call x7, Pallas kernels, gradient_parts(): pl.pallas_call(functools.partial(gradient_kernel, steps), grid_spec=pltpu...  85.4 us
    pallas_call x7, Pallas kernels, expert_step(): pl.pallas_call(functools.partial(expert_step_kernel, index, parts, len(ea...  74.9 us
    ppermute x26, waiting for transfers between devices, receive(): lax.ppermute(values, axis, [((i + distance) % size, i) for i in range(siz...  44.9 us
    ppermute x26, starting transfers between devices, receive(): lax.ppermute(values, axis, [((i + distance) % size, i) for i in range(siz...  33.3 us
    pallas_call x2, Pallas kernels, combine(): pl.pallas_call(lambda *refs: combine_kernel(len(lefts), len(lanes), *refs...  31.8 us
    dot_general x13, matrix products, dot(): lax.dot_general(left, right, (((over[0],), (over[1],)), ((), ())), prefer...  31.1 us
  transfers between devices with their start and end apart: 41, of which 13 were waited for; matrix products, arithmetic and copies ran while one was open for 11% of the time, Pallas kernels for 70%

profile of v6, /device:TPU:0, one launch (start us, length us, event | category | flops | bytes accessed | tf_op | source)
XLA Modules:
  0.0 855.9 jit_solution(18306967216078395567)
XLA Ops:
  8.5 13.2 %own_weights.1 = (bf16[1024,768]{1,0:T(8,128)(2,1)}, bf16[1024,2304]{1,0:T(8,128)(2,1)}, bf16[1024,384]{1,0:T(8,128)(2,1)}, bf16[1024,512]{1,0:T(8,128)(2,1)S(1)}) custom-call(s32[1]{0:T(128)} %bitcast.3.index, bf16[1024,64,128]{2,1,0:T(8,128)(2,1)} %bitcast.203, bf16[1024,32,128]{2,1,0:T(8,128)(2,1)} %bitcast.207, bf16[3,1024,512]{2,1,0:T(8,128)(2,1)} %bitcast.225, ...), custom_call_target="tpu_custom_call" | custom-call | flops 1024 | bytes 1024 | tf_op jit(solution)/shard_map/own_weights/pallas_call | solution.py:617
  39.0 64.1 %gather_rows.2 = (bf16[4,4,96,2048]{3,2,1,0:T(8,128)(2,1)}, bf16[4,4,96,2048]{3,2,1,0:T(8,128)(2,1)}) custom-call(bf16[384,2048]{1,0:T(8,128)(2,1)} %bitcast.224, bf16[384,2048]{1,0:T(8,128)(2,1)} %bitcast.227, bf16[1024,384]{1,0:T(8,128)(2,1)} %get-tuple-element.70.refs_2_), custom_call_target="tpu_custom_call" | custom-call | flops 1024 | bytes 1024 | tf_op jit(solution)/shard_map/gather_rows/pallas_call | solution.py:233
  109.5 10.5 %project.1 = (bf16[1536,2048]{1,0:T(8,128)(2,1)}, f32[1536,256]{1,0:T(8,128)S(1)}, bf16[1536,128]{1,0:T(8,128)(2,1)S(1)}, bf16[1536,128]{1,0:T(8,128)(2,1)S(1)}, bf16[1536,128]{1,0:T(8,128)(2,1)S(1)}) custom-call(bf16[1536,2048]{1,0:T(8,128)(2,1)} %bitcast.212, f32[1,2048]{1,0:T(1,128)S(1)} %get-tuple-element.164.gain, bf16[2048,384]{1,0:T(8,128)(2,1)S(1)} %copy-done.37, ...), custom_call_target="tpu_custom_call" | custom-call | flops 1024 | bytes 1024 | tf_op jit(solution)/shard_map/project/pallas_call | solution.py:732
  165.2 38.9 %gather_rows.3 = bf16[4,4,96,2048]{3,2,1,0:T(8,128)(2,1)} custom-call(bf16[96,2048]{1,0:T(8,128)(2,1)} %multiply_convert_fusion.refs_0_), custom_call_target="tpu_custom_call" | custom-call | flops 1024 | bytes 1024 | tf_op jit(solution)/shard_map/gather_rows/pallas_call | solution.py:233
  221.4 12.8 %gradient_parts.7 = (f32[1024,768]{1,0:T(8,128)}, bf16[1024,768]{1,0:T(8,128)(2,1)}) custom-call(s32[1]{0:T(128)} %bitcast.31.shard.index, bf16[1536,2048]{1,0:T(8,128)(2,1)} %bitcast.176, bf16[1536,2048]{1,0:T(8,128)(2,1)} %bitcast.190, bf16[1536,512]{1,0:T(8,128)(2,1)S(1)} %get-tuple-element.79.inner_grad.refs_0_.refs_4_, ...), custom_call_target="tpu_custom_call" | custom-call | flops 1024 | bytes 1024 | tf_op jit(solution)/shard_map/gradient_parts/pallas_call | solution.py:983
  247.2 12.9 %gradient_parts.8 = (f32[1024,768]{1,0:T(8,128)}, bf16[1024,768]{1,0:T(8,128)(2,1)}) custom-call(s32[1]{0:T(128)} %bitcast.31.shard.index, bf16[1536,2048]{1,0:T(8,128)(2,1)} %bitcast.178, bf16[1536,2048]{1,0:T(8,128)(2,1)} %bitcast.192, bf16[1536,512]{1,0:T(8,128)(2,1)S(1)} %get-tuple-element.83.inner_grad.refs_1_.refs_5_, ...), custom_call_target="tpu_custom_call" | custom-call | flops 1024 | bytes 1024 | tf_op jit(solution)/shard_map/gradient_parts/pallas_call | solution.py:983
  275.5 16.3 %shared_weights.1 = (bf16[1024,768]{1,0:T(8,128)(2,1)S(1)}, bf16[1024,768]{1,0:T(8,128)(2,1)S(1)}, bf16[1024,768]{1,0:T(8,128)(2,1)S(1)}) custom-call(s32[1]{0:T(128)} %bitcast.3.index, bf16[1024,64,128]{2,1,0:T(8,128)(2,1)} %bitcast.204, bf16[1024,64,128]{2,1,0:T(8,128)(2,1)} %bitcast.205, bf16[1024,64,128]{2,1,0:T(8,128)(2,1)} %bitcast.206, ...), custom_call_target="tpu_custom_call" | custom-call | flops 1024 | bytes 1024 | tf_op jit(solution)/shard_map/shared_weights/pallas_call | solution.py:686
  295.4 10.5 %expert_step.9 = (bf16[1536,256]{1,0:T(8,128)(2,1)S(1)}, bf16[1536,512]{1,0:T(8,128)(2,1)S(1)}, f32[1536,128]{1,0:T(8,128)S(1)}) custom-call(s32[1]{0:T(128)} %bitcast.31.shard.index, bf16[1536,2048]{1,0:T(8,128)(2,1)} %bitcast.179, bf16[1536,2048]{1,0:T(8,128)(2,1)} %bitcast.193, ...), custom_call_target="tpu_custom_call" | custom-call | flops 1024 | bytes 1024 | tf_op jit(solution)/shard_map/expert_step/pallas_call | solution.py:903
  312.2 11.8 %gradient_parts.9 = (f32[1024,768]{1,0:T(8,128)}, bf16[1024,768]{1,0:T(8,128)(2,1)}) custom-call(s32[1]{0:T(128)} %bitcast.31.shard.index, bf16[1536,2048]{1,0:T(8,128)(2,1)} %bitcast.180, bf16[1536,2048]{1,0:T(8,128)(2,1)} %bitcast.194, bf16[1536,512]{1,0:T(8,128)(2,1)S(1)} %get-tuple-element.89.inner_grad.refs_2_.refs_6_, ...), custom_call_target="tpu_custom_call" | custom-call | flops 1024 | bytes 1024 | tf_op jit(solution)/shard_map/gradient_parts/pallas_call | solution.py:983
  327.1 10.7 %expert_step.10 = (bf16[1536,256]{1,0:T(8,128)(2,1)S(1)}, bf16[1536,512]{1,0:T(8,128)(2,1)S(1)}, f32[1536,128]{1,0:T(8,128)S(1)}) custom-call(s32[1]{0:T(128)} %bitcast.31.shard.index, bf16[1536,2048]{1,0:T(8,128)(2,1)} %bitcast.181, bf16[1536,2048]{1,0:T(8,128)(2,1)} %bitcast.195, ...), custom_call_target="tpu_custom_call" | custom-call | flops 1024 | bytes 1024 | tf_op jit(solution)/shard_map/expert_step/pallas_call | solution.py:903
  337.8 12.9 %gradient_parts.10 = (f32[1024,768]{1,0:T(8,128)}, bf16[1024,768]{1,0:T(8,128)(2,1)}) custom-call(s32[1]{0:T(128)} %bitcast.31.shard.index, bf16[1536,2048]{1,0:T(8,128)(2,1)} %bitcast.182, bf16[1536,2048]{1,0:T(8,128)(2,1)} %bitcast.196, bf16[1536,512]{1,0:T(8,128)(2,1)S(1)} %get-tuple-element.92.inner_grad.refs_3_.refs_7_, ...), custom_call_target="tpu_custom_call" | custom-call | flops 1024 | bytes 1024 | tf_op jit(solution)/shard_map/gradient_parts/pallas_call | solution.py:983
  351.3 20.0 %combine.2 = bf16[1536,2176]{1,0:T(8,128)(2,1)} custom-call(bf16[1536,512]{1,0:T(8,128)(2,1)} %copy-done.9, bf16[1536,512]{1,0:T(8,128)(2,1)} %copy-done.10, bf16[1536,512]{1,0:T(8,128)(2,1)} %copy-done.11, bf16[1536,512]{1,0:T(8,128)(2,1)} %copy-done.12, bf16[1536,512]{1,0:T(8,128)(2,1)} %copy-done.9, bf16[1536,512]{1,0:T(8,128)(2,1)} %copy-done.10, ...), custom_call_target="tpu_custom_call" | custom-call | flops 1024 | bytes 1024 | tf_op jit(solution)/shard_map/combine/pallas_call | solution.py:940
  371.3 89.8 %scatter_rows.2 = (f32[96,2176]{1,0:T(8,128)S(1)}, bf16[1024,768]{1,0:T(8,128)(2,1)S(1)}, bf16[1024,768]{1,0:T(8,128)(2,1)S(1)}) custom-call(bf16[4,4,96,2176]{3,2,1,0:T(8,128)(2,1)} %bitcast.211, bf16[1024,768]{1,0:T(8,128)(2,1)S(1)} %copy-done.3, bf16[1024,768]{1,0:T(8,128)(2,1)} %copy-done), custom_call_target="tpu_custom_call" | custom-call | flops 1024 | bytes 1024 | tf_op jit(solution)/shard_map/scatter_rows/pallas_call | solution.py:422
  503.0 15.9 %collective-permute-done.16 = bf16[4,96,128]{2,1,0:T(8,128)(2,1)S(1)} collective-permute-done((bf16[4,96,128]{2,1,0:T(8,128)(2,1)S(1)}, bf16[4,96,128]{2,1,0:T(8,128)(2,1)S(1)}, u32[]{:S(2)}, u32[]{:S(2)}) %collective-permute-start.16) | collective-permute-done | bytes 98336 | tf_op jit(solution)/shard_map/ppermute | solution.py:30
  519.1 13.2 %attend_back.1 = (bf16[1536,384]{1,0:T(8,128)(2,1)S(1)}, f32[8,128]{1,0:T(8,128)S(1)}) custom-call(bf16[1536,128]{1,0:T(8,128)(2,1)S(1)} %copy-done.32, bf16[1536,128]{1,0:T(8,128)(2,1)S(1)} %copy-done.34, bf16[1536,128]{1,0:T(8,128)(2,1)S(1)} %copy-done.36, f32[1536,256]{1,0:T(8,128)} %copy-done.30, f32[1536,128]{1,0:T(8,128)S(1)} %copy-done.17, ...), custom_call_target="tpu_custom_call" | custom-call | flops 1024 | bytes 1024 | tf_op jit(solution)/shard_map/attend_back/pallas_call | solution.py:833
  545.8 11.4 %expert_step.11 = (bf16[1536,256]{1,0:T(8,128)(2,1)S(1)}, bf16[1536,512]{1,0:T(8,128)(2,1)S(1)}, f32[1536,128]{1,0:T(8,128)}) custom-call(s32[1]{0:T(128)} %bitcast.31.shard.index, bf16[1536,2048]{1,0:T(8,128)(2,1)} %bitcast.183, bf16[1536,2048]{1,0:T(8,128)(2,1)} %bitcast.197, bf16[1024,768]{1,0:T(8,128)(2,1)} %copy-done.2, bf16[1024,768]{1,0:T(8,128)(2,1)} %copy-done.8, ...), custom_call_target="tpu_custom_call" | custom-call | flops 1024 | bytes 1024 | tf_op jit(solution)/shard_map/expert_step/pallas_call | solution.py:903
  557.2 11.9 %gradient_parts.11 = (f32[1024,768]{1,0:T(8,128)}, bf16[1024,768]{1,0:T(8,128)(2,1)}) custom-call(s32[1]{0:T(128)} %bitcast.31.shard.index, bf16[1536,2048]{1,0:T(8,128)(2,1)} %bitcast.184, bf16[1536,2048]{1,0:T(8,128)(2,1)} %bitcast.198, bf16[1536,512]{1,0:T(8,128)(2,1)S(1)} %get-tuple-element.107.inner_grad, bf16[1536,256]{1,0:T(8,128)(2,1)S(1)} %get-tuple-element.108.scaled), custom_call_target="tpu_custom_call" | custom-call | flops 1024 | bytes 1024 | tf_op jit(solution)/shard_map/gradient_parts/pallas_call | solution.py:983
  581.9 10.8 %expert_step.12 = (bf16[1536,256]{1,0:T(8,128)(2,1)S(1)}, bf16[1536,512]{1,0:T(8,128)(2,1)S(1)}, f32[1536,128]{1,0:T(8,128)}) custom-call(s32[1]{0:T(128)} %bitcast.31.shard.index, bf16[1536,2048]{1,0:T(8,128)(2,1)} %bitcast.185, bf16[1536,2048]{1,0:T(8,128)(2,1)} %bitcast.199, bf16[1024,768]{1,0:T(8,128)(2,1)S(1)} %copy-done.1, ...), custom_call_target="tpu_custom_call" | custom-call | flops 1024 | bytes 1024 | tf_op jit(solution)/shard_map/expert_step/pallas_call | solution.py:903
  592.7 11.7 %gradient_parts.12 = (f32[1024,768]{1,0:T(8,128)}, bf16[1024,768]{1,0:T(8,128)(2,1)S(1)}) custom-call(s32[1]{0:T(128)} %bitcast.31.shard.index, bf16[1536,2048]{1,0:T(8,128)(2,1)} %bitcast.186, bf16[1536,2048]{1,0:T(8,128)(2,1)} %bitcast.200, bf16[1536,512]{1,0:T(8,128)(2,1)S(1)} %get-tuple-element.111.inner_grad, ...), custom_call_target="tpu_custom_call" | custom-call | flops 1024 | bytes 1024 | tf_op jit(solution)/shard_map/gradient_parts/pallas_call | solution.py:983
  605.5 10.9 %expert_step.13 = (bf16[1536,256]{1,0:T(8,128)(2,1)S(1)}, bf16[1536,512]{1,0:T(8,128)(2,1)S(1)}, f32[1536,128]{1,0:T(8,128)}) custom-call(s32[1]{0:T(128)} %bitcast.31.shard.index, bf16[1536,2048]{1,0:T(8,128)(2,1)} %bitcast.187, bf16[1536,2048]{1,0:T(8,128)(2,1)} %bitcast.201, bf16[1024,768]{1,0:T(8,128)(2,1)S(1)} %copy-done.5, ...), custom_call_target="tpu_custom_call" | custom-call | flops 1024 | bytes 1024 | tf_op jit(solution)/shard_map/expert_step/pallas_call | solution.py:903
  616.5 11.5 %gradient_parts.13 = (f32[1024,768]{1,0:T(8,128)}, bf16[1024,768]{1,0:T(8,128)(2,1)S(1)}) custom-call(s32[1]{0:T(128)} %bitcast.31.shard.index, bf16[1536,2048]{1,0:T(8,128)(2,1)} %bitcast.188, bf16[1536,2048]{1,0:T(8,128)(2,1)} %bitcast.202, bf16[1536,512]{1,0:T(8,128)(2,1)S(1)} %get-tuple-element.114.inner_grad, ...), custom_call_target="tpu_custom_call" | custom-call | flops 1024 | bytes 1024 | tf_op jit(solution)/shard_map/gradient_parts/pallas_call | solution.py:983
  638.4 11.8 %combine.3 = bf16[1536,2048]{1,0:T(8,128)(2,1)} custom-call(bf16[1536,256]{1,0:T(8,128)(2,1)} %copy-done.26, bf16[1536,256]{1,0:T(8,128)(2,1)} %copy-done.27, bf16[1536,256]{1,0:T(8,128)(2,1)} %copy-done.28, bf16[1536,256]{1,0:T(8,128)(2,1)} %copy-done.29, bf16[2048,768]{1,0:T(8,128)(2,1)} %all-gather.13.cloned.1.call-done.refs_0_.refs_1_.refs_2_.refs_8_.refs_12_.refs_4_, ...), custom_call_target="tpu_custom_call" | custom-call | flops 1024 | bytes 1024 | tf_op jit(solution)/shard_map/combine/pallas_call | solution.py:940
  653.3 140.5 %scatter_rows.3 = (f32[96,2048]{1,0:T(8,128)S(1)}, f32[96,2048]{1,0:T(8,128)S(1)}, bf16[1024,768]{1,0:T(8,128)(2,1)S(1)}, bf16[1024,768]{1,0:T(8,128)(2,1)S(1)}, f32[24,2048]{1,0:T(8,128)S(1)}) custom-call(bf16[4,4,96,2048]{3,2,1,0:T(8,128)(2,1)} %bitcast.220, bf16[4,4,96,2048]{3,2,1,0:T(8,128)(2,1)} %bitcast.217, bf16[1024,768]{1,0:T(8,128)(2,1)} %copy-done.22, ...), custom_call_target="tpu_custom_call" | custom-call | flops 1024 | bytes 1024 | tf_op jit(solution)/shard_map/scatter_rows/pallas_call | solution.py:422
  805.8 27.7 %expert_gradients.1 = (f32[65536,128]{1,0:T(8,128)}, f32[32768,128]{1,0:T(8,128)}) custom-call(s32[1]{0:T(128)} %bitcast.3.index, bf16[4,1024,768]{2,1,0:T(8,128)(2,1)} %bitcast.222, bf16[4,1024,768]{2,1,0:T(8,128)(2,1)} %bitcast.216, bf16[4,1024,768]{2,1,0:T(8,128)(2,1)} %bitcast.223, bf16[4,1024,768]{2,1,0:T(8,128)(2,1)} %pad_maximum_fusion.refs_3_.refs_4_.refs_5_.refs_6_, ...), custom_call_target="tpu_custom_call" | custom-call | flops 1024 | bytes 1024 | tf_op jit(solution)/shard_map/expert_gradients/pallas_call | solution.py:1047
  (416 shorter events, 234.3 us)
Async XLA Ops:
  7.2 100.7 %all-gather.11.cloned.1.call-start = ((), (), s32[]{:S(2)}) async-start(), calls=%async_computation | async-start | bytes 2359296 | tf_op jit(solution)/shard_map/all_gather | solution.py:495
  21.7 189.4 %all-gather.13.cloned.1.call-start = ((), (), s32[]{:S(2)}) async-start(), calls=%async_computation.1 | async-start | bytes 4718592 | tf_op jit(solution)/shard_map/all_gather | solution.py:495
  22.4 214.4 %all-gather.15.cloned.1.call-start = ((), (), s32[]{:S(2)}) async-start(), calls=%async_computation.2 | async-start | bytes 14155776 | tf_op jit(solution)/shard_map/all_gather | solution.py:495
  22.5 82.9 %collective-permute-start.8 = (s32[384,8]{0,1:T(8,128)S(1)}, s32[384,8]{0,1:T(8,128)S(1)}, u32[]{:S(2)}, u32[]{:S(2)}) collective-permute-start(s32[384,8]{0,1:T(8,128)S(1)} %bitcast.251), channel_id=1, source_target_pairs={{4,0},{8,4},{12,8},{0,12},{5,1},{9,5},{13,9},{1,13},{6,2},{10,6},{... | collective-permute-start | bytes 36872 | tf_op jit(solution)/shard_map/ppermute | solution.py:30
  27.6 78.5 %collective-permute-start.9 = (s32[384,8]{0,1:T(8,128)S(1)}, s32[384,8]{0,1:T(8,128)S(1)}, u32[]{:S(2)}, u32[]{:S(2)}) collective-permute-start(s32[384,8]{0,1:T(8,128)S(1)} %bitcast.252), channel_id=1, source_target_pairs={{8,0},{12,4},{0,8},{4,12},{9,1},{13,5},{1,9},{5,13},{10,2},{14,6},... | collective-permute-start | bytes 36872 | tf_op jit(solution)/shard_map/ppermute | solution.py:30
  27.6 79.1 %collective-permute-start.10 = (s32[384,8]{0,1:T(8,128)S(1)}, s32[384,8]{0,1:T(8,128)S(1)}, u32[]{:S(2)}, u32[]{:S(2)}) collective-permute-start(s32[384,8]{0,1:T(8,128)S(1)} %bitcast.253), channel_id=1, source_target_pairs={{12,0},{0,4},{4,8},{8,12},{13,1},{1,5},{5,9},{9,13},{14,2},{2,6},{... | collective-permute-start | bytes 36872 | tf_op jit(solution)/shard_map/ppermute | solution.py:30
  28.6 76.0 %collective-permute-start = (bf16[2,1024]{1,0:T(2,128)(2,1)S(1)}, bf16[2,1024]{1,0:T(2,128)(2,1)S(1)}, u32[]{:S(2)}, u32[]{:S(2)}) collective-permute-start(bf16[2,1024]{1,0:T(2,128)(2,1)S(1)} %pad_maximum_fusion.13), channel_id=1, source_target_pairs={{16,0},{0,16},{17,1},{1,17},{18,2},{2,18},{19,3},{3,19},{20,4},{4,... | collective-permute-start | bytes 12296 | tf_op jit(solution)/shard_map/ppermute | solution.py:30
  30.2 72.8 %collective-permute-start.1 = (bf16[1,128]{1,0:T(2,128)(2,1)S(1)}, bf16[1,128]{1,0:T(2,128)(2,1)S(1)}, u32[]{:S(2)}, u32[]{:S(2)}) collective-permute-start(bf16[1,128]{1,0:T(2,128)(2,1)S(1)} %bitcast.267), channel_id=1, source_target_pairs={{16,0},{0,16},{17,1},{1,17},{18,2},{2,18},{19,3},{3,19},{20,4},{4,... | collective-permute-start | bytes 776 | tf_op jit(solution)/shard_map/ppermute | solution.py:30
  30.8 436.2 %all-gather.19.cloned.1.call-start = ((), (), s32[]{:S(2)}) async-start(), calls=%async_computation.4 | async-start | bytes 7864320 | tf_op jit(solution)/shard_map/all_gather | solution.py:1196
  104.7 59.7 %collective-permute-start.11 = (bf16[1024,16]{0,1:T(8,128)(2,1)}, bf16[1024,16]{0,1:T(8,128)(2,1)}, u32[]{:S(2)}, u32[]{:S(2)}) collective-permute-start(bf16[1024,16]{0,1:T(8,128)(2,1)} %param.21), channel_id=1, source_target_pairs={{16,0},{0,16},{17,1},{1,17},{18,2},{2,18},{19,3},{3,19},{20,4},{4,... | collective-permute-start | bytes 98312 | tf_op jit(solution)/shard_map/ppermute | solution.py:30
  273.7 307.1 %all-gather.21.cloned.1.call-start = ((), (), s32[]{:S(2)}) async-start(), calls=%async_computation.5 | async-start | bytes 7864320 | tf_op jit(solution)/shard_map/all_gather | solution.py:1196
  311.7 494.1 %all-gather.23.cloned.1.call-start = ((), (), s32[]{:S(2)}) async-start(), calls=%async_computation.6 | async-start | bytes 7864320 | tf_op jit(solution)/shard_map/all_gather | solution.py:1196
  324.0 141.3 %collective-permute-start.21 = (bf16[1024,768]{1,0:T(8,128)(2,1)}, bf16[1024,768]{1,0:T(8,128)(2,1)S(1)}, u32[]{:S(2)}, u32[]{:S(2)}) collective-permute-start(bf16[1024,768]{1,0:T(8,128)(2,1)} %get-tuple-element.91.refs_8_), channel_id=1, source_target_pairs={{16,0},{0,16},{17,1},{1,17},{18,2},{2,18},{19,3},{3,19},{20,4},{4,... | collective-permute-start | bytes 4718600 | tf_op jit(solution)/shard_map/ppermute | solution.py:30
  350.7 133.9 %collective-permute-start.22 = (bf16[1024,768]{1,0:T(8,128)(2,1)}, bf16[1024,768]{1,0:T(8,128)(2,1)}, u32[]{:S(2)}, u32[]{:S(2)}) collective-permute-start(bf16[1024,768]{1,0:T(8,128)(2,1)} %get-tuple-element.98.refs_20_), channel_id=1, source_target_pairs={{16,0},{0,16},{17,1},{1,17},{18,2},{2,18},{19,3},{3,19},{20,4},{4,... | collective-permute-start | bytes 4718600 | tf_op jit(solution)/shard_map/ppermute | solution.py:30
  466.9 374.2 %all-gather.17.cloned.1.call-start = ((), (), s32[]{:S(2)}) async-start(), calls=%async_computation.3 | async-start | bytes 5242880 | tf_op jit(solution)/shard_map/all_gather | solution.py:1253
  483.6 94.4 %collective-permute-start.18 = (bf16[1024,768]{1,0:T(8,128)(2,1)S(1)}, bf16[1024,768]{1,0:T(8,128)(2,1)}, u32[]{:S(2)}, u32[]{:S(2)}) collective-permute-start(bf16[1024,768]{1,0:T(8,128)(2,1)S(1)} %copy-done.5), channel_id=1, source_target_pairs={{16,0},{0,16},{17,1},{1,17},{18,2},{2,18},{19,3},{3,19},{20,4},{4,... | collective-permute-start | bytes 4718600 | tf_op jit(solution)/shard_map/ppermute | solution.py:30
  498.1 45.2 %collective-permute-start.19 = (bf16[1024,512]{1,0:T(8,128)(2,1)S(1)}, bf16[1024,512]{1,0:T(8,128)(2,1)S(1)}, u32[]{:S(2)}, u32[]{:S(2)}) collective-permute-start(bf16[1024,512]{1,0:T(8,128)(2,1)S(1)} %convolution_convert_fusion.1), channel_id=1, source_target_pairs={{16,0},{0,16},{17,1},{1,17},{18,2},{2,18},{19,3},{3,19},{20,4},{4,... | collective-permute-start | bytes 3145736 | tf_op jit(solution)/shard_map/ppermute | solution.py:30
  537.8 93.9 %collective-permute-start.23 = (bf16[1024,384]{1,0:T(8,128)(2,1)}, bf16[1024,384]{1,0:T(8,128)(2,1)}, u32[]{:S(2)}, u32[]{:S(2)}) collective-permute-start(bf16[1024,384]{1,0:T(8,128)(2,1)} %fusion.11.refs_9_), channel_id=1, source_target_pairs={{16,0},{0,16},{17,1},{1,17},{18,2},{2,18},{19,3},{3,19},{20,4},{4,... | collective-permute-start | bytes 2359304 | tf_op jit(solution)/shard_map/ppermute | solution.py:30
  569.1 81.1 %collective-permute-start.27 = (bf16[1024,768]{1,0:T(8,128)(2,1)}, bf16[1024,768]{1,0:T(8,128)(2,1)}, u32[]{:S(2)}, u32[]{:S(2)}) collective-permute-start(bf16[1024,768]{1,0:T(8,128)(2,1)} %get-tuple-element.109.refs_8_), channel_id=1, source_target_pairs={{16,0},{0,16},{17,1},{1,17},{18,2},{2,18},{19,3},{3,19},{20,4},{4,... | collective-permute-start | bytes 4718600 | tf_op jit(solution)/shard_map/ppermute | solution.py:30
  576.7 58.0 %collective-permute-start.24 = (bf16[1024,128]{1,0:T(8,128)(2,1)}, bf16[1024,128]{1,0:T(8,128)(2,1)}, u32[]{:S(2)}, u32[]{:S(2)}) collective-permute-start(bf16[1024,128]{1,0:T(8,128)(2,1)} %get-tuple-element.146), channel_id=1, source_target_pairs={{12,0},{0,4},{4,8},{8,12},{13,1},{1,5},{5,9},{9,13},{14,2},{2,6},{... | collective-permute-start | bytes 786440 | tf_op jit(solution)/shard_map/ppermute | solution.py:30
  577.5 57.3 %collective-permute-start.25 = (bf16[1024,128]{1,0:T(8,128)(2,1)}, bf16[1024,128]{1,0:T(8,128)(2,1)}, u32[]{:S(2)}, u32[]{:S(2)}) collective-permute-start(bf16[1024,128]{1,0:T(8,128)(2,1)} %get-tuple-element.148), channel_id=1, source_target_pairs={{8,0},{12,4},{0,8},{4,12},{9,1},{13,5},{1,9},{5,13},{10,2},{14,6},... | collective-permute-start | bytes 786440 | tf_op jit(solution)/shard_map/ppermute | solution.py:30
  578.0 56.7 %collective-permute-start.26 = (bf16[1024,128]{1,0:T(8,128)(2,1)}, bf16[1024,128]{1,0:T(8,128)(2,1)}, u32[]{:S(2)}, u32[]{:S(2)}) collective-permute-start(bf16[1024,128]{1,0:T(8,128)(2,1)} %get-tuple-element.147), channel_id=1, source_target_pairs={{4,0},{8,4},{12,8},{0,12},{5,1},{9,5},{13,9},{1,13},{6,2},{10,6},{... | collective-permute-start | bytes 786440 | tf_op jit(solution)/shard_map/ppermute | solution.py:30
  793.9 40.3 %collective-permute-start.32 = (f32[18,1024]{1,0:T(8,128)S(1)}, f32[18,1024]{1,0:T(8,128)S(1)}, u32[]{:S(2)}, u32[]{:S(2)}) collective-permute-start(f32[18,1024]{1,0:T(8,128)S(1)} %constant_dynamic-slice_fusion.5), channel_id=1, source_target_pairs={{16,0},{0,16},{17,1},{1,17},{18,2},{2,18},{19,3},{3,19},{20,4},{4,... | collective-permute-start | bytes 221192 | tf_op jit(solution)/shard_map/ppermute | solution.py:30
  794.0 39.5 %collective-permute-start.33 = (f32[1,128]{1,0:T(1,128)S(1)}, f32[1,128]{1,0:T(1,128)S(1)}, u32[]{:S(2)}, u32[]{:S(2)}) collective-permute-start(f32[1,128]{1,0:T(1,128)S(1)} %constant_dynamic-slice_fusion.3), channel_id=1, source_target_pairs={{16,0},{0,16},{17,1},{1,17},{18,2},{2,18},{19,3},{3,19},{20,4},{4,... | collective-permute-start | bytes 1544 | tf_op jit(solution)/shard_map/ppermute | solution.py:30
  (111 other events, 1958.5 us)
Sparse Core Ops, SparseCore 0:
  21.8 29.9 all-gather.10
  53.9 44.9 all-gather.12
  101.0 129.6 all-gather.14
  273.8 113.3 all-gather.18
  388.6 135.5 all-gather.20
  525.7 137.1 all-gather.22
  664.4 133.5 all-gather.16

commit v7 on v6

--- a/solution.py
+++ b/solution.py
@@ -1001,8 +1001,19 @@
     )(s.astype(jnp.int32)[None], rows, upstream, inner_grad, scaled)
 
 
+def attention_kernel(chunk, entry, exit_out):
+    ctxs, _, width = chunk.shape
+    head = width // 4
+    for j in range(ctxs):
+        for k in range(3):
+            entry[k, :, j * head : (j + 1) * head] = chunk[j, :, k * head : (k + 1) * head].astype(F32)
+        exit_out[:, j * head : (j + 1) * head] = chunk[j, :, 3 * head :].astype(F32)
+
+
 def expert_kernel(group, ctxs, tall, hidden, index, *refs):
-    gathered, shared, (up, down) = refs[: group - 1], refs[group - 1 : group - 1 + ctxs], refs[group - 1 + ctxs :]
+    gathered, shared = refs[: group - 1], refs[group - 1 : group - 1 + ctxs]
+    chunk, up, down, entry, exit_out = refs[group - 1 + ctxs :]
+    attention_kernel(chunk, entry, exit_out)
     pieces = hidden // 128
     experts = group * ctxs
     deep = 16
@@ -1038,13 +1049,14 @@
         place(down, downs, start)
 
 
-def expert_gradients(gathered, shared):
+def weight_gradients(gathered, shared, chunk):
     (ctxs, rows, width), group = shared.shape, len(gathered) + 1
     hidden, experts = width // 3, group * ctxs
     pieces = hidden // 128
     assert experts % 8 == 0 and hidden % 128 == 0
     tall = 64
-    up, down = pl.pallas_call(
+    wide = ctxs * chunk.shape[2] // 4
+    up, down, entry, exit_out = pl.pallas_call(
         functools.partial(expert_kernel, group, ctxs, tall, hidden),
         grid_spec=pltpu.PrefetchScalarGridSpec(
             num_scalar_prefetch=1,
@@ -1055,42 +1067,23 @@
                     (1, tall, width), functools.partial(lambda j, b, c: (lax.rem(ctxs + j - c[0], ctxs), b, 0), j)
                 )
                 for j in range(ctxs)
+            ]
+            + [pl.BlockSpec((ctxs, tall, chunk.shape[2]), lambda b, c: (0, b, 0))],
+            out_specs=[pl.BlockSpec((tall * experts * pieces * k, 128), lambda b, c: (b, 0)) for k in (2, 1)]
+            + [
+                pl.BlockSpec((3, tall, wide), lambda b, c: (0, b, 0)),
+                pl.BlockSpec((tall, wide), lambda b, c: (b, 0)),
             ],
-            out_specs=[pl.BlockSpec((tall * experts * pieces * k, 128), lambda b, c: (b, 0)) for k in (2, 1)],
         ),
-        out_shape=[jax.ShapeDtypeStruct((rows * experts * pieces * k, 128), F32) for k in (2, 1)],
+        out_shape=[jax.ShapeDtypeStruct((rows * experts * pieces * k, 128), F32) for k in (2, 1)]
+        + [jax.ShapeDtypeStruct((3, rows, wide), F32), jax.ShapeDtypeStruct((rows, wide), F32)],
         compiler_params=pltpu.CompilerParams(vmem_limit_bytes=48 * 1024 * 1024),
-        name="expert_gradients",
+        name="weight_gradients",
         cost_estimate=COST,
-    )(lax.axis_index("ctx").astype(jnp.int32)[None], *gathered, *([shared] * ctxs))
+    )(lax.axis_index("ctx").astype(jnp.int32)[None], *gathered, *([shared] * ctxs), chunk)
     up = up.reshape(rows, experts, pieces, 2, 128).transpose(0, 1, 3, 2, 4).reshape(rows, experts, 2, hidden)
     down = down.reshape(rows, experts // 8, pieces, 8, 128).transpose(0, 1, 3, 2, 4).reshape(rows, experts, hidden)
-    return up, down
-
-
-def attention_kernel(chunk, entry, exit_out):
-    ctxs, _, width = chunk.shape
-    head = width // 4
-    for j in range(ctxs):
-        for k in range(3):
-            entry[k, :, j * head : (j + 1) * head] = chunk[j, :, k * head : (k + 1) * head].astype(F32)
-        exit_out[:, j * head : (j + 1) * head] = chunk[j, :, 3 * head :].astype(F32)
-
-
-def attention_gradients(chunk):
-    ctxs, rows, width = chunk.shape
-    wide = ctxs * width // 4
-    tall = 128
-    entry, exit_out = pl.pallas_call(
-        attention_kernel,
-        grid=(rows // tall,),
-        in_specs=[pl.BlockSpec((ctxs, tall, width), lambda b: (0, b, 0))],
-        out_specs=[pl.BlockSpec((3, tall, wide), lambda b: (0, b, 0)), pl.BlockSpec((tall, wide), lambda b: (b, 0))],
-        out_shape=[jax.ShapeDtypeStruct((3, rows, wide), F32), jax.ShapeDtypeStruct((rows, wide), F32)],
-        name="attention_gradients",
-        cost_estimate=COST,
-    )(chunk)
-    return entry.transpose(1, 0, 2), exit_out
+    return up, down, entry.transpose(1, 0, 2), exit_out
 
 
 def local(
@@ -1276,10 +1269,9 @@
     input_back, _ = norm_back(first_normed_grad, layer_in, gain_one)
     input_gradient = natural_rows(gather_tp(lower(residual_grad + input_back))).astype(F32)[None]
 
-    upward_gradient, downward_gradient = expert_gradients(
-        gathered, jnp.stack(shared_chunks)
+    upward_gradient, downward_gradient, entry_gradient, exit_gradient = weight_gradients(
+        gathered, jnp.stack(shared_chunks), attention_gathered
     )
-    entry_gradient, exit_gradient = attention_gradients(attention_gathered)
     return (
         layer_output,
         input_gradient,

time: 868 us -> 865 us (level)
    pallas_call x2 -> x1, Pallas kernels: 35.1 us -> 29.8 us  [weight_gradients(): pl.pallas_call(functools.partial(expert_kernel, group, ctxs, tall, hidden...]
    unnamed x203 -> x205, local copies, waits for them, and re-layouts: 24 us -> 26 us
  transfers between devices with their start and end apart: 41 -> 41, of which waited for: 13 -> 13; matrix products, arithmetic and copies ran while one was open for 11% -> 11% of each run, Pallas kernels for 70% -> 67%
where the time goes in v7:
time: 865 us; the launch traced here: 853 us
  Pallas kernels  615 us (71%)
  waiting for transfers between devices  60.5 us (7%)
  other arithmetic  47.3 us (5%)
  local copies, waits for them, and re-layouts  41.8 us (5%)
  starting transfers between devices  38.2 us (4%)
  matrix products  31.1 us (4%)
  between operations  19.9 us (2%)
    pallas_call x2, Pallas kernels, scatter_rows(): pl.pallas_call(functools.partial(scatter_kernel, size, arrays, tuple((ahe...  230 us
    pallas_call x2, Pallas kernels, gather_rows(): pl.pallas_call(functools.partial(gather_kernel, size, pieces, arrays, sha...  103 us
    pallas_call x7, Pallas kernels, gradient_parts(): pl.pallas_call(functools.partial(gradient_kernel, steps), grid_spec=pltpu...  85.4 us
    pallas_call x7, Pallas kernels, expert_step(): pl.pallas_call(functools.partial(expert_step_kernel, index, parts, len(ea...  74.9 us
    ppermute x26, waiting for transfers between devices, receive(): lax.ppermute(values, axis, [((i + distance) % size, i) for i in range(siz...  44.7 us
    ppermute x26, starting transfers between devices, receive(): lax.ppermute(values, axis, [((i + distance) % size, i) for i in range(siz...  33.6 us
    pallas_call x2, Pallas kernels, combine(): pl.pallas_call(lambda *refs: combine_kernel(len(lefts), len(lanes), *refs...  31.8 us
    dot_general x13, matrix products, dot(): lax.dot_general(left, right, (((over[0],), (over[1],)), ((), ())), prefer...  31.1 us
  transfers between devices with their start and end apart: 41, of which 13 were waited for; matrix products, arithmetic and copies ran while one was open for 11% of the time, Pallas kernels for 67%

profile of v7, /device:TPU:0, one launch (start us, length us, event | category | flops | bytes accessed | tf_op | source)
XLA Modules:
  0.0 853.5 jit_solution(8949910106668855113)
XLA Ops:
  8.5 13.1 %own_weights.1 = (bf16[1024,768]{1,0:T(8,128)(2,1)}, bf16[1024,2304]{1,0:T(8,128)(2,1)}, bf16[1024,384]{1,0:T(8,128)(2,1)}, bf16[1024,512]{1,0:T(8,128)(2,1)S(1)}) custom-call(s32[1]{0:T(128)} %bitcast.3.index, bf16[1024,64,128]{2,1,0:T(8,128)(2,1)} %bitcast.203, bf16[1024,32,128]{2,1,0:T(8,128)(2,1)} %bitcast.207, bf16[3,1024,512]{2,1,0:T(8,128)(2,1)} %bitcast.225, ...), custom_call_target="tpu_custom_call" | custom-call | flops 1024 | bytes 1024 | tf_op jit(solution)/shard_map/own_weights/pallas_call | solution.py:617
  39.0 64.1 %gather_rows.2 = (bf16[4,4,96,2048]{3,2,1,0:T(8,128)(2,1)}, bf16[4,4,96,2048]{3,2,1,0:T(8,128)(2,1)}) custom-call(bf16[384,2048]{1,0:T(8,128)(2,1)} %bitcast.224, bf16[384,2048]{1,0:T(8,128)(2,1)} %bitcast.227, bf16[1024,384]{1,0:T(8,128)(2,1)} %get-tuple-element.70.refs_2_), custom_call_target="tpu_custom_call" | custom-call | flops 1024 | bytes 1024 | tf_op jit(solution)/shard_map/gather_rows/pallas_call | solution.py:233
  109.5 10.5 %project.1 = (bf16[1536,2048]{1,0:T(8,128)(2,1)}, f32[1536,256]{1,0:T(8,128)S(1)}, bf16[1536,128]{1,0:T(8,128)(2,1)S(1)}, bf16[1536,128]{1,0:T(8,128)(2,1)S(1)}, bf16[1536,128]{1,0:T(8,128)(2,1)S(1)}) custom-call(bf16[1536,2048]{1,0:T(8,128)(2,1)} %bitcast.214, f32[1,2048]{1,0:T(1,128)S(1)} %get-tuple-element.164.gain, bf16[2048,384]{1,0:T(8,128)(2,1)S(1)} %copy-done.38, ...), custom_call_target="tpu_custom_call" | custom-call | flops 1024 | bytes 1024 | tf_op jit(solution)/shard_map/project/pallas_call | solution.py:732
  165.2 38.9 %gather_rows.3 = bf16[4,4,96,2048]{3,2,1,0:T(8,128)(2,1)} custom-call(bf16[96,2048]{1,0:T(8,128)(2,1)} %multiply_convert_fusion.refs_0_), custom_call_target="tpu_custom_call" | custom-call | flops 1024 | bytes 1024 | tf_op jit(solution)/shard_map/gather_rows/pallas_call | solution.py:233
  221.4 12.8 %gradient_parts.7 = (f32[1024,768]{1,0:T(8,128)}, bf16[1024,768]{1,0:T(8,128)(2,1)}) custom-call(s32[1]{0:T(128)} %bitcast.31.shard.index, bf16[1536,2048]{1,0:T(8,128)(2,1)} %bitcast.176, bf16[1536,2048]{1,0:T(8,128)(2,1)} %bitcast.190, bf16[1536,512]{1,0:T(8,128)(2,1)S(1)} %get-tuple-element.79.inner_grad.refs_0_.refs_4_, ...), custom_call_target="tpu_custom_call" | custom-call | flops 1024 | bytes 1024 | tf_op jit(solution)/shard_map/gradient_parts/pallas_call | solution.py:983
  247.2 12.9 %gradient_parts.8 = (f32[1024,768]{1,0:T(8,128)}, bf16[1024,768]{1,0:T(8,128)(2,1)}) custom-call(s32[1]{0:T(128)} %bitcast.31.shard.index, bf16[1536,2048]{1,0:T(8,128)(2,1)} %bitcast.178, bf16[1536,2048]{1,0:T(8,128)(2,1)} %bitcast.192, bf16[1536,512]{1,0:T(8,128)(2,1)S(1)} %get-tuple-element.83.inner_grad.refs_1_.refs_5_, ...), custom_call_target="tpu_custom_call" | custom-call | flops 1024 | bytes 1024 | tf_op jit(solution)/shard_map/gradient_parts/pallas_call | solution.py:983
  275.5 16.3 %shared_weights.1 = (bf16[1024,768]{1,0:T(8,128)(2,1)S(1)}, bf16[1024,768]{1,0:T(8,128)(2,1)S(1)}, bf16[1024,768]{1,0:T(8,128)(2,1)S(1)}) custom-call(s32[1]{0:T(128)} %bitcast.3.index, bf16[1024,64,128]{2,1,0:T(8,128)(2,1)} %bitcast.204, bf16[1024,64,128]{2,1,0:T(8,128)(2,1)} %bitcast.205, bf16[1024,64,128]{2,1,0:T(8,128)(2,1)} %bitcast.206, ...), custom_call_target="tpu_custom_call" | custom-call | flops 1024 | bytes 1024 | tf_op jit(solution)/shard_map/shared_weights/pallas_call | solution.py:686
  295.4 10.5 %expert_step.9 = (bf16[1536,256]{1,0:T(8,128)(2,1)S(1)}, bf16[1536,512]{1,0:T(8,128)(2,1)S(1)}, f32[1536,128]{1,0:T(8,128)S(1)}) custom-call(s32[1]{0:T(128)} %bitcast.31.shard.index, bf16[1536,2048]{1,0:T(8,128)(2,1)} %bitcast.179, bf16[1536,2048]{1,0:T(8,128)(2,1)} %bitcast.193, ...), custom_call_target="tpu_custom_call" | custom-call | flops 1024 | bytes 1024 | tf_op jit(solution)/shard_map/expert_step/pallas_call | solution.py:903
  312.0 11.8 %gradient_parts.9 = (f32[1024,768]{1,0:T(8,128)}, bf16[1024,768]{1,0:T(8,128)(2,1)}) custom-call(s32[1]{0:T(128)} %bitcast.31.shard.index, bf16[1536,2048]{1,0:T(8,128)(2,1)} %bitcast.180, bf16[1536,2048]{1,0:T(8,128)(2,1)} %bitcast.194, bf16[1536,512]{1,0:T(8,128)(2,1)S(1)} %get-tuple-element.89.inner_grad.refs_2_.refs_6_, ...), custom_call_target="tpu_custom_call" | custom-call | flops 1024 | bytes 1024 | tf_op jit(solution)/shard_map/gradient_parts/pallas_call | solution.py:983
  326.9 10.7 %expert_step.10 = (bf16[1536,256]{1,0:T(8,128)(2,1)S(1)}, bf16[1536,512]{1,0:T(8,128)(2,1)S(1)}, f32[1536,128]{1,0:T(8,128)S(1)}) custom-call(s32[1]{0:T(128)} %bitcast.31.shard.index, bf16[1536,2048]{1,0:T(8,128)(2,1)} %bitcast.181, bf16[1536,2048]{1,0:T(8,128)(2,1)} %bitcast.195, ...), custom_call_target="tpu_custom_call" | custom-call | flops 1024 | bytes 1024 | tf_op jit(solution)/shard_map/expert_step/pallas_call | solution.py:903
  337.6 12.9 %gradient_parts.10 = (f32[1024,768]{1,0:T(8,128)}, bf16[1024,768]{1,0:T(8,128)(2,1)}) custom-call(s32[1]{0:T(128)} %bitcast.31.shard.index, bf16[1536,2048]{1,0:T(8,128)(2,1)} %bitcast.182, bf16[1536,2048]{1,0:T(8,128)(2,1)} %bitcast.196, bf16[1536,512]{1,0:T(8,128)(2,1)S(1)} %get-tuple-element.92.inner_grad.refs_3_.refs_7_, ...), custom_call_target="tpu_custom_call" | custom-call | flops 1024 | bytes 1024 | tf_op jit(solution)/shard_map/gradient_parts/pallas_call | solution.py:983
  351.1 20.0 %combine.2 = bf16[1536,2176]{1,0:T(8,128)(2,1)} custom-call(bf16[1536,512]{1,0:T(8,128)(2,1)} %copy-done.9, bf16[1536,512]{1,0:T(8,128)(2,1)} %copy-done.10, bf16[1536,512]{1,0:T(8,128)(2,1)} %copy-done.11, bf16[1536,512]{1,0:T(8,128)(2,1)} %copy-done.12, bf16[1536,512]{1,0:T(8,128)(2,1)} %copy-done.9, bf16[1536,512]{1,0:T(8,128)(2,1)} %copy-done.10, ...), custom_call_target="tpu_custom_call" | custom-call | flops 1024 | bytes 1024 | tf_op jit(solution)/shard_map/combine/pallas_call | solution.py:940
  371.1 89.8 %scatter_rows.2 = (f32[96,2176]{1,0:T(8,128)S(1)}, bf16[1024,768]{1,0:T(8,128)(2,1)S(1)}, bf16[1024,768]{1,0:T(8,128)(2,1)S(1)}) custom-call(bf16[4,4,96,2176]{3,2,1,0:T(8,128)(2,1)} %bitcast.211, bf16[1024,768]{1,0:T(8,128)(2,1)S(1)} %copy-done.3, bf16[1024,768]{1,0:T(8,128)(2,1)} %copy-done), custom_call_target="tpu_custom_call" | custom-call | flops 1024 | bytes 1024 | tf_op jit(solution)/shard_map/scatter_rows/pallas_call | solution.py:422
  502.8 15.9 %collective-permute-done.16 = bf16[4,96,128]{2,1,0:T(8,128)(2,1)S(1)} collective-permute-done((bf16[4,96,128]{2,1,0:T(8,128)(2,1)S(1)}, bf16[4,96,128]{2,1,0:T(8,128)(2,1)S(1)}, u32[]{:S(2)}, u32[]{:S(2)}) %collective-permute-start.16) | collective-permute-done | bytes 98336 | tf_op jit(solution)/shard_map/ppermute | solution.py:30
  518.9 13.2 %attend_back.1 = (bf16[1536,384]{1,0:T(8,128)(2,1)S(1)}, f32[8,128]{1,0:T(8,128)S(1)}) custom-call(bf16[1536,128]{1,0:T(8,128)(2,1)S(1)} %copy-done.33, bf16[1536,128]{1,0:T(8,128)(2,1)S(1)} %copy-done.35, bf16[1536,128]{1,0:T(8,128)(2,1)S(1)} %copy-done.37, f32[1536,256]{1,0:T(8,128)} %copy-done.31, f32[1536,128]{1,0:T(8,128)S(1)} %copy-done.17, ...), custom_call_target="tpu_custom_call" | custom-call | flops 1024 | bytes 1024 | tf_op jit(solution)/shard_map/attend_back/pallas_call | solution.py:833
  545.5 11.4 %expert_step.11 = (bf16[1536,256]{1,0:T(8,128)(2,1)S(1)}, bf16[1536,512]{1,0:T(8,128)(2,1)S(1)}, f32[1536,128]{1,0:T(8,128)}) custom-call(s32[1]{0:T(128)} %bitcast.31.shard.index, bf16[1536,2048]{1,0:T(8,128)(2,1)} %bitcast.183, bf16[1536,2048]{1,0:T(8,128)(2,1)} %bitcast.197, bf16[1024,768]{1,0:T(8,128)(2,1)} %copy-done.2, bf16[1024,768]{1,0:T(8,128)(2,1)} %copy-done.8, ...), custom_call_target="tpu_custom_call" | custom-call | flops 1024 | bytes 1024 | tf_op jit(solution)/shard_map/expert_step/pallas_call | solution.py:903
  557.0 11.9 %gradient_parts.11 = (f32[1024,768]{1,0:T(8,128)}, bf16[1024,768]{1,0:T(8,128)(2,1)}) custom-call(s32[1]{0:T(128)} %bitcast.31.shard.index, bf16[1536,2048]{1,0:T(8,128)(2,1)} %bitcast.184, bf16[1536,2048]{1,0:T(8,128)(2,1)} %bitcast.198, bf16[1536,512]{1,0:T(8,128)(2,1)S(1)} %get-tuple-element.107.inner_grad, bf16[1536,256]{1,0:T(8,128)(2,1)S(1)} %get-tuple-element.108.scaled), custom_call_target="tpu_custom_call" | custom-call | flops 1024 | bytes 1024 | tf_op jit(solution)/shard_map/gradient_parts/pallas_call | solution.py:983
  581.7 10.8 %expert_step.12 = (bf16[1536,256]{1,0:T(8,128)(2,1)S(1)}, bf16[1536,512]{1,0:T(8,128)(2,1)S(1)}, f32[1536,128]{1,0:T(8,128)}) custom-call(s32[1]{0:T(128)} %bitcast.31.shard.index, bf16[1536,2048]{1,0:T(8,128)(2,1)} %bitcast.185, bf16[1536,2048]{1,0:T(8,128)(2,1)} %bitcast.199, bf16[1024,768]{1,0:T(8,128)(2,1)S(1)} %copy-done.1, ...), custom_call_target="tpu_custom_call" | custom-call | flops 1024 | bytes 1024 | tf_op jit(solution)/shard_map/expert_step/pallas_call | solution.py:903
  592.4 11.7 %gradient_parts.12 = (f32[1024,768]{1,0:T(8,128)}, bf16[1024,768]{1,0:T(8,128)(2,1)S(1)}) custom-call(s32[1]{0:T(128)} %bitcast.31.shard.index, bf16[1536,2048]{1,0:T(8,128)(2,1)} %bitcast.186, bf16[1536,2048]{1,0:T(8,128)(2,1)} %bitcast.200, bf16[1536,512]{1,0:T(8,128)(2,1)S(1)} %get-tuple-element.111.inner_grad, ...), custom_call_target="tpu_custom_call" | custom-call | flops 1024 | bytes 1024 | tf_op jit(solution)/shard_map/gradient_parts/pallas_call | solution.py:983
  605.3 11.0 %expert_step.13 = (bf16[1536,256]{1,0:T(8,128)(2,1)S(1)}, bf16[1536,512]{1,0:T(8,128)(2,1)S(1)}, f32[1536,128]{1,0:T(8,128)}) custom-call(s32[1]{0:T(128)} %bitcast.31.shard.index, bf16[1536,2048]{1,0:T(8,128)(2,1)} %bitcast.187, bf16[1536,2048]{1,0:T(8,128)(2,1)} %bitcast.201, bf16[1024,768]{1,0:T(8,128)(2,1)S(1)} %copy-done.5, ...), custom_call_target="tpu_custom_call" | custom-call | flops 1024 | bytes 1024 | tf_op jit(solution)/shard_map/expert_step/pallas_call | solution.py:903
  616.2 11.5 %gradient_parts.13 = (f32[1024,768]{1,0:T(8,128)}, bf16[1024,768]{1,0:T(8,128)(2,1)S(1)}) custom-call(s32[1]{0:T(128)} %bitcast.31.shard.index, bf16[1536,2048]{1,0:T(8,128)(2,1)} %bitcast.188, bf16[1536,2048]{1,0:T(8,128)(2,1)} %bitcast.202, bf16[1536,512]{1,0:T(8,128)(2,1)S(1)} %get-tuple-element.114.inner_grad, ...), custom_call_target="tpu_custom_call" | custom-call | flops 1024 | bytes 1024 | tf_op jit(solution)/shard_map/gradient_parts/pallas_call | solution.py:983
  638.1 11.8 %combine.3 = bf16[1536,2048]{1,0:T(8,128)(2,1)} custom-call(bf16[1536,256]{1,0:T(8,128)(2,1)} %copy-done.27, bf16[1536,256]{1,0:T(8,128)(2,1)} %copy-done.28, bf16[1536,256]{1,0:T(8,128)(2,1)} %copy-done.29, bf16[1536,256]{1,0:T(8,128)(2,1)} %copy-done.30, bf16[2048,768]{1,0:T(8,128)(2,1)} %all-gather.13.cloned.1.call-done.refs_0_.refs_1_.refs_2_.refs_8_.refs_12_.refs_4_, ...), custom_call_target="tpu_custom_call" | custom-call | flops 1024 | bytes 1024 | tf_op jit(solution)/shard_map/combine/pallas_call | solution.py:940
  653.0 140.5 %scatter_rows.3 = (f32[96,2048]{1,0:T(8,128)S(1)}, f32[96,2048]{1,0:T(8,128)S(1)}, bf16[1024,768]{1,0:T(8,128)(2,1)S(1)}, bf16[1024,768]{1,0:T(8,128)(2,1)S(1)}, f32[24,2048]{1,0:T(8,128)S(1)}) custom-call(bf16[4,4,96,2048]{3,2,1,0:T(8,128)(2,1)} %bitcast.223, bf16[4,4,96,2048]{3,2,1,0:T(8,128)(2,1)} %bitcast.217, bf16[1024,768]{1,0:T(8,128)(2,1)} %copy-done.22, ...), custom_call_target="tpu_custom_call" | custom-call | flops 1024 | bytes 1024 | tf_op jit(solution)/shard_map/scatter_rows/pallas_call | solution.py:422
  816.6 29.8 %weight_gradients.1 = (f32[65536,128]{1,0:T(8,128)}, f32[32768,128]{1,0:T(8,128)}, f32[3,1024,512]{2,1,0:T(8,128)}, f32[1024,512]{1,0:T(8,128)}) custom-call(s32[1]{0:T(128)} %bitcast.3.index, bf16[4,1024,768]{2,1,0:T(8,128)(2,1)} %bitcast.221, bf16[4,1024,768]{2,1,0:T(8,128)(2,1)} %bitcast.213, bf16[4,1024,768]{2,1,0:T(8,128)(2,1)} %bitcast.222, ...), custom_call_target="tpu_custom_call" | custom-call | flops 1024 | bytes 1024 | tf_op jit(solution)/shard_map/weight_gradients/pallas_call | solution.py:1059
  (417 shorter events, 230.1 us)
Async XLA Ops:
  7.2 100.7 %all-gather.11.cloned.1.call-start = ((), (), s32[]{:S(2)}) async-start(), calls=%async_computation | async-start | bytes 2359296 | tf_op jit(solution)/shard_map/all_gather | solution.py:495
  21.7 189.4 %all-gather.13.cloned.1.call-start = ((), (), s32[]{:S(2)}) async-start(), calls=%async_computation.1 | async-start | bytes 4718592 | tf_op jit(solution)/shard_map/all_gather | solution.py:495
  22.4 214.4 %all-gather.15.cloned.1.call-start = ((), (), s32[]{:S(2)}) async-start(), calls=%async_computation.2 | async-start | bytes 14155776 | tf_op jit(solution)/shard_map/all_gather | solution.py:495
  22.5 82.9 %collective-permute-start.8 = (s32[384,8]{0,1:T(8,128)S(1)}, s32[384,8]{0,1:T(8,128)S(1)}, u32[]{:S(2)}, u32[]{:S(2)}) collective-permute-start(s32[384,8]{0,1:T(8,128)S(1)} %bitcast.251), channel_id=1, source_target_pairs={{4,0},{8,4},{12,8},{0,12},{5,1},{9,5},{13,9},{1,13},{6,2},{10,6},{... | collective-permute-start | bytes 36872 | tf_op jit(solution)/shard_map/ppermute | solution.py:30
  27.6 78.4 %collective-permute-start.9 = (s32[384,8]{0,1:T(8,128)S(1)}, s32[384,8]{0,1:T(8,128)S(1)}, u32[]{:S(2)}, u32[]{:S(2)}) collective-permute-start(s32[384,8]{0,1:T(8,128)S(1)} %bitcast.252), channel_id=1, source_target_pairs={{8,0},{12,4},{0,8},{4,12},{9,1},{13,5},{1,9},{5,13},{10,2},{14,6},... | collective-permute-start | bytes 36872 | tf_op jit(solution)/shard_map/ppermute | solution.py:30
  27.6 79.0 %collective-permute-start.10 = (s32[384,8]{0,1:T(8,128)S(1)}, s32[384,8]{0,1:T(8,128)S(1)}, u32[]{:S(2)}, u32[]{:S(2)}) collective-permute-start(s32[384,8]{0,1:T(8,128)S(1)} %bitcast.253), channel_id=1, source_target_pairs={{12,0},{0,4},{4,8},{8,12},{13,1},{1,5},{5,9},{9,13},{14,2},{2,6},{... | collective-permute-start | bytes 36872 | tf_op jit(solution)/shard_map/ppermute | solution.py:30
  28.6 76.0 %collective-permute-start = (bf16[2,1024]{1,0:T(2,128)(2,1)S(1)}, bf16[2,1024]{1,0:T(2,128)(2,1)S(1)}, u32[]{:S(2)}, u32[]{:S(2)}) collective-permute-start(bf16[2,1024]{1,0:T(2,128)(2,1)S(1)} %pad_maximum_fusion.13), channel_id=1, source_target_pairs={{16,0},{0,16},{17,1},{1,17},{18,2},{2,18},{19,3},{3,19},{20,4},{4,... | collective-permute-start | bytes 12296 | tf_op jit(solution)/shard_map/ppermute | solution.py:30
  30.2 72.8 %collective-permute-start.1 = (bf16[1,128]{1,0:T(2,128)(2,1)S(1)}, bf16[1,128]{1,0:T(2,128)(2,1)S(1)}, u32[]{:S(2)}, u32[]{:S(2)}) collective-permute-start(bf16[1,128]{1,0:T(2,128)(2,1)S(1)} %bitcast.267), channel_id=1, source_target_pairs={{16,0},{0,16},{17,1},{1,17},{18,2},{2,18},{19,3},{3,19},{20,4},{4,... | collective-permute-start | bytes 776 | tf_op jit(solution)/shard_map/ppermute | solution.py:30
  30.8 436.0 %all-gather.19.cloned.1.call-start = ((), (), s32[]{:S(2)}) async-start(), calls=%async_computation.4 | async-start | bytes 7864320 | tf_op jit(solution)/shard_map/all_gather | solution.py:1189
  103.1 37.4 %collective-permute-start.5 = (bf16[1024,512]{1,0:T(8,128)(2,1)S(1)}, bf16[1024,512]{1,0:T(8,128)(2,1)}, u32[]{:S(2)}, u32[]{:S(2)}) collective-permute-start(bf16[1024,512]{1,0:T(8,128)(2,1)S(1)} %get-tuple-element.75), channel_id=1, source_target_pairs={{16,0},{0,16},{17,1},{1,17},{18,2},{2,18},{19,3},{3,19},{20,4},{4,... | collective-permute-start | bytes 3145736 | tf_op jit(solution)/shard_map/ppermute | solution.py:30
  104.7 59.7 %collective-permute-start.11 = (bf16[1024,16]{0,1:T(8,128)(2,1)}, bf16[1024,16]{0,1:T(8,128)(2,1)}, u32[]{:S(2)}, u32[]{:S(2)}) collective-permute-start(bf16[1024,16]{0,1:T(8,128)(2,1)} %param.21), channel_id=1, source_target_pairs={{16,0},{0,16},{17,1},{1,17},{18,2},{2,18},{19,3},{3,19},{20,4},{4,... | collective-permute-start | bytes 98312 | tf_op jit(solution)/shard_map/ppermute | solution.py:30
  234.3 37.7 %collective-permute-start.12 = (bf16[1024,768]{1,0:T(8,128)(2,1)}, bf16[1024,768]{1,0:T(8,128)(2,1)S(1)}, u32[]{:S(2)}, u32[]{:S(2)}) collective-permute-start(bf16[1024,768]{1,0:T(8,128)(2,1)} %get-tuple-element.82.refs_5_), channel_id=1, source_target_pairs={{16,0},{0,16},{17,1},{1,17},{18,2},{2,18},{19,3},{3,19},{20,4},{4,... | collective-permute-start | bytes 4718600 | tf_op jit(solution)/shard_map/ppermute | solution.py:30
  273.7 306.8 %all-gather.21.cloned.1.call-start = ((), (), s32[]{:S(2)}) async-start(), calls=%async_computation.5 | async-start | bytes 7864320 | tf_op jit(solution)/shard_map/all_gather | solution.py:1189
  311.7 502.7 %all-gather.23.cloned.1.call-start = ((), (), s32[]{:S(2)}) async-start(), calls=%async_computation.6 | async-start | bytes 7864320 | tf_op jit(solution)/shard_map/all_gather | solution.py:1189
  323.8 141.2 %collective-permute-start.21 = (bf16[1024,768]{1,0:T(8,128)(2,1)}, bf16[1024,768]{1,0:T(8,128)(2,1)S(1)}, u32[]{:S(2)}, u32[]{:S(2)}) collective-permute-start(bf16[1024,768]{1,0:T(8,128)(2,1)} %get-tuple-element.91.refs_8_), channel_id=1, source_target_pairs={{16,0},{0,16},{17,1},{1,17},{18,2},{2,18},{19,3},{3,19},{20,4},{4,... | collective-permute-start | bytes 4718600 | tf_op jit(solution)/shard_map/ppermute | solution.py:30
  350.5 133.9 %collective-permute-start.22 = (bf16[1024,768]{1,0:T(8,128)(2,1)}, bf16[1024,768]{1,0:T(8,128)(2,1)}, u32[]{:S(2)}, u32[]{:S(2)}) collective-permute-start(bf16[1024,768]{1,0:T(8,128)(2,1)} %get-tuple-element.98.refs_20_), channel_id=1, source_target_pairs={{16,0},{0,16},{17,1},{1,17},{18,2},{2,18},{19,3},{3,19},{20,4},{4,... | collective-permute-start | bytes 4718600 | tf_op jit(solution)/shard_map/ppermute | solution.py:30
  466.7 347.8 %all-gather.17.cloned.1.call-start = ((), (), s32[]{:S(2)}) async-start(), calls=%async_computation.3 | async-start | bytes 5242880 | tf_op jit(solution)/shard_map/all_gather | solution.py:1246
  483.4 94.3 %collective-permute-start.18 = (bf16[1024,768]{1,0:T(8,128)(2,1)S(1)}, bf16[1024,768]{1,0:T(8,128)(2,1)}, u32[]{:S(2)}, u32[]{:S(2)}) collective-permute-start(bf16[1024,768]{1,0:T(8,128)(2,1)S(1)} %copy-done.5), channel_id=1, source_target_pairs={{16,0},{0,16},{17,1},{1,17},{18,2},{2,18},{19,3},{3,19},{20,4},{4,... | collective-permute-start | bytes 4718600 | tf_op jit(solution)/shard_map/ppermute | solution.py:30
  498.2 45.0 %collective-permute-start.19 = (bf16[1024,512]{1,0:T(8,128)(2,1)S(1)}, bf16[1024,512]{1,0:T(8,128)(2,1)S(1)}, u32[]{:S(2)}, u32[]{:S(2)}) collective-permute-start(bf16[1024,512]{1,0:T(8,128)(2,1)S(1)} %convolution_convert_fusion.1), channel_id=1, source_target_pairs={{16,0},{0,16},{17,1},{1,17},{18,2},{2,18},{19,3},{3,19},{20,4},{4,... | collective-permute-start | bytes 3145736 | tf_op jit(solution)/shard_map/ppermute | solution.py:30
  537.6 93.8 %collective-permute-start.23 = (bf16[1024,384]{1,0:T(8,128)(2,1)}, bf16[1024,384]{1,0:T(8,128)(2,1)}, u32[]{:S(2)}, u32[]{:S(2)}) collective-permute-start(bf16[1024,384]{1,0:T(8,128)(2,1)} %fusion.11.refs_9_), channel_id=1, source_target_pairs={{16,0},{0,16},{17,1},{1,17},{18,2},{2,18},{19,3},{3,19},{20,4},{4,... | collective-permute-start | bytes 2359304 | tf_op jit(solution)/shard_map/ppermute | solution.py:30
  568.9 81.1 %collective-permute-start.27 = (bf16[1024,768]{1,0:T(8,128)(2,1)}, bf16[1024,768]{1,0:T(8,128)(2,1)}, u32[]{:S(2)}, u32[]{:S(2)}) collective-permute-start(bf16[1024,768]{1,0:T(8,128)(2,1)} %get-tuple-element.109.refs_8_), channel_id=1, source_target_pairs={{16,0},{0,16},{17,1},{1,17},{18,2},{2,18},{19,3},{3,19},{20,4},{4,... | collective-permute-start | bytes 4718600 | tf_op jit(solution)/shard_map/ppermute | solution.py:30
  576.5 58.0 %collective-permute-start.24 = (bf16[1024,128]{1,0:T(8,128)(2,1)}, bf16[1024,128]{1,0:T(8,128)(2,1)}, u32[]{:S(2)}, u32[]{:S(2)}) collective-permute-start(bf16[1024,128]{1,0:T(8,128)(2,1)} %get-tuple-element.146), channel_id=1, source_target_pairs={{12,0},{0,4},{4,8},{8,12},{13,1},{1,5},{5,9},{9,13},{14,2},{2,6},{... | collective-permute-start | bytes 786440 | tf_op jit(solution)/shard_map/ppermute | solution.py:30
  577.3 57.2 %collective-permute-start.25 = (bf16[1024,128]{1,0:T(8,128)(2,1)}, bf16[1024,128]{1,0:T(8,128)(2,1)}, u32[]{:S(2)}, u32[]{:S(2)}) collective-permute-start(bf16[1024,128]{1,0:T(8,128)(2,1)} %get-tuple-element.148), channel_id=1, source_target_pairs={{8,0},{12,4},{0,8},{4,12},{9,1},{13,5},{1,9},{5,13},{10,2},{14,6},... | collective-permute-start | bytes 786440 | tf_op jit(solution)/shard_map/ppermute | solution.py:30
  577.7 56.9 %collective-permute-start.26 = (bf16[1024,128]{1,0:T(8,128)(2,1)}, bf16[1024,128]{1,0:T(8,128)(2,1)}, u32[]{:S(2)}, u32[]{:S(2)}) collective-permute-start(bf16[1024,128]{1,0:T(8,128)(2,1)} %get-tuple-element.147), channel_id=1, source_target_pairs={{4,0},{8,4},{12,8},{0,12},{5,1},{9,5},{13,9},{1,13},{6,2},{10,6},{... | collective-permute-start | bytes 786440 | tf_op jit(solution)/shard_map/ppermute | solution.py:30
  (112 other events, 1856.6 us)
Sparse Core Ops, SparseCore 0:
  21.8 29.8 all-gather.10
  53.9 44.9 all-gather.12
  101.0 129.6 all-gather.14
  273.8 113.3 all-gather.18
  388.6 135.7 all-gather.20
  525.9 136.7 all-gather.22
  664.2 133.4 all-gather.16
